TPU v7x, 32 devices: a whole 2x2x4 slice. The times are simulated.
32 devices in a mesh: dp: 8 (over z, x), ctx: 4 (over y, core).
Axes of the slice: x: 2, y: 2, z: 4, core: 2. Of those that a mesh axis runs over, the one named last changes fastest.
Arguments:
- inputs: bfloat16 [8, 1024, 2048], P('dp', 'ctx'), may hold values from -6 to 6
- segments: int32 [8, 1024], P('dp', 'ctx'), may hold values from 0 to 3, as said below
- ln_gain: bfloat16 [2, 2048], P(None, 'dp'), may hold values from 0.5 to 1.5
- ln_bias: bfloat16 [2, 2048], P(None, 'dp'), may hold values from -1.5 to 1.5
- qkv_weight: bfloat16 [2048, 6144], P('dp'), may hold values from -0.125 to 0.125
- qkv_bias: bfloat16 [6144], P('dp'), may hold values from -2.5 to 2.5
- out_weight: bfloat16 [2048, 2048], P('dp'), may hold values from -1 to 1
- out_bias: bfloat16 [2048], P('dp'), may hold values from -1.5 to 1.5
- up_weight: bfloat16 [2048, 8192], P('dp'), may hold values from -0.125 to 0.125
- up_bias: bfloat16 [8192], P('dp'), may hold values from -2.5 to 2.5
- down_weight: bfloat16 [8192, 2048], P('dp'), may hold values from -0.125 to 0.125
- down_bias: bfloat16 [2048], P('dp'), may hold values from -1.5 to 1.5
- cotangent: bfloat16 [8, 1024, 2048], P('dp', 'ctx'), may hold values from -6 to 6
Outputs:
- result: bfloat16 [8, 1024, 2048], P('dp', 'ctx')
- grad_inputs: bfloat16 [8, 1024, 2048], P('dp', 'ctx')
- grad_ln_gain: float32 [2, 2048], P(None, 'dp')
- grad_ln_bias: float32 [2, 2048], P(None, 'dp')
- grad_qkv_weight: float32 [2048, 6144], P('dp')
- grad_qkv_bias: float32 [6144], P('dp')
- grad_out_weight: float32 [2048, 2048], P('dp')
- grad_out_bias: float32 [2048], P('dp')
- grad_up_weight: float32 [2048, 8192], P('dp')
- grad_up_bias: float32 [8192], P('dp')
- grad_down_weight: float32 [8192, 2048], P('dp')
- grad_down_bias: float32 [2048], P('dp')
Inputs may be any that keep to these rules, and one draw needn't show every extreme that they name: `segments`: each sequence holds four documents in order, numbered 0 to 3; document 1 begins within the first 256 tokens and ends within the last 256 tokens.
All inputs are finite; a program needn't handle non-finite values.
Results may differ from a plain program's by a relative error of at most 0.017.
Values may be sent and summed in bfloat16 or wider, within the bound.
A program may use at most 512 MiB of HBM per device.

v0:
```python
from functools import partial

import jax
import jax.numpy as jnp
from jax import lax
from jax.sharding import PartitionSpec as P

HEADS = 8
HEAD = 256
ROT = 64


EPSILON = 1e-05
MASKED = -1e30


def rotary_tables(positions):
    exponent = jnp.arange(0, ROT, 2).astype(jnp.float32) / ROT
    frequency = 10000.0 ** (-exponent)
    angles = positions[:, None] * frequency[None, :]
    angles = jnp.concatenate([angles, angles], -1)[:, None, :]
    return (jnp.cos(angles), jnp.sin(angles))


def rotate(values, cosine_table, sine_table):
    section = values[..., :ROT]
    half_rot = ROT // 2
    turned = jnp.concatenate([-section[..., half_rot:], section[..., :half_rot]], -1)
    return jnp.concatenate([section * cosine_table + turned * sine_table, values[..., ROT:]], -1)


def unrotate(grads, cosine_table, sine_table):
    section = grads[..., :ROT]
    half_rot = ROT // 2
    scaled = section * sine_table
    turned = jnp.concatenate([scaled[..., half_rot:], -scaled[..., :half_rot]], -1)
    return jnp.concatenate([section * cosine_table + turned, grads[..., ROT:]], -1)


def norm_forward(values, gain, offset):
    average = jnp.mean(values, -1, keepdims=True)
    centred = values - average
    variance = jnp.mean(centred * centred, -1, keepdims=True)
    inverse = lax.rsqrt(variance + EPSILON)
    unit = centred * inverse
    return (unit * gain + offset, unit, inverse)


def norm_backward(grad_normed, unit, inverse, gain):
    grad_unit = grad_normed * gain
    first_mean = jnp.mean(grad_unit, -1, keepdims=True)
    second_mean = jnp.mean(grad_unit * unit, -1, keepdims=True)
    return inverse * (grad_unit - first_mean - unit * second_mean)


def contract_last(left, right):
    return lax.dot_general(
        left, right, (((1,), (1,)), ((), ())), preferred_element_type=jnp.float32
    )


def contract_first(left, right):
    return lax.dot_general(
        left, right, (((0,), (0,)), ((), ())), preferred_element_type=jnp.float32
    )


def gelu_exact(values):
    return jax.nn.gelu(values, approximate=False)


def masked_scores(queries, keys_all, allowed, softmax_scale):
    scores = (
        jnp.einsum("qhd,khd->hqk", queries, keys_all, preferred_element_type=jnp.float32)
        * softmax_scale
    )
    return jnp.where(allowed[None], scores, MASKED)


def attend_forward(queries, keys_all, values_all, allowed, softmax_scale):
    scores = masked_scores(queries, keys_all, allowed, softmax_scale)
    highest = jnp.max(scores, -1, keepdims=True)
    expanded = jnp.exp(scores - highest)
    totals = jnp.sum(expanded, -1, keepdims=True)
    probs = (expanded / totals).astype(jnp.bfloat16)
    attended = jnp.einsum("hqk,khd->qhd", probs, values_all, preferred_element_type=jnp.float32)
    return (attended.astype(jnp.bfloat16), highest + jnp.log(totals))


def attend_backward(
    queries, keys_all, values_all, allowed, log_totals, grad_attended, softmax_scale
):
    scores = masked_scores(queries, keys_all, allowed, softmax_scale)
    probs = jnp.exp(scores - log_totals)
    grad_probs = jnp.einsum(
        "qhd,khd->hqk", grad_attended, values_all, preferred_element_type=jnp.float32
    )
    row_dot = jnp.sum(probs * grad_probs, -1, keepdims=True)
    grad_scores = (probs * (grad_probs - row_dot)).astype(jnp.bfloat16)
    grad_queries = (
        jnp.einsum("hqk,khd->qhd", grad_scores, keys_all, preferred_element_type=jnp.float32)
        * softmax_scale
    )
    grad_keys = (
        jnp.einsum("hqk,qhd->khd", grad_scores, queries, preferred_element_type=jnp.float32)
        * softmax_scale
    )
    grad_values = jnp.einsum(
        "hqk,qhd->khd",
        probs.astype(jnp.bfloat16),
        grad_attended,
        preferred_element_type=jnp.float32,
    )
    return (grad_queries, grad_keys, grad_values)


def on_device(
    inputs,
    segments,
    ln_gain,
    ln_bias,
    qkv_weight,
    qkv_bias,
    out_weight,
    out_bias,
    up_weight,
    up_bias,
    down_weight,
    down_bias,
    cotangent,
):
    local_seqs, local_tokens, width = inputs.shape
    token_count = local_seqs * local_tokens
    softmax_scale = HEAD ** (-0.5)
    gain_full, shift_full, w_qkv, b_qkv, w_out, b_out, w_up, b_up, w_down, b_down = (
        lax.all_gather(ln_gain, "dp", axis=1, tiled=True),
        lax.all_gather(ln_bias, "dp", axis=1, tiled=True),
        lax.all_gather(qkv_weight, "dp", axis=0, tiled=True),
        lax.all_gather(qkv_bias, "dp", axis=0, tiled=True),
        lax.all_gather(out_weight, "dp", axis=0, tiled=True),
        lax.all_gather(out_bias, "dp", axis=0, tiled=True),
        lax.all_gather(up_weight, "dp", axis=0, tiled=True),
        lax.all_gather(up_bias, "dp", axis=0, tiled=True),
        lax.all_gather(down_weight, "dp", axis=0, tiled=True),
        lax.all_gather(down_bias, "dp", axis=0, tiled=True),
    )
    gains = gain_full.astype(jnp.float32)
    shifts = shift_full.astype(jnp.float32)
    token_rows = inputs.reshape(token_count, width).astype(jnp.float32)
    normed_attn, unit_attn, inverse_attn = norm_forward(token_rows, gains[0], shifts[0])
    normed_mlp, unit_mlp, inverse_mlp = norm_forward(token_rows, gains[1], shifts[1])
    attn_input = normed_attn.astype(jnp.bfloat16)
    mlp_input = normed_mlp.astype(jnp.bfloat16)
    projected = jnp.dot(attn_input, w_qkv, preferred_element_type=jnp.float32) + b_qkv.astype(
        jnp.float32
    )
    shaped = projected.reshape(local_seqs, local_tokens, 3, HEADS, HEAD)
    query_pos = lax.axis_index("ctx") * local_tokens + jnp.arange(local_tokens, dtype=jnp.int32)
    cosine_table, sine_table = rotary_tables(query_pos.astype(jnp.float32))
    queries = rotate(shaped[:, :, 0], cosine_table, sine_table).astype(jnp.bfloat16)
    keys_local = rotate(shaped[:, :, 1], cosine_table, sine_table).astype(jnp.bfloat16)
    values_local = shaped[:, :, 2].astype(jnp.bfloat16)
    keys_all, values_all, segments_all = (
        lax.all_gather(keys_local, "ctx", axis=1, tiled=True),
        lax.all_gather(values_local, "ctx", axis=1, tiled=True),
        lax.all_gather(segments, "ctx", axis=1, tiled=True),
    )
    key_pos = jnp.arange(keys_all.shape[1], dtype=jnp.int32)
    allowed = (query_pos[None, :, None] >= key_pos[None, None, :]) & (
        segments[:, :, None] == segments_all[:, None, :]
    )
    attended, log_totals = jax.vmap(partial(attend_forward, softmax_scale=softmax_scale))(
        queries, keys_all, values_all, allowed
    )
    attn_flat = attended.reshape(token_count, width)
    attn_branch = jnp.dot(attn_flat, w_out, preferred_element_type=jnp.float32) + b_out.astype(
        jnp.float32
    )
    up_values = jnp.dot(mlp_input, w_up, preferred_element_type=jnp.float32) + b_up.astype(
        jnp.float32
    )
    activated, gelu_back = jax.vjp(gelu_exact, up_values)
    activated_low = activated.astype(jnp.bfloat16)
    mlp_branch = jnp.dot(activated_low, w_down, preferred_element_type=jnp.float32) + b_down.astype(
        jnp.float32
    )
    result = (
        (token_rows + attn_branch + mlp_branch)
        .astype(jnp.bfloat16)
        .reshape(local_seqs, local_tokens, width)
    )
    gain_back, w_qkv_back, w_out_back, w_up_back, w_down_back = (
        lax.all_gather(ln_gain, "dp", axis=1, tiled=True),
        lax.all_gather(qkv_weight, "dp", axis=0, tiled=True),
        lax.all_gather(out_weight, "dp", axis=0, tiled=True),
        lax.all_gather(up_weight, "dp", axis=0, tiled=True),
        lax.all_gather(down_weight, "dp", axis=0, tiled=True),
    )
    gains_back = gain_back.astype(jnp.float32)
    grad_rows = cotangent.reshape(token_count, width)
    grad_attended = (
        contract_last(grad_rows, w_out_back)
        .astype(jnp.bfloat16)
        .reshape(local_seqs, local_tokens, HEADS, HEAD)
    )
    grad_queries, key_terms, value_terms = jax.vmap(
        partial(attend_backward, softmax_scale=softmax_scale)
    )(queries, keys_all, values_all, allowed, log_totals, grad_attended)
    grad_keys, grad_values = (
        lax.psum_scatter(
            key_terms.astype(jnp.bfloat16), "ctx", scatter_dimension=1, tiled=True
        ).astype(jnp.float32),
        lax.psum_scatter(
            value_terms.astype(jnp.bfloat16), "ctx", scatter_dimension=1, tiled=True
        ).astype(jnp.float32),
    )
    grad_queries = unrotate(grad_queries, cosine_table, sine_table)
    grad_keys = unrotate(grad_keys, cosine_table, sine_table)
    grad_qkv = (
        jnp.stack([grad_queries, grad_keys, grad_values], 2)
        .reshape(token_count, 3 * width)
        .astype(jnp.bfloat16)
    )
    grad_activated = contract_last(grad_rows, w_down_back)
    grad_up = gelu_back(grad_activated)[0].astype(jnp.bfloat16)
    grad_attn_in = contract_last(grad_qkv, w_qkv_back)
    grad_mlp_in = contract_last(grad_up, w_up_back)
    grad_float = grad_rows.astype(jnp.float32)
    grad_tokens = (
        grad_float
        + norm_backward(grad_attn_in, unit_attn, inverse_attn, gains_back[0])
        + norm_backward(grad_mlp_in, unit_mlp, inverse_mlp, gains_back[1])
    )
    grad_inputs = grad_tokens.astype(jnp.bfloat16).reshape(local_seqs, local_tokens, width)
    term_qkv = contract_first(attn_input, grad_qkv)
    term_qkv_bias = jnp.sum(grad_qkv.astype(jnp.float32), 0)
    term_out = contract_first(attn_flat, grad_rows)
    term_out_bias = jnp.sum(grad_float, 0)
    term_up = contract_first(mlp_input, grad_up)
    term_up_bias = jnp.sum(grad_up.astype(jnp.float32), 0)
    term_down = contract_first(activated_low, grad_rows)
    term_down_bias = jnp.sum(grad_float, 0)
    term_gain = jnp.stack(
        [jnp.sum(grad_attn_in * unit_attn, 0), jnp.sum(grad_mlp_in * unit_mlp, 0)]
    )
    term_shift = jnp.stack([jnp.sum(grad_attn_in, 0), jnp.sum(grad_mlp_in, 0)])
    piece_qkv, piece_qkv_bias, piece_out, piece_out_bias = (
        lax.psum_scatter(
            term_qkv.astype(jnp.bfloat16), "dp", scatter_dimension=0, tiled=True
        ).astype(jnp.float32),
        lax.psum_scatter(
            term_qkv_bias.astype(jnp.bfloat16), "dp", scatter_dimension=0, tiled=True
        ).astype(jnp.float32),
        lax.psum_scatter(
            term_out.astype(jnp.bfloat16), "dp", scatter_dimension=0, tiled=True
        ).astype(jnp.float32),
        lax.psum_scatter(
            term_out_bias.astype(jnp.bfloat16), "dp", scatter_dimension=0, tiled=True
        ).astype(jnp.float32),
    )
    piece_up, piece_up_bias, piece_down, piece_down_bias, piece_gain, piece_shift = (
        lax.psum_scatter(
            term_up.astype(jnp.bfloat16), "dp", scatter_dimension=0, tiled=True
        ).astype(jnp.float32),
        lax.psum_scatter(
            term_up_bias.astype(jnp.bfloat16), "dp", scatter_dimension=0, tiled=True
        ).astype(jnp.float32),
        lax.psum_scatter(
            term_down.astype(jnp.bfloat16), "dp", scatter_dimension=0, tiled=True
        ).astype(jnp.float32),
        lax.psum_scatter(
            term_down_bias.astype(jnp.bfloat16), "dp", scatter_dimension=0, tiled=True
        ).astype(jnp.float32),
        lax.psum_scatter(
            term_gain.astype(jnp.bfloat16), "dp", scatter_dimension=1, tiled=True
        ).astype(jnp.float32),
        lax.psum_scatter(
            term_shift.astype(jnp.bfloat16), "dp", scatter_dimension=1, tiled=True
        ).astype(jnp.float32),
    )
    owned = (
        lax.psum(piece_qkv.astype(jnp.bfloat16), "ctx").astype(jnp.float32),
        lax.psum(piece_qkv_bias.astype(jnp.bfloat16), "ctx").astype(jnp.float32),
        lax.psum(piece_out.astype(jnp.bfloat16), "ctx").astype(jnp.float32),
        lax.psum(piece_out_bias.astype(jnp.bfloat16), "ctx").astype(jnp.float32),
        lax.psum(piece_up.astype(jnp.bfloat16), "ctx").astype(jnp.float32),
        lax.psum(piece_up_bias.astype(jnp.bfloat16), "ctx").astype(jnp.float32),
        lax.psum(piece_down.astype(jnp.bfloat16), "ctx").astype(jnp.float32),
        lax.psum(piece_down_bias.astype(jnp.bfloat16), "ctx").astype(jnp.float32),
        lax.psum(piece_gain.astype(jnp.bfloat16), "ctx").astype(jnp.float32),
        lax.psum(piece_shift.astype(jnp.bfloat16), "ctx").astype(jnp.float32),
    )
    (
        grad_qkv_w,
        grad_qkv_b,
        grad_out_w,
        grad_out_b,
        grad_up_w,
        grad_up_b,
        grad_down_w,
        grad_down_b,
        grad_gain,
        grad_shift,
    ) = owned
    return (
        result,
        grad_inputs,
        grad_gain,
        grad_shift,
        grad_qkv_w,
        grad_qkv_b,
        grad_out_w,
        grad_out_b,
        grad_up_w,
        grad_up_b,
        grad_down_w,
        grad_down_b,
    )


def solution(mesh):
    placed = (
        P("dp", "ctx", None),
        P("dp", "ctx"),
        P(None, "dp"),
        P(None, "dp"),
        P("dp", None),
        P("dp"),
        P("dp", None),
        P("dp"),
        P("dp", None),
        P("dp"),
        P("dp", None),
        P("dp"),
        P("dp", "ctx", None),
    )
    return jax.shard_map(
        on_device,
        mesh=mesh,
        in_specs=placed,
        out_specs=(
            P("dp", "ctx", None),
            P("dp", "ctx", None),
            P(None, "dp"),
            P(None, "dp"),
            P("dp", None),
            P("dp"),
            P("dp", None),
            P("dp"),
            P("dp", None),
            P("dp"),
            P("dp", None),
            P("dp"),
        ),
        check_vma=False,
    )
```

profile of v0, /device:TPU:19, one launch (start us, length us, event | category | flops | bytes accessed | tf_op | source)
XLA Modules:
  0.0 4106.1 jit_solution(2576556376566868199)
XLA Ops:
  9.4 52.2 %all-gather.1 = bf16[8,1,768]{2,1,0:T(2,128)(2,1)S(1)} all-gather(bf16[1,1,768]{2,1,0:T(2,128)(2,1)S(1)} %reshape.508), channel_id=1, replica_groups=mesh['dp'=8,'ctx'=4] {'dp'}, dimensions={0}, use_global_device_ids=true | all-gather | bytes 13824 | tf_op jit(solution)/shard_map/all_gather | solution.py:139
  61.6 16.3 all_gather.46
  77.9 20.5 all_gather.47
  99.1 1.4 convert_reduce_fusion
  100.5 1.6 fusion.54
  102.2 388.6 %all-gather.11.cloned.1.call-done = bf16[2048,6144]{1,0:T(8,128)(2,1)} async-done(((bf16[256,6144]{1,0:T(8,128)(2,1)}), bf16[2048,6144]{1,0:T(8,128)(2,1)}) %all-gather.11.cloned.1.call-update) | async-done | bytes 25165840 | tf_op jit(solution)/shard_map/all_gather | solution.py:138
  490.8 12.1 convolution_add_fusion.1
  502.9 2.6 copy.101
  509.3 1.4 fusion.89
  510.7 1.5 pad_maximum_fusion.1
  512.3 2.7 slice.103
  514.9 2.4 copy.100
  517.4 5.8 all_gather.51
  524.2 92.3 %all-gather.15.cloned.1.call-done = bf16[2048,2048]{1,0:T(8,128)(2,1)} async-done(((bf16[256,2048]{1,0:T(8,128)(2,1)}), bf16[2048,2048]{1,0:T(8,128)(2,1)}) %all-gather.15.cloned.1.call-update) | async-done | bytes 8388624 | tf_op jit(solution)/shard_map/all_gather | solution.py:140
  616.5 6.7 convolution_convert_fusion.4
  623.2 2.3 copy.99
  626.8 27.1 all-gather.13.cloned.1.call-done
  654.0 4.5 fusion.103
  658.6 3.4 copy-done
  663.1 27.9 all-gather.21.cloned.1.call-done
  691.1 7.4 multiply_reduce_fusion
  698.5 1.7 multiply_convert_fusion.1
  700.2 2.1 copy-done.4
  702.2 3.3 fusion.10
  705.6 10.9 reduce-scatter.15.cloned.1.call-start
  716.5 6.8 convert_bitcast_fusion
  724.9 6.6 fusion.61
  732.4 5.7 convolution_convert_fusion.3
  738.2 4.9 multiply_bitcast_fusion
  743.1 1.3 slice.119
  744.5 5.4 reduce-scatter.13.cloned.1.call-done
  749.8 1.7 slice.123
  751.5 1.4 convert_element_type.251
  755.0 1.5 maximum_bitcast_fusion.1
  756.5 41.0 reduce-scatter.15.cloned.1.call-done
  797.5 4.1 fusion.97
  801.6 4.7 copy.80
  806.2 14.2 convolution_convert_fusion.2
  821.1 44.2 %all_gather.57 = bf16[8192]{0:T(1024)(128)(2,1)S(1)} all-gather(bf16[1024]{0:T(1024)(128)(2,1)S(1)} %copy-done.18), channel_id=1, replica_groups=mesh['dp'=8,'ctx'=4] {'dp'}, dimensions={0}, use_global_device_ids=true | all-gather | bytes 18432 | tf_op jit(solution)/shard_map/all_gather | solution.py:143
  865.3 570.9 %all-gather.17.cloned.1.call-done = bf16[2048,8192]{1,0:T(8,128)(2,1)} async-done(((bf16[256,8192]{1,0:T(8,128)(2,1)}), bf16[2048,8192]{1,0:T(8,128)(2,1)}) %all-gather.17.cloned.1.call-update) | async-done | bytes 33554448 | tf_op jit(solution)/shard_map/all_gather | solution.py:142
  1436.2 32.2 multiply_convert_fusion.2
  1468.4 607.1 %all-gather.19.cloned.1.call-done = bf16[8192,2048]{1,0:T(8,128)(2,1)} async-done(((bf16[1024,2048]{1,0:T(8,128)(2,1)}), bf16[8192,2048]{1,0:T(8,128)(2,1)}) %all-gather.19.cloned.1.call-update) | async-done | bytes 33554448 | tf_op jit(solution)/shard_map/all_gather | solution.py:144
  2075.5 33.3 fusion.104
  2108.7 16.6 convolution_convert_fusion.1
  2125.4 16.1 convolution_convert_fusion
  2141.5 14.0 fusion.105
  2155.5 18.7 fusion.53
  2176.7 51.8 %reduce-scatter.19.cloned.1.call-done = bf16[256,2048]{1,0:T(8,128)(2,1)} async-done(((bf16[2048,2048]{1,0:T(8,128)(2,1)}), bf16[256,2048]{1,0:T(8,128)(2,1)}) %reduce-scatter.19.cloned.1.call-update) | async-done | bytes 1048592 | tf_op jit(solution)/shard_map/reduce_scatter | solution.py:254
  2228.5 407.2 %reduce-scatter.17.cloned.1.call-done = bf16[256,6144]{1,0:T(8,128)(2,1)} async-done(((bf16[2048,6144]{1,0:T(8,128)(2,1)}), bf16[256,6144]{1,0:T(8,128)(2,1)}) %reduce-scatter.17.cloned.1.call-update) | async-done | bytes 3145744 | tf_op jit(solution)/shard_map/reduce_scatter | solution.py:248
  2635.7 545.6 %reduce-scatter.21.cloned.1.call-done = bf16[256,8192]{1,0:T(8,128)(2,1)} async-done(((bf16[2048,8192]{1,0:T(8,128)(2,1)}), bf16[256,8192]{1,0:T(8,128)(2,1)}) %reduce-scatter.21.cloned.1.call-update) | async-done | bytes 4194320 | tf_op jit(solution)/shard_map/reduce_scatter | solution.py:262
  3181.3 546.3 %reduce-scatter.23.cloned.1.call-done = bf16[1024,2048]{1,0:T(8,128)(2,1)} async-done(((bf16[8192,2048]{1,0:T(8,128)(2,1)}), bf16[1024,2048]{1,0:T(8,128)(2,1)}) %reduce-scatter.23.cloned.1.call-update) | async-done | bytes 4194320 | tf_op jit(solution)/shard_map/reduce_scatter | solution.py:268
  3730.5 11.6 all-gather.3
  3742.1 14.9 all-gather.2
  3757.0 7.1 fusion.24
  3764.1 26.1 all-reduce.3
  3790.4 4.4 fusion.88
  3794.8 17.6 fusion.38
  3813.3 42.1 %reduce-scatter.27.cloned.1.call-done = bf16[256,2]{1,0:T(8,128)(2,1)} async-done(((bf16[2048,2]{1,0:T(8,128)(2,1)}), bf16[256,2]{1,0:T(8,128)(2,1)}) %reduce-scatter.27.cloned.1.call-update) | async-done | bytes 1040
  3856.3 7.7 all-reduce.4
  3866.4 215.3 %all-reduce.8.cloned.1.call-done = (bf16[256,6144]{1,0:T(8,128)(2,1)}, bf16[256,2048]{1,0:T(8,128)(2,1)}, bf16[256,8192]{1,0:T(8,128)(2,1)}, bf16[1024,2048]{1,0:T(8,128)(2,1)}) async-done(((bf16[256,6144]{1,0:T(8,128)(2,1)}, bf16[256,2048]{1,0:T(8,128)(2,1)}, bf16[256,8192]{1,0:T(8,128)(2,1)}, bf16[1024,2048]{1,0:T(8,128)(2,1)}), (bf16[256,6144]{1,0:T(8,128)(2,1)}, bf16[256,2048]{1,0:T(8,128)(2,1)}, ...) | async-done | bytes 12582928 | tf_op jit(solution)/shard_map/psum | solution.py:282
  4081.7 2.9 convert_element_type.268
  4084.7 5.3 convert_element_type.265
  4090.0 4.4 convert_element_type.271
  4094.4 4.4 convert_element_type.274
  (130 shorter events, 23.9 us)
Async XLA Ops:
  7.2 483.6 %all-gather.11.cloned.1.call-start = ((), (), s32[]{:S(2)}) async-start(), calls=%async_computation.8 | async-start | bytes 28311552 | tf_op jit(solution)/shard_map/all_gather | solution.py:138
  7.9 608.6 %all-gather.15.cloned.1.call-start = ((), (), s32[]{:S(2)}) async-start(), calls=%async_computation.10 | async-start | bytes 9437184 | tf_op jit(solution)/shard_map/all_gather | solution.py:140
  8.7 645.3 %all-gather.13.cloned.1.call-start = ((), (), s32[]{:S(2)}) async-start(), calls=%async_computation.9 | async-start | bytes 5242880 | tf_op jit(solution)/shard_map/all_gather | solution.py:164
  102.2 704.0 %copy-start.14 = (f32[1,2048]{1,0:T(1,128)}, f32[1,2048]{1,0:T(1,128)S(1)}, u32[]{:S(2)}) copy-start(f32[1,2048]{1,0:T(1,128)S(1)} %get-tuple-element.57) | copy-start | bytes 24580
  505.5 2.7 copy-start.3
  509.3 8.1 copy-start.17
  509.3 107.2 %copy-start.5 = (bf16[1,256,2048]{2,1,0:T(8,128)(2,1)S(1)}, bf16[1,256,2048]{2,1,0:T(8,128)(2,1)}, u32[]{:S(2)}) copy-start(bf16[1,256,2048]{2,1,0:T(8,128)(2,1)} %param.25) | copy-start | bytes 3145732
  512.2 178.8 %all-gather.21.cloned.1.call-start = ((), (), s32[]{:S(2)}) async-start(), calls=%async_computation.19 | async-start | bytes 5242880 | tf_op jit(solution)/shard_map/all_gather | solution.py:165
  517.4 232.4 %reduce-scatter.13.cloned.1.call-start = ((), (), s32[]{:S(2)}) async-start(), calls=%async_computation.13 | async-start | bytes 5242880 | tf_op jit(solution)/shard_map/reduce_scatter | solution.py:210
  654.0 37.1 copy-start.6
  658.5 3.4 copy-start
  691.0 7.4 copy-start.1
  698.4 3.8 copy-start.12
  698.5 3.8 copy-start.13
  700.2 2.1 copy-start.4
  705.6 91.9 %reduce-scatter.15.cloned.1.call-start = ((), (), s32[]{:S(2)}) async-start(), calls=%async_computation.14 | async-start | bytes 5242880 | tf_op jit(solution)/shard_map/reduce_scatter | solution.py:213
  723.3 712.9 %all-gather.17.cloned.1.call-start = ((), (), s32[]{:S(2)}) async-start(), calls=%async_computation.11 | async-start | bytes 37748736 | tf_op jit(solution)/shard_map/all_gather | solution.py:142
  724.1 1351.4 %all-gather.19.cloned.1.call-start = ((), (), s32[]{:S(2)}) async-start(), calls=%async_computation.12 | async-start | bytes 37748736 | tf_op jit(solution)/shard_map/all_gather | solution.py:144
  724.8 1503.7 %reduce-scatter.19.cloned.1.call-start = ((), (), s32[]{:S(2)}) async-start(), calls=%async_computation.16 | async-start | bytes 9437184 | tf_op jit(solution)/shard_map/reduce_scatter | solution.py:254
  731.4 1.0 copy-start.7
  738.2 1897.5 %reduce-scatter.17.cloned.1.call-start = ((), (), s32[]{:S(2)}) async-start(), calls=%async_computation.15 | async-start | bytes 28311552 | tf_op jit(solution)/shard_map/reduce_scatter | solution.py:248
  753.1 1.4 copy-start.11
  754.5 51.8 %copy-start.2 = (bf16[1,256,2048]{2,1,0:T(8,128)(2,1)S(1)}, bf16[1,256,2048]{2,1,0:T(8,128)(2,1)}, u32[]{:S(2)}) copy-start(bf16[1,256,2048]{2,1,0:T(8,128)(2,1)} %param.13) | copy-start | bytes 3145732
  820.4 0.7 copy-start.18
  820.4 2360.9 %reduce-scatter.21.cloned.1.call-start = ((), (), s32[]{:S(2)}) async-start(), calls=%async_computation.17 | async-start | bytes 37748736 | tf_op jit(solution)/shard_map/reduce_scatter | solution.py:262
  2125.3 1602.3 %reduce-scatter.23.cloned.1.call-start = ((), (), s32[]{:S(2)}) async-start(), calls=%async_computation.18 | async-start | bytes 37748736 | tf_op jit(solution)/shard_map/reduce_scatter | solution.py:268
  2141.5 14.1 copy-start.15
  2141.5 1670.9 %reduce-scatter.25.cloned.1.call-start = ((), (), s32[]{:S(2)}) async-start(), calls=%async_computation.20 | async-start | bytes 589824
  2174.2 1553.5 %copy-start.22 = (u32[32]{0:T(128)S(1)}, u32[32]{0:T(128)}, u32[]{:S(2)}) copy-start(u32[32]{0:T(128)} %constant.103) | copy-start | bytes 388
  2174.2 1556.0 %copy-start.20 = (bf16[256]{0:T(256)(128)(2,1)S(1)}, bf16[256]{0:T(256)(128)(2,1)}, u32[]{:S(2)}) copy-start(bf16[256]{0:T(256)(128)(2,1)} %param.20) | copy-start | bytes 1540
  2174.2 1556.0 %copy-start.21 = (bf16[256]{0:T(256)(128)(2,1)S(1)}, bf16[256]{0:T(256)(128)(2,1)}, u32[]{:S(2)}) copy-start(bf16[256]{0:T(256)(128)(2,1)} %param.24) | copy-start | bytes 1540
  2174.2 1582.8 %copy-start.8 = (bf16[8,256,256]{2,1,0:T(8,128)(2,1)S(1)}, bf16[8,256,256]{2,1,0:T(8,128)(2,1)}, u32[]{:S(2)}) copy-start(bf16[8,256,256]{2,1,0:T(8,128)(2,1)} %copy-done.7) | copy-start | bytes 3145732
  2175.4 1680.0 %reduce-scatter.27.cloned.1.call-start = ((), (), s32[]{:S(2)}) async-start(), calls=%async_computation.21 | async-start | bytes 589824
  2176.6 1905.1 %all-reduce.8.cloned.1.call-start = ((), (), s32[]{:S(2)}) async-start(), calls=%async_computation.22 | async-start | bytes 25165824 | tf_op jit(solution)/shard_map/psum | solution.py:282
  3730.3 33.8 copy-start.16
  3864.1 234.8 %copy-start.19 = (f32[256]{0:T(256)}, f32[256]{0:T(256)S(1)}, u32[]{:S(2)}) copy-start(f32[256]{0:T(256)S(1)} %convert_element_type.269) | copy-start | bytes 3076
  4081.7 8.3 copy-start.10
  4090.0 4.4 copy-start.9
Sparse Core Ops, SparseCore 0:
  9.5 481.1 all-gather.10
  492.9 123.5 all-gather.14
  618.7 35.2 all-gather.12
  656.0 35.0 all-gather.20
  705.7 44.0 reduce-scatter.12
  752.9 44.5 reduce-scatter.14
  799.0 637.1 all-gather.16
  1437.7 637.6 all-gather.18
  2079.7 148.7 reduce-scatter.18
  2232.7 402.9 reduce-scatter.16
  2639.9 541.3 reduce-scatter.20
  3185.4 542.1 reduce-scatter.22
  3731.4 59.8 reduce-scatter.24
  3794.5 60.9 reduce-scatter.26
  3858.2 223.4 all-reduce.7
where the time goes:
time: 4120 us; the launch traced here: 4110 us
  waiting for transfers between devices  3570 us (87%)
  matrix products  228 us (6%)
  blocking collectives  199 us (5%)
  other arithmetic  44.4 us (1%)
    all_gather x1, waiting for transfers between devices, on_device(): lax.all_gather(down_weight, 'dp', axis=0, tiled=True)  607 us
    all_gather x1, waiting for transfers between devices, on_device(): lax.all_gather(up_weight, 'dp', axis=0, tiled=True)  571 us
    reduce_scatter x1, waiting for transfers between devices, on_device(): lax.psum_scatter(term_down.astype(jnp.bfloat16), 'dp', scatter_dimension=...  546 us
    reduce_scatter x1, waiting for transfers between devices, on_device(): lax.psum_scatter(term_up.astype(jnp.bfloat16), 'dp', scatter_dimension=0,...  546 us
    reduce_scatter x1, waiting for transfers between devices, on_device(): lax.psum_scatter(term_qkv.astype(jnp.bfloat16), 'dp', scatter_dimension=0...  407 us
    all_gather x1, waiting for transfers between devices, on_device(): lax.all_gather(qkv_weight, 'dp', axis=0, tiled=True)  389 us
    psum x1, waiting for transfers between devices, on_device(): lax.psum(piece_qkv.astype(jnp.bfloat16), 'ctx').astype(jnp.float32)  215 us
    all_gather x1, waiting for transfers between devices, on_device(): lax.all_gather(out_weight, 'dp', axis=0, tiled=True)  92.3 us
  transfers between devices with their start and end apart: 15, of which 14 were waited for; matrix products, arithmetic and copies ran while one was open for 7% of the time, Pallas kernels for 0%

commit v1 on v0

v1 whole, which is shorter than its diff:
```python
from functools import partial

import jax
import jax.numpy as jnp
from jax import lax
from jax.experimental import pallas as pl
from jax.experimental.pallas import tpu as pltpu
from jax.sharding import PartitionSpec as P

HEADS = 8
HEAD = 256
ROT = 64
EPSILON = 1e-05
MASKED = -1e30
F32 = jnp.float32
BF16 = jnp.bfloat16


def dot(left, right):
    return jnp.dot(left, right, preferred_element_type=F32)


def contract_last(left, right):
    return lax.dot_general(left, right, (((1,), (1,)), ((), ())), preferred_element_type=F32)


def contract_first(left, right):
    return lax.dot_general(left, right, (((0,), (0,)), ((), ())), preferred_element_type=F32)


def rotary_tables(positions):
    half = ROT // 2
    exponent = jnp.arange(0, ROT, 2).astype(F32) / ROT
    frequency = 10000.0 ** (-exponent)
    angles = positions[:, None] * frequency[None, :]
    rows = positions.shape[0]
    cosine, sine = jnp.cos(angles), jnp.sin(angles)
    one, nought = jnp.ones((rows, 64), F32), jnp.zeros((rows, 64), F32)
    blank = jnp.zeros((rows, half), F32)
    return (
        jnp.concatenate([cosine, cosine, one], -1),
        jnp.concatenate([-sine, blank, nought], -1),
        jnp.concatenate([blank, sine, nought], -1),
    )


def rotate(values, tables):
    half = ROT // 2
    cosine, above, below = tables
    low = values[..., :128]
    low = low * cosine + jnp.roll(low, -half, -1) * above + jnp.roll(low, half, -1) * below
    return jnp.concatenate([low, values[..., 128:]], -1)


def attention_kernel(
    block, q_ref, k_ref, v_ref, do_ref, col_ref, row_ref, cos_ref, above_ref, below_ref,
    o_ref, dq_ref, dk_ref, dv_ref, dk_sum, dv_sum,
):
    scale = HEAD ** (-0.5)
    half = ROT // 2
    length = q_ref.shape[0]

    def unrotate(grads, rows):
        low = grads[:, :128]
        low = (
            low * cos_ref[rows, :]
            + pltpu.roll(low * below_ref[rows, :], 128 - half, 1)
            + pltpu.roll(low * above_ref[rows, :], half, 1)
        )
        return jnp.concatenate([low, grads[:, 128:]], -1)

    dk_sum[...] = jnp.zeros_like(dk_sum)
    dv_sum[...] = jnp.zeros_like(dv_sum)
    for start in range(0, length, block):
        rows = pl.ds(start, block)
        keys = pl.ds(0, start + block)
        queries, grads = q_ref[rows, :], do_ref[rows, :]
        key_block, value_block = k_ref[keys, :], v_ref[keys, :]
        scores = contract_last(queries, key_block) * scale
        shape = scores.shape
        query_pos = start + lax.broadcasted_iota(jnp.int32, shape, 0)
        key_pos = lax.broadcasted_iota(jnp.int32, shape, 1)
        allowed = (query_pos >= key_pos) & (col_ref[rows, :] == row_ref[:, keys])
        scores = jnp.where(allowed, scores, MASKED)
        expanded = jnp.exp(scores - jnp.max(scores, -1, keepdims=True))
        probs = expanded / jnp.sum(expanded, -1, keepdims=True)
        probs_low = probs.astype(BF16)
        o_ref[rows, :] = dot(probs_low, value_block).astype(BF16)
        grad_probs = contract_last(grads, value_block)
        row_dot = jnp.sum(probs * grad_probs, -1, keepdims=True)
        grad_scores = (probs * (grad_probs - row_dot)).astype(BF16)
        dq_ref[rows, :] = unrotate(dot(grad_scores, key_block) * scale, rows).astype(BF16)
        dk_sum[keys, :] += contract_first(grad_scores, queries)
        dv_sum[keys, :] += contract_first(probs_low, grads)
    dk_ref[...] = unrotate(dk_sum[...] * scale, pl.ds(0, length)).astype(BF16)
    dv_ref[...] = dv_sum[...].astype(BF16)


def attention(queries, keys, values, grads, segments, tables):
    seqs, length, head = queries.shape
    whole = pl.BlockSpec((None, length, head), lambda s: (s, 0, 0))
    table = pl.BlockSpec((length, 128), lambda s: (0, 0))
    shape = jax.ShapeDtypeStruct(queries.shape, BF16)
    return pl.pallas_call(
        partial(attention_kernel, min(256, length)),
        grid=(seqs,),
        in_specs=[whole] * 4
        + [
            pl.BlockSpec((None, length, 1), lambda s: (s, 0, 0)),
            pl.BlockSpec((None, 1, length), lambda s: (s, 0, 0)),
        ]
        + [table] * 3,
        out_specs=[whole] * 4,
        out_shape=[shape] * 4,
        scratch_shapes=[pltpu.VMEM((length, head), F32)] * 2,
        compiler_params=pltpu.CompilerParams(vmem_limit_bytes=48 << 20),
    )(queries, keys, values, grads, segments[:, :, None], segments[:, None, :], *tables)


def normalize(rows):
    average = jnp.mean(rows, -1, keepdims=True)
    centred = rows - average
    variance = jnp.mean(centred * centred, -1, keepdims=True)
    inverse = lax.rsqrt(variance + EPSILON)
    return centred * inverse, inverse


def gelu_exact(values):
    return jax.nn.gelu(values, approximate=False)


def on_device(
    dp,
    ctx,
    inputs,
    segments,
    ln_gain,
    ln_bias,
    qkv_weight,
    qkv_bias,
    out_weight,
    out_bias,
    up_weight,
    up_bias,
    down_weight,
    down_bias,
    cotangent,
):
    team = HEADS
    teams = dp // team
    together = None if teams == 1 else [[g * team + i for i in range(team)] for g in range(teams)]
    across = None if teams == 1 else [[g * team + i for g in range(teams)] for i in range(team)]
    gather = partial(lax.all_gather, axis_name="dp", tiled=True, axis_index_groups=together)
    place = lax.axis_index("dp")
    rank = place % team
    quarter = lax.axis_index("ctx")
    _, tokens, width = inputs.shape
    rows = qkv_weight.shape[0]
    hidden = up_weight.shape[1] // team
    part = rows // ctx

    small = jnp.concatenate(
        [ln_gain.reshape(-1), ln_bias.reshape(-1), qkv_bias, out_bias, up_bias, down_bias]
    )
    small = lax.all_gather(small, "dp", axis=0).astype(F32)
    cuts = [0]
    for size in (2 * rows, 2 * rows, qkv_bias.shape[0], rows, up_bias.shape[0], rows):
        cuts.append(cuts[-1] + size)
    pieces = [small[:, a:b] for a, b in zip(cuts[:-1], cuts[1:])]
    gains = pieces[0].reshape(dp, 2, rows).transpose(1, 0, 2).reshape(2, width)
    shifts = pieces[1].reshape(dp, 2, rows).transpose(1, 0, 2).reshape(2, width)
    b_qkv = lax.dynamic_index_in_dim(pieces[2].reshape(3, HEADS, HEAD), rank, 1, False)
    b_out, b_down = pieces[3].reshape(width), pieces[5].reshape(width)
    b_up = lax.dynamic_index_in_dim(pieces[4].reshape(team, hidden), rank, 0, False)

    my_rows = quarter * part
    columns = jnp.concatenate(
        [
            lax.dynamic_slice_in_dim(qkv_weight, my_rows, part, 0).reshape(part, 3, HEADS, HEAD)
            .transpose(2, 0, 1, 3).reshape(team, part, 3 * HEAD),
            lax.dynamic_slice_in_dim(up_weight, my_rows, part, 0).reshape(part, team, hidden)
            .transpose(1, 0, 2),
        ],
        -1,
    )
    columns = lax.all_to_all(columns, "dp", 0, 0, axis_index_groups=together, tiled=True)
    columns = lax.all_gather(columns, "ctx", axis=1, tiled=True)
    if across is not None:
        columns = lax.all_gather(columns, "dp", axis=0, tiled=True, axis_index_groups=across)
        w_out = lax.all_gather(out_weight, "dp", axis=0, tiled=True)
        w_out = lax.dynamic_slice_in_dim(w_out, rank * HEAD, HEAD, 0)
        w_down = lax.all_gather(down_weight, "dp", axis=0, tiled=True)
        w_down = lax.dynamic_slice_in_dim(w_down, rank * hidden, hidden, 0)
    else:
        w_out, w_down = out_weight, down_weight
    columns = columns.reshape(width, 3 * HEAD + hidden)
    w_qkv, w_up = columns[:, : 3 * HEAD], columns[:, 3 * HEAD :]

    everyone = gather(inputs, axis=0).reshape(team * tokens, width)
    grad_rows = gather(cotangent, axis=0).reshape(team * tokens, width)
    segments_all = lax.all_gather(segments, "ctx", axis=1, tiled=True)
    segments_all = gather(segments_all, axis=0)
    share = team // ctx
    segments_mine = lax.dynamic_slice_in_dim(segments_all, quarter * share, share, 0)

    unit, _ = normalize(everyone.astype(F32))
    attn_input = (unit * gains[0] + shifts[0]).astype(BF16)
    mlp_input = (unit * gains[1] + shifts[1]).astype(BF16)
    positions = (quarter * tokens + jnp.arange(tokens, dtype=jnp.int32)).astype(F32)
    tables = [table[None, :, None, :] for table in rotary_tables(positions)]
    projected = (dot(attn_input, w_qkv) + b_qkv.reshape(-1)).reshape(team, tokens, 3, HEAD)
    turned = rotate(projected[:, :, :2], tables).astype(BF16)
    grad_attended = contract_last(grad_rows, w_out).astype(BF16).reshape(team, tokens, HEAD)
    sent = jnp.stack(
        [turned[:, :, 0], turned[:, :, 1], projected[:, :, 2].astype(BF16), grad_attended]
    )
    whole = lax.all_to_all(sent, "ctx", 1, 2, tiled=True)
    length = tokens * ctx
    outs = attention(
        whole[0], whole[1], whole[2], whole[3], segments_mine,
        rotary_tables(jnp.arange(length).astype(F32)),
    )
    back = lax.all_to_all(jnp.stack(outs), "ctx", 2, 1, tiled=True)
    back = back.reshape(4, team * tokens, HEAD)
    attended = back[0]
    grad_qkv = jnp.concatenate([back[1], back[2], back[3]], -1)

    up_values = dot(mlp_input, w_up) + b_up
    activated, gelu_back = jax.vjp(gelu_exact, up_values)
    activated = activated.astype(BF16)
    grad_up = gelu_back(contract_last(grad_rows, w_down))[0].astype(BF16)

    branches = (dot(attended, w_out) + dot(activated, w_down)).astype(BF16)
    branches = lax.psum_scatter(
        branches, "dp", scatter_dimension=0, axis_index_groups=together, tiled=True
    ).astype(F32)
    mine = inputs.reshape(tokens, width).astype(F32)
    result = (mine + (branches + (b_out + b_down))).astype(BF16)

    grad_attn_in = contract_last(grad_qkv, w_qkv)
    grad_mlp_in = contract_last(grad_up, w_up)
    pulled = (grad_attn_in * gains[0] + grad_mlp_in * gains[1]).astype(BF16)
    pulled = lax.psum_scatter(
        pulled, "dp", scatter_dimension=0, axis_index_groups=together, tiled=True
    ).astype(F32)
    my_unit, my_inverse = normalize(mine)
    grad_inputs = cotangent.reshape(tokens, width).astype(F32) + my_inverse * (
        pulled
        - jnp.mean(pulled, -1, keepdims=True)
        - my_unit * jnp.mean(pulled * my_unit, -1, keepdims=True)
    )

    grad_float = grad_rows.astype(F32)
    qkv_bias_sum = jnp.sum(grad_qkv.astype(F32), 0).reshape(3, 1, HEAD)
    qkv_bias_sum = lax.dynamic_update_slice_in_dim(
        jnp.zeros((3, HEADS, HEAD), F32), qkv_bias_sum, rank, 1
    )
    up_bias_sum = lax.dynamic_update_slice_in_dim(
        jnp.zeros((team, hidden), F32), jnp.sum(grad_up.astype(F32), 0)[None], rank, 0
    )
    dy_sum = jnp.sum(grad_float, 0) * jnp.where(rank == 0, 1.0, 0.0)
    vector = jnp.concatenate(
        [
            jnp.sum(grad_attn_in * unit, 0),
            jnp.sum(grad_mlp_in * unit, 0),
            jnp.sum(grad_attn_in, 0),
            jnp.sum(grad_mlp_in, 0),
            qkv_bias_sum.reshape(-1),
            dy_sum,
            up_bias_sum.reshape(-1),
        ]
    )
    vector = lax.psum(vector, ("dp", "ctx"))

    def own(start, size):
        return lax.dynamic_slice_in_dim(vector, start + place * (size // dp), size // dp, 0)

    grad_gain = jnp.stack([own(0, width), own(width, width)])
    grad_shift = jnp.stack([own(2 * width, width), own(3 * width, width)])
    grad_qkv_b = own(4 * width, 3 * width)
    grad_out_b = own(7 * width, width)
    grad_up_b = own(8 * width, team * hidden)

    term_out = contract_first(attended, grad_rows).astype(BF16)
    term_down = contract_first(activated, grad_rows).astype(BF16)
    term_columns = jnp.concatenate(
        [
            contract_first(attn_input, grad_qkv).astype(BF16),
            contract_first(mlp_input, grad_up).astype(BF16),
        ],
        -1,
    )
    if across is not None:
        full = jnp.zeros((team, HEAD, width), BF16)
        full = lax.dynamic_update_slice_in_dim(full, term_out[None], rank, 0)
        term_out = lax.psum_scatter(
            full.reshape(width, width), "dp", scatter_dimension=0, tiled=True
        )
        full = jnp.zeros((team, hidden, width), BF16)
        full = lax.dynamic_update_slice_in_dim(full, term_down[None], rank, 0)
        term_down = lax.psum_scatter(
            full.reshape(team * hidden, width), "dp", scatter_dimension=0, tiled=True
        )
        term_columns = lax.psum_scatter(
            term_columns, "dp", scatter_dimension=0, axis_index_groups=across, tiled=True
        )
    grad_out_w = lax.psum(term_out, "ctx").astype(F32)
    grad_down_w = lax.psum(term_down, "ctx").astype(F32)
    term_columns = term_columns.reshape(team, rows, 3 * HEAD + hidden)
    term_columns = lax.psum_scatter(term_columns, "ctx", scatter_dimension=1, tiled=True)
    term_columns = lax.all_to_all(
        term_columns, "dp", 0, 0, axis_index_groups=together, tiled=True
    )
    term_columns = lax.all_gather(term_columns, "ctx", axis=1, tiled=True)
    grad_qkv_w = (
        term_columns[:, :, : 3 * HEAD].reshape(team, rows, 3, HEAD).transpose(1, 2, 0, 3)
        .reshape(rows, 3 * width).astype(F32)
    )
    grad_up_w = (
        term_columns[:, :, 3 * HEAD :].transpose(1, 0, 2).reshape(rows, team * hidden).astype(F32)
    )
    return (
        result.reshape(inputs.shape),
        grad_inputs.astype(BF16).reshape(inputs.shape),
        grad_gain,
        grad_shift,
        grad_qkv_w,
        grad_qkv_b,
        grad_out_w,
        grad_out_b,
        grad_up_w,
        grad_up_b,
        grad_down_w,
        grad_out_b,
    )


def solution(mesh):
    placed = (
        P("dp", "ctx", None),
        P("dp", "ctx"),
        P(None, "dp"),
        P(None, "dp"),
        P("dp", None),
        P("dp"),
        P("dp", None),
        P("dp"),
        P("dp", None),
        P("dp"),
        P("dp", None),
        P("dp"),
        P("dp", "ctx", None),
    )
    return jax.shard_map(
        partial(on_device, mesh.shape["dp"], mesh.shape["ctx"]),
        mesh=mesh,
        in_specs=placed,
        out_specs=(
            P("dp", "ctx", None),
            P("dp", "ctx", None),
            P(None, "dp"),
            P(None, "dp"),
            P("dp", None),
            P("dp"),
            P("dp", None),
            P("dp"),
            P("dp", None),
            P("dp"),
            P("dp", None),
            P("dp"),
        ),
        check_vma=False,
    )
```

time: 4120 us -> 1310 us (0.32)
  waiting for transfers between devices: 3570 us -> 713 us
  local copies, waits for them, and re-layouts: 35.2 us -> 124 us
  matrix products: 228 us -> 168 us
    all_gather x6 -> x4, waiting for transfers between devices: 1710 us -> 275 us  [the longest x1 117 us: on_device(): everyone = gather(inputs, axis=0).reshape(team * tokens, width)]
    reduce_scatter x6 -> x3, waiting for transfers between devices: 1600 us -> 293 us  [the longest x1 150 us: on_device(): lax.psum_scatter(branches, 'dp', scatter_dimension=0, axis_index_groups=t...]
    all_to_all x0 -> x2, blocking collectives: none -> 93 us  [the longest x1 48.5 us: on_device(): lax.all_to_all(term_columns, 'dp', 0, 0, axis_index_groups=together, tile...]
    psum x1 -> x2, waiting for transfers between devices: 215 us -> 143 us  [the longest x1 103 us: on_device(): grad_out_w = lax.psum(term_out, 'ctx').astype(F32)]
    all_gather x7 -> x3, blocking collectives: 165 us -> 93.3 us  [the longest x1 48.2 us: on_device(): segments_all = lax.all_gather(segments, 'ctx', axis=1, tiled=True)]
    dot_general x10 -> x4, matrix products: 102 us -> 51.5 us  [dot(): return jnp.dot(left, right, preferred_element_type=F32)]
    unnamed x17 -> x9, waiting for transfers between devices: 45.1 us -> 2.17 us
  transfers between devices with their start and end apart: 15 -> 11, of which waited for: 14 -> 8; matrix products, arithmetic and copies ran while one was open for 7% -> 19% of each run, Pallas kernels for 0% -> 0%
where the time goes in v1:
time: 1310 us; the launch traced here: 1300 us
  waiting for transfers between devices  713 us (54%)
  blocking collectives  186 us (14%)
  matrix products  168 us (13%)
  local copies, waits for them, and re-layouts  124 us (9%)
  other arithmetic  68.8 us (5%)
  starting transfers between devices  17.9 us (1%)
  between operations  15.2 us (1%)
    reduce_scatter x1, waiting for transfers between devices, on_device(): lax.psum_scatter(branches, 'dp', scatter_dimension=0, axis_index_groups=t...  150 us
    reduce_scatter x1, waiting for transfers between devices, on_device(): lax.psum_scatter(pulled, 'dp', scatter_dimension=0, axis_index_groups=tog...  143 us
    all_gather x1, waiting for transfers between devices, on_device(): everyone = gather(inputs, axis=0).reshape(team * tokens, width)  117 us
    psum x1, waiting for transfers between devices, on_device(): grad_out_w = lax.psum(term_out, 'ctx').astype(F32)  103 us
    all_gather x1, waiting for transfers between devices, on_device(): grad_rows = gather(cotangent, axis=0).reshape(team * tokens, width)  78.8 us
    dot_general x4, matrix products, contract_last(): lax.dot_general(left, right, (((1,), (1,)), ((), ())), preferred_element_...  74.6 us
    dot_general x4, matrix products, dot(): return jnp.dot(left, right, preferred_element_type=F32)  51.5 us
    all_gather x1, waiting for transfers between devices, on_device(): term_columns = lax.all_gather(term_columns, 'ctx', axis=1, tiled=True)  51 us
  transfers between devices with their start and end apart: 11, of which 8 were waited for; matrix products, arithmetic and copies ran while one was open for 19% of the time, Pallas kernels for 0%

profile of v1, /device:TPU:19, one launch (start us, length us, event | category | flops | bytes accessed | tf_op | source)
XLA Modules:
  0.0 1303.8 jit_solution(16519022797789670772)
XLA Ops:
  7.2 1.8 copy-done
  11.7 44.5 %all_to_all.40 = bf16[8,64,1792]{2,1,0:T(8,128)(2,1)S(1)} all-to-all(bf16[8,64,1792]{2,1,0:T(8,128)(2,1)S(1)} %copy.84), channel_id=1, replica_groups=mesh['dp'=8,'ctx'=4] {'dp'}, dimensions={0} | all-to-all | bytes 3670016 | tf_op jit(solution)/shard_map/all_to_all | solution.py:186
  56.3 2.2 copy.85
  61.2 24.0 %all-gather.1 = bf16[8,1,3328]{2,1,0:T(2,128)(2,1)S(1)} all-gather(bf16[1,1,3328]{2,1,0:T(2,128)(2,1)S(1)} %reshape.241), channel_id=2, replica_groups=mesh['dp'=8,'ctx'=4] {'dp'}, dimensions={0}, use_global_device_ids=true | all-gather | bytes 59904 | tf_op jit(solution)/shard_map/all_gather | solution.py:165
  85.8 28.2 %all-gather.10.cloned.1.call-done = bf16[8,256,1792]{2,0,1:T(8,128)(2,1)} async-done(((bf16[8,64,1792]{2,0,1:T(8,128)(2,1)}), bf16[8,256,1792]{2,0,1:T(8,128)(2,1)}) %all-gather.10.cloned.1.call-update) | async-done | bytes 7340048 | tf_op jit(solution)/shard_map/all_gather | solution.py:187
  114.0 7.4 copy.86
  121.4 117.0 %all-gather.8.cloned.1.call-done = bf16[8,256,2048]{2,1,0:T(8,128)(2,1)} async-done(((bf16[1,256,2048]{2,1,0:T(8,128)(2,1)}), bf16[8,256,2048]{2,1,0:T(8,128)(2,1)}) %all-gather.8.cloned.1.call-update) | async-done | bytes 8388624 | tf_op jit(solution)/shard_map/all_gather | solution.py:199
  238.4 4.7 convert_reduce_fusion.1
  244.2 2.4 multiply_reduce_fusion.2
  246.6 7.6 add_convert_fusion.3
  254.2 3.3 copy-done.5
  257.4 10.4 broadcast_add_fusion
  267.8 6.6 copy.87
  274.4 5.8 copy.117
  281.9 1.7 fusion.42
  284.9 78.8 %all-gather.12.cloned.1.call-done = bf16[8,256,2048]{2,1,0:T(8,128)(2,1)} async-done(((bf16[1,256,2048]{2,1,0:T(8,128)(2,1)}), bf16[8,256,2048]{2,1,0:T(8,128)(2,1)}) %all-gather.12.cloned.1.call-update) | async-done | bytes 8388624 | tf_op jit(solution)/shard_map/all_gather | solution.py:200
  363.7 7.0 convolution_convert_fusion.4
  370.7 3.1 copy.90
  373.8 2.6 fusion.28
  377.2 2.9 copy.91
  380.2 5.9 all-to-all-start.1
  386.9 48.2 %all_gather.29 = s32[1,1024]{1,0:T(1,128)S(1)} all-gather(s32[1,256]{1,0:T(1,128)S(1)} %copy-done.25), channel_id=1, replica_groups=mesh['dp'=8,'ctx'=4] {'ctx'}, dimensions={1}, use_global_device_ids=true | all-gather | bytes 5120 | tf_op jit(solution)/shard_map/all_gather | solution.py:201
  435.0 21.1 %all-gather.2 = s32[8,1,1024]{2,1,0:T(1,128)S(1)} all-gather(s32[1,1,1024]{2,1,0:T(1,128)S(1)} %bitcast.239), channel_id=1, replica_groups=mesh['dp'=8,'ctx'=4] {'dp'}, dimensions={0}, use_global_device_ids=true | all-gather | bytes 36864 | tf_op jit(solution)/shard_map/all_gather | solution.py:202
  457.5 1.9 multiply_sine_fusion
  460.0 14.5 %fusion.9 = f32[2048,1024]{1,0:T(8,128)} fusion(bf16[2048,2048]{1,0:T(8,128)(2,1)} %get-tuple-element.37, bf16[2048,1792]{1,0:T(8,128)(2,1)} %bitcast.197), kind=kOutput, calls=%fused_computation.38 | convolution fusion | flops 8589934592 | bytes 20971520 | tf_op jit(solution)/shard_map/dot_general | solution.py:20
  474.5 6.2 copy.92
  480.7 2.6 fusion.45
  487.4 10.5 shard_map.220
  497.9 2.4 pad_maximum_fusion.2
  500.3 8.5 copy.98
  508.8 11.4 all-to-all-start.2
  520.2 32.9 %convert_reduce_fusion.2 = (f32[1024]{0:T(1024)S(1)}, bf16[2048,1024]{1,0:T(8,128)(2,1)S(1)}, f32[2048,1024]{1,0:T(8,128)}) fusion(f32[2048,1024]{1,0:T(8,128)} %fusion.9, f32[1024]{0:T(1024)S(1)} %bitcast.240, bf16[2048,2048]{1,0:T(8,128)(2,1)} %bitcast.176, bf16[1024,2048]{1,0:T(8,128)(2,1)} %param.23), kind=kOutput, calls=%fused_computation.13 | convolution fusion | flops 8747219968 | bytes 33562624 | tf_op jit(solution)/shard_map/dot_general | solution.py:24
  553.1 2.0 copy-done.30
  555.1 12.9 convolution_convert_fusion.1
  568.0 3.2 copy.99
  574.0 8.1 convolution_convert_fusion.2
  582.1 6.5 pad_maximum_fusion
  588.6 9.2 copy.123
  597.8 11.6 copy.104
  610.0 4.7 convert_reduce_fusion
  614.8 11.7 multiply_convert_fusion
  626.5 14.3 %convolution_convert_fusion = bf16[1024,2048]{1,0:T(8,128)(2,1)} fusion(bf16[2048,1024]{1,0:T(8,128)(2,1)} %multiply_convert_fusion, bf16[2048,2048]{1,0:T(8,128)(2,1)} %bitcast.177), kind=kOutput, calls=%fused_computation.34 | convolution fusion | flops 8592031744 | bytes 16777216 | tf_op jit(solution)/shard_map/dot_general | solution.py:28
  643.0 11.9 fusion.11
  654.9 22.8 %fusion.38 = (f32[2048]{0:T(1024)S(1)}, f32[2048]{0:T(1024)S(1)}, bf16[2048,2048]{1,0:T(8,128)(2,1)}, f32[2048]{0:T(1024)S(1)}, f32[2048]{0:T(1024)S(1)}) fusion(f32[2048]{0:T(1024)S(1)} %bitcast.235, f32[2048]{0:T(1024)S(1)} %bitcast.233, bf16[8,256,2048]{2,1,0:T(8,128)(2,1)} %all-gather.8.cloned.1.call-done, f32[2048]{0:T(1024)S(1)} %bitcast.231, ...), kind=kOutput, calls=%fused_computation.126 | convolution fusion | flops 8644452352 | bytes 42008576 | tf_op jit(solution)/shard_map/dot_general | solution.py:24
  678.5 6.7 convolution_convert_fusion.3
  686.2 15.2 %fusion.48 = f32[2048,2048]{1,0:T(8,128)} fusion(bf16[2048,1024]{1,0:T(8,128)(2,1)} %multiply_convert_fusion, bf16[1024,2048]{1,0:T(8,128)(2,1)} %param.23), kind=kOutput, calls=%fused_computation.135 | convolution fusion | flops 8589934592 | bytes 25165824 | tf_op jit(solution)/shard_map/dot_general | solution.py:20
  701.4 11.5 add_convert_fusion.1
  713.0 1.9 copy.105
  714.8 48.5 %all_to_all.41 = bf16[8,64,1792]{2,1,0:T(8,128)(2,1)S(1)} all-to-all(bf16[8,64,1792]{2,1,0:T(8,128)(2,1)S(1)} %copy.105), channel_id=1, replica_groups=mesh['dp'=8,'ctx'=4] {'dp'}, dimensions={0} | all-to-all | bytes 3670016 | tf_op jit(solution)/shard_map/all_to_all | solution.py:311
  763.3 2.2 copy.106
  767.0 39.9 %all-reduce.4.cloned.1.call-done = f32[24576]{0:T(1024)} async-done(((f32[24576]{0:T(1024)}), f32[24576]{0:T(1024)}) %all-reduce.4.cloned.1.call-update) | async-done | bytes 98320 | tf_op jit(solution)/shard_map/psum | solution.py:273
  807.7 1.4 dynamic_slice.47
  811.5 102.7 %all-reduce.6.cloned.1.call-done = (bf16[256,2048]{1,0:T(8,128)(2,1)}, bf16[1024,2048]{1,0:T(8,128)(2,1)}) async-done(((bf16[256,2048]{1,0:T(8,128)(2,1)}, bf16[1024,2048]{1,0:T(8,128)(2,1)}), (bf16[256,2048]{1,0:T(8,128)(2,1)}, bf16[1024,2048]{1,0:T(8,128)(2,1)})) %all-reduce.6.cloned.1.call-update) | async-done | bytes 5242896 | tf_op jit(solution)/shard_map/psum | solution.py:307
  914.2 2.8 convert_element_type.188
  917.0 6.7 convert_element_type.193
  923.7 143.5 %reduce-scatter.6.cloned.1.call-done = bf16[256,2048]{1,0:T(8,128)(2,1)} async-done(((bf16[2048,2048]{1,0:T(8,128)(2,1)}), bf16[256,2048]{1,0:T(8,128)(2,1)}) %reduce-scatter.6.cloned.1.call-update) | async-done | bytes 1048592 | tf_op jit(solution)/shard_map/reduce_scatter | solution.py:243
  1067.2 1.9 convert_reduce_fusion.4
  1069.1 149.8 %reduce-scatter.4.cloned.1.call-done = bf16[256,2048]{1,0:T(8,128)(2,1)} async-done(((bf16[2048,2048]{1,0:T(8,128)(2,1)}), bf16[256,2048]{1,0:T(8,128)(2,1)}) %reduce-scatter.4.cloned.1.call-update) | async-done | bytes 1048592 | tf_op jit(solution)/shard_map/reduce_scatter | solution.py:234
  1218.9 4.0 fusion.32
  1222.9 51.0 %all-gather.14.cloned.1.call-done = bf16[8,256,1792]{2,0,1:T(8,128)(2,1)} async-done(((bf16[8,64,1792]{2,0,1:T(8,128)(2,1)}), bf16[8,256,1792]{2,0,1:T(8,128)(2,1)}) %all-gather.14.cloned.1.call-update) | async-done | bytes 7340048 | tf_op jit(solution)/shard_map/all_gather | solution.py:314
  1274.0 3.2 slice_convert_fusion
  1277.2 11.3 copy.125
  1288.4 1.9 slice-done
  1290.8 5.3 copy.124
  (177 shorter events, 30.2 us)
Async XLA Ops:
  7.2 1.9 copy-start
  7.2 106.8 %all-gather.10.cloned.1.call-start = ((), (), s32[]{:S(2)}) async-start(), calls=%async_computation.8 | async-start | bytes 9175040 | tf_op jit(solution)/shard_map/all_gather | solution.py:187
  11.3 48.9 %copy-start.26 = (bf16[2,256]{1,0:T(2,128)(2,1)S(1)}, bf16[2,256]{1,0:T(2,128)(2,1)}, u32[]{:S(2)}) copy-start(bf16[2,256]{1,0:T(2,128)(2,1)} %param.15) | copy-start | bytes 3076
  11.3 48.9 %copy-start.27 = (bf16[2,256]{1,0:T(2,128)(2,1)S(1)}, bf16[2,256]{1,0:T(2,128)(2,1)}, u32[]{:S(2)}) copy-start(bf16[2,256]{1,0:T(2,128)(2,1)} %param.16) | copy-start | bytes 3076
  11.4 49.3 %copy-start.24 = (bf16[768]{0:T(1024)(128)(2,1)S(1)}, bf16[768]{0:T(1024)(128)(2,1)}, u32[]{:S(2)}) copy-start(bf16[768]{0:T(1024)(128)(2,1)} %param.18) | copy-start | bytes 4612
  11.4 49.5 %copy-start.28 = (bf16[256]{0:T(256)(128)(2,1)S(1)}, bf16[256]{0:T(256)(128)(2,1)}, u32[]{:S(2)}) copy-start(bf16[256]{0:T(256)(128)(2,1)} %param.20) | copy-start | bytes 1540
  11.4 49.7 %copy-start.23 = (bf16[1024]{0:T(1024)(128)(2,1)S(1)}, bf16[1024]{0:T(1024)(128)(2,1)}, u32[]{:S(2)}) copy-start(bf16[1024]{0:T(1024)(128)(2,1)} %param.22) | copy-start | bytes 6148
  11.4 49.7 %copy-start.29 = (bf16[256]{0:T(256)(128)(2,1)S(1)}, bf16[256]{0:T(256)(128)(2,1)}, u32[]{:S(2)}) copy-start(bf16[256]{0:T(256)(128)(2,1)} %param.24) | copy-start | bytes 1540
  58.5 179.9 %all-gather.8.cloned.1.call-start = ((), (), s32[]{:S(2)}) async-start(), calls=%async_computation.7 | async-start | bytes 9437184 | tf_op jit(solution)/shard_map/all_gather | solution.py:199
  59.3 304.5 %all-gather.12.cloned.1.call-start = ((), (), s32[]{:S(2)}) async-start(), calls=%async_computation.9 | async-start | bytes 9437184 | tf_op jit(solution)/shard_map/all_gather | solution.py:200
  85.2 36.1 %copy-start.12 = (f32[8,1,3328]{2,0,1:T(8,128)}, f32[8,1,3328]{2,0,1:T(8,128)S(1)}, u32[]{:S(2)}) copy-start(f32[8,1,3328]{2,0,1:T(8,128)S(1)} %copy.128) | copy-start | bytes 319492
  85.4 161.2 %copy-start.14 = (f32[1,2,8,128]{3,1,2,0:T(2,128)}, f32[1,2,8,128]{3,1,2,0:T(2,128)S(1)}, u32[]{:S(2)}) copy-start(f32[1,2,8,128]{3,1,2,0:T(2,128)S(1)} %copy.113) | copy-start | bytes 24580
  85.4 161.2 %copy-start.16 = (f32[1,2,8,128]{3,1,2,0:T(2,128)}, f32[1,2,8,128]{3,1,2,0:T(2,128)S(1)}, u32[]{:S(2)}) copy-start(f32[1,2,8,128]{3,1,2,0:T(2,128)S(1)} %copy.118) | copy-start | bytes 24580
  238.4 5.8 copy-start.2
  243.1 11.1 copy-start.18
  246.6 7.6 copy-start.20
  254.2 3.3 copy-start.5
  280.3 4.4 copy-start.3
  373.8 2.6 copy-start.8
  373.8 2.8 copy-start.9
  373.8 2.8 copy-start.10
  377.2 9.7 copy-start.25
  380.2 94.3 %all-to-all-start.1 = ((bf16[4,8,256,256]{2,3,0,1:T(8,128)(2,1)}), bf16[4,8,256,256]{2,3,0,1:T(8,128)(2,1)}, u32[]{:S(2)}, u32[]{:S(2)}) async-start(bf16[4,8,256,256]{2,3,0,1:T(8,128)(2,1)} %copy.91), calls=%async_computation.1 | async-start | bytes 8388608 | tf_op jit(solution)/shard_map/all_to_all | solution.py:217
  508.8 59.2 %all-to-all-start.2 = ((bf16[4,2,1024,256]{3,1,0,2:T(2,128)(2,1)}), bf16[4,2,1024,256]{3,1,0,2:T(2,128)(2,1)}, u32[]{:S(2)}, u32[]{:S(2)}) async-start(bf16[4,2,1024,256]{3,1,0,2:T(2,128)(2,1)} %copy.98), calls=%async_computation.2 | async-start | bytes 8388608 | tf_op jit(solution)/shard_map/all_to_all | solution.py:223
  520.2 192.7 %reduce-scatter.8.cloned.1.call-start = ((), (), s32[]{:S(2)}) async-start(), calls=%async_computation.13 | async-start | bytes 9175040 | tf_op jit(solution)/shard_map/reduce_scatter | solution.py:310
  553.1 2.0 copy-start.30
  568.0 4.7 slice-start.1
  571.2 2.8 slice-start.2
  572.7 68.1 %copy-start.6 = (bf16[1,4,2,256,256]{4,3,2,1,0:T(8,128)(2,1)}, bf16[1,4,2,256,256]{4,3,2,1,0:T(8,128)(2,1)S(1)}, u32[]{:S(2)}) copy-start(bf16[1,4,2,256,256]{4,3,2,1,0:T(8,128)(2,1)S(1)} %copy.102) | copy-start | bytes 3145732
  609.4 197.4 %all-reduce.4.cloned.1.call-start = ((), (), s32[]{:S(2)}) async-start(), calls=%async_computation.12 | async-start | bytes 196608 | tf_op jit(solution)/shard_map/psum | solution.py:273
  642.9 11.9 copy-start.15
  642.9 11.9 copy-start.17
  642.9 11.9 copy-start.19
  642.9 11.9 copy-start.21
  677.8 0.6 copy-start.13
  678.4 235.7 %all-reduce.6.cloned.1.call-start = ((), (), s32[]{:S(2)}) async-start(), calls=%async_computation.15 | async-start | bytes 10485760 | tf_op jit(solution)/shard_map/psum | solution.py:307
  685.2 382.0 %reduce-scatter.6.cloned.1.call-start = ((), (), s32[]{:S(2)}) async-start(), calls=%async_computation.11 | async-start | bytes 9437184 | tf_op jit(solution)/shard_map/reduce_scatter | solution.py:243
  686.0 15.4 %copy-start.11 = (bf16[256,2048]{1,0:T(8,128)(2,1)S(1)}, bf16[256,2048]{1,0:T(8,128)(2,1)}, u32[]{:S(2)}) copy-start(bf16[256,2048]{1,0:T(8,128)(2,1)} %param.19) | copy-start | bytes 3145732
  686.0 532.9 %reduce-scatter.4.cloned.1.call-start = ((), (), s32[]{:S(2)}) async-start(), calls=%async_computation.10 | async-start | bytes 9437184 | tf_op jit(solution)/shard_map/reduce_scatter | solution.py:234
  712.9 53.5 %copy-start.4 = (bf16[1,256,2048]{2,1,0:T(8,128)(2,1)S(1)}, bf16[1,256,2048]{2,1,0:T(8,128)(2,1)}, u32[]{:S(2)}) copy-start(bf16[1,256,2048]{2,1,0:T(8,128)(2,1)} %param.13) | copy-start | bytes 3145732
  712.9 561.1 %all-gather.14.cloned.1.call-start = ((), (), s32[]{:S(2)}) async-start(), calls=%async_computation.14 | async-start | bytes 9175040 | tf_op jit(solution)/shard_map/all_gather | solution.py:314
  807.7 488.5 %copy-start.22 = (f32[256]{0:T(256)}, f32[256]{0:T(256)S(1)}, u32[]{:S(2)}) copy-start(f32[256]{0:T(256)S(1)} %get-tuple-element.102) | copy-start | bytes 3076
  917.0 301.9 %copy-start.7 = (bf16[1,256,2048]{2,1,0:T(8,128)(2,1)S(1)}, bf16[1,256,2048]{2,1,0:T(8,128)(2,1)}, u32[]{:S(2)}) copy-start(bf16[1,256,2048]{2,1,0:T(8,128)(2,1)} %param.25) | copy-start | bytes 3145732
  1288.4 1.9 slice-start
  1290.3 6.4 copy-start.1
Sparse Core Ops, SparseCore 0:
  58.6 55.2 all-gather.9
  116.1 122.2 all-gather.7
  240.5 123.1 all-gather.11
  609.6 68.0 reduce-scatter.7
  684.5 122.2 all-reduce.3
  809.9 104.2 all-reduce.5
  918.8 148.3 reduce-scatter.5
  1070.8 148.0 reduce-scatter.3
  1221.1 52.8 all-gather.13

commit v2 on v1

v2 whole, which is shorter than its diff:
```python
from functools import partial

import jax
import jax.numpy as jnp
from jax import lax
from jax.experimental import pallas as pl
from jax.experimental.pallas import tpu as pltpu
from jax.sharding import PartitionSpec as P

HEADS = 8
HEAD = 256
ROT = 64
EPSILON = 1e-05
MASKED = -1e30
F32 = jnp.float32
BF16 = jnp.bfloat16
MESH = pl.DeviceIdType.MESH
TEAM = HEADS
PAIRS = TEAM // 2
QUARTERS = 4
RIGHT, LEFT = 0, 1
VECTOR_ROWS = 24


def dot(left, right):
    return jnp.dot(left, right, preferred_element_type=F32)


def contract_last(left, right):
    return lax.dot_general(left, right, (((1,), (1,)), ((), ())), preferred_element_type=F32)


def contract_first(left, right):
    return lax.dot_general(left, right, (((0,), (0,)), ((), ())), preferred_element_type=F32)


def rotary_tables(positions):
    half = ROT // 2
    exponent = jnp.arange(0, ROT, 2).astype(F32) / ROT
    frequency = 10000.0 ** (-exponent)
    angles = positions[:, None] * frequency[None, :]
    rows = positions.shape[0]
    cosine, sine = jnp.cos(angles), jnp.sin(angles)
    one, nought = jnp.ones((rows, 64), F32), jnp.zeros((rows, 64), F32)
    blank = jnp.zeros((rows, half), F32)
    return (
        jnp.concatenate([cosine, cosine, one], -1),
        jnp.concatenate([-sine, blank, nought], -1),
        jnp.concatenate([blank, sine, nought], -1),
    )


def spot():
    place = lax.axis_index("dp")
    rank = lax.rem(place, TEAM)
    return place - rank, lax.div(rank, 2), lax.rem(rank, 2), lax.axis_index("ctx")


def near_first(line):
    second = 1 + lax.rem(line, 2)
    last = 3 * (1 - lax.div(line, 2))
    return (line, second, 6 - line - second - last, last)


def core_peer(quarter):
    return quarter + 1 - 2 * lax.rem(quarter, 2)


def chip_peer(quarter):
    return quarter + 2 - 4 * lax.div(quarter, 2)


def send(src, dst, send_sem, recv_sem, place, quarter):
    return pltpu.make_async_remote_copy(
        src_ref=src, dst_ref=dst, send_sem=send_sem, recv_sem=recv_sem,
        device_id=(place, quarter), device_id_type=MESH,
    )


def greet_line(base, line, side, quarter):
    barrier = pltpu.get_barrier_semaphore()

    def hail(place, quarter):
        pl.semaphore_signal(barrier, inc=1, device_id=(place, quarter), device_id_type=MESH)

    rank = line * 2 + side
    hail(base + line * 2 + 1 - side, quarter)

    pl.when(line < PAIRS - 1)(lambda: hail(base + rank + 2, quarter))
    pl.when(line > 0)(lambda: hail(base + rank - 2, quarter))
    for step in range(1, QUARTERS):
        hail(base + rank, lax.rem(quarter + step, QUARTERS))
    neighbours = 1 + lax.div(line + 2, 3) - lax.div(line, 3)
    pl.semaphore_wait(barrier, neighbours + QUARTERS)


def greet_team(base, line, side, quarter):
    barrier = pltpu.get_barrier_semaphore()
    rank = line * 2 + side
    for step in range(1, TEAM):
        pl.semaphore_signal(
            barrier, inc=1, device_id=(base + lax.rem(rank + step, TEAM), quarter),
            device_id_type=MESH,
        )
    for step in range(1, QUARTERS):
        pl.semaphore_signal(
            barrier, inc=1, device_id=(base + rank, lax.rem(quarter + step, QUARTERS)),
            device_id_type=MESH,
        )
    pl.semaphore_wait(barrier, TEAM + QUARTERS - 2)


class Relay:
    def __init__(self, held, line_send, line_recv, side_send, side_recv):
        self.held = held
        self.sems = line_send, line_recv, side_send, side_recv
        self.base, self.line, self.side, self.quarter = spot()

    def along(self, source, way):
        line_send, line_recv, _, _ = self.sems
        block = self.held.at[source * 2 + self.side]
        place = self.base + self.line * 2 + self.side + (2 if way == RIGHT else -2)
        return send(
            block, block, line_send.at[way, source], line_recv.at[source], place, self.quarter
        )

    def over(self, source, side):
        _, _, side_send, side_recv = self.sems
        block = self.held.at[source * 2 + side]
        place = self.base + self.line * 2 + 1 - self.side
        return send(block, block, side_send.at[source], side_recv.at[source], place, self.quarter)

    def each(self, step, act):
        line = self.line
        if step == 0:
            pl.when(line < PAIRS - 1)(lambda: act(line, RIGHT))
            pl.when(line > 0)(lambda: act(line, LEFT))
            act(line, None)
            return

        @pl.when(line >= step)
        def _():
            source = line - step
            act(source, "arrive")
            pl.when(line < PAIRS - 1)(lambda: act(source, RIGHT))
            act(source, None)

        @pl.when(line + step < PAIRS)
        def _():
            source = line + step
            act(source, "arrive")
            pl.when(line > 0)(lambda: act(source, LEFT))
            act(source, None)

    def start(self, step):
        def act(source, way):
            if way == "arrive":
                self.along(source, RIGHT).wait_recv()
            elif way is None:
                self.over(source, self.side).start()
            else:
                self.along(source, way).start()

        self.each(step, act)

    def finish(self):
        def act(source, way):
            if way is None:
                self.over(source, self.side).wait_send()
            elif way != "arrive":
                self.along(source, way).wait_send()

        for step in range(PAIRS):
            self.each(step, act)

    def wait_over(self, source):
        self.over(source, 1 - self.side).wait_recv()


RELAY_SEMS = [
    pltpu.SemaphoreType.DMA((2, PAIRS)),
    pltpu.SemaphoreType.DMA((PAIRS,)),
    pltpu.SemaphoreType.DMA((PAIRS,)),
    pltpu.SemaphoreType.DMA((PAIRS,)),
]


def normalize(rows):
    average = jnp.mean(rows, -1, keepdims=True)
    centred = rows - average
    variance = jnp.mean(centred * centred, -1, keepdims=True)
    inverse = lax.rsqrt(variance + EPSILON)
    return centred * inverse, inverse


def rotate_low(low, cosine, above, below):
    half = ROT // 2
    return (
        low * cosine + pltpu.roll(low, 128 - half, 1) * above + pltpu.roll(low, half, 1) * below
    )


def unrotate_low(low, cosine, above, below):
    half = ROT // 2
    return (
        low * cosine + pltpu.roll(low * below, 128 - half, 1) + pltpu.roll(low * above, half, 1)
    )


class Spread:
    def __init__(self, pieces, send_sem, recv_sem, own_sem):
        self.pieces, self.sems = pieces, (send_sem, recv_sem, own_sem)
        base, line, side, self.quarter = spot()
        self.place = base + line * 2 + side

    def _remote(self, index, sequence, to, origin):
        src, dst = self.pieces[index]
        send_sem, recv_sem, _ = self.sems
        return send(
            src(sequence), dst(lax.rem(sequence, 2), origin), send_sem.at[index, sequence],
            recv_sem.at[index, origin, lax.rem(sequence, 2)], self.place, to,
        )

    def _own(self, index, sequence):
        src, dst = self.pieces[index]
        return pltpu.make_async_copy(
            src(sequence), dst(lax.rem(sequence, 2), self.quarter),
            self.sems[2].at[index, lax.rem(sequence, 2)],
        )

    def start(self, sequence):
        to = lax.div(sequence, 2)

        @pl.when(to == self.quarter)
        def _():
            for index in range(len(self.pieces)):
                self._own(index, sequence).start()

        @pl.when(to != self.quarter)
        def _():
            for index in range(len(self.pieces)):
                self._remote(index, sequence, to, self.quarter).start()

    def finish(self):
        def sent(sequence, _):
            to = lax.div(sequence, 2)

            @pl.when(to == self.quarter)
            def _():
                for index in range(len(self.pieces)):
                    self._own(index, sequence).wait()

            @pl.when(to != self.quarter)
            def _():
                for index in range(len(self.pieces)):
                    self._remote(index, sequence, to, self.quarter).wait_send()

        lax.fori_loop(0, TEAM, sent, None)

        def landed(step, _):
            origin = lax.rem(self.quarter + 1 + lax.div(step, 2), QUARTERS)
            sequence = lax.rem(step, 2)
            for index in range(len(self.pieces)):
                self._remote(index, sequence, origin, origin).wait_recv()

        lax.fori_loop(0, 2 * (QUARTERS - 1), landed, None)


def spread_sems(count):
    return [
        pltpu.SemaphoreType.DMA((count, TEAM)),
        pltpu.SemaphoreType.DMA((count, QUARTERS, 2)),
        pltpu.SemaphoreType.DMA((count, 2)),
    ]


def first_kernel(
    x_ref, wq_ref, wu_ref, vec_ref, upb_ref, cos_ref, above_ref, below_ref,
    x_out, ha_out, hm_out, u_out, w_out, qkv_out, seg_out, vec_out,
    held, weight, vecs, ha, hm, up, qkv, vectors,
    own_sem, store_sem, w_send, w_recv, w_own, core_send, core_recv, chip_send, chip_recv,
    last_send, last_recv, v_send, v_recv, spread_send, spread_recv, spread_own, *relay_sems,
):
    base, line, side, quarter = spot()
    rank = line * 2 + side
    tokens, width = x_ref.shape
    rows = wq_ref.shape[0]
    part = rows // QUARTERS
    hidden = up.shape[-1]
    core, chip = core_peer(quarter), chip_peer(quarter)
    relay = Relay(held, *relay_sems)
    spread = Spread(
        [
            (
                lambda s: qkv.at[s],
                lambda j, origin: qkv_out.at[j, :, pl.ds(origin * tokens, tokens), :],
            ),
            (lambda s: vecs.at[s, pl.ds(16, 8), :], lambda j, origin: seg_out.at[j, origin]),
        ],
        spread_send, spread_recv, spread_own,
    )
    greet_team(base, line, side, quarter)

    own_x = pltpu.make_async_copy(x_ref, held.at[rank], own_sem.at[0])
    own_x.start()
    own_v = pltpu.make_async_copy(vec_ref, vecs.at[rank], own_sem.at[1])
    own_v.start()

    def band(origin, slice_of):
        return pl.ds(pl.multiple_of(origin * rows + slice_of * part, 16), part)

    def columns(source, target):
        mine = pl.ds(pl.multiple_of(quarter * part, 16), part)
        pieces = []
        for kind in range(3):
            start = pl.multiple_of(kind * width + target * HEAD, HEAD)
            pieces.append(
                (
                    wq_ref.at[mine, pl.ds(start, HEAD)],
                    weight.at[band(source, quarter), pl.ds(kind * HEAD, HEAD)],
                )
            )
        start = pl.multiple_of(target * hidden, hidden)
        pieces.append(
            (
                wu_ref.at[mine, pl.ds(start, hidden)],
                weight.at[band(source, quarter), pl.ds(3 * HEAD, hidden)],
            )
        )
        return pieces

    def column_copies(source, target, peer):
        return [
            send(src, dst, w_send.at[kind, target], w_recv.at[kind, source], base + peer, quarter)
            for kind, (src, dst) in enumerate(columns(source, target))
        ]

    def vector_copy(source, target, peer):
        return send(
            vec_ref, vecs.at[source], v_send.at[target], v_recv.at[source], base + peer, quarter
        )

    def send_columns(step, _):
        target = lax.rem(rank + step, TEAM)
        vector_copy(rank, target, target).start()
        for copy in column_copies(rank, target, target):
            copy.start()

    lax.fori_loop(1, TEAM, send_columns, None)
    own_columns = [
        pltpu.make_async_copy(src, dst, w_own.at[kind])
        for kind, (src, dst) in enumerate(columns(rank, rank))
    ]
    for copy in own_columns:
        copy.start()
    own_x.wait()
    own_v.wait()
    relay.start(0)

    def pass_on(origin, slice_of, sends, recvs, to):
        block = weight.at[band(origin, slice_of), :]
        return send(block, block, sends.at[origin], recvs.at[origin], base + rank, to)

    def to_core(origin):
        return pass_on(origin, quarter, core_send, core_recv, core)

    def to_chip(origin):
        return pass_on(origin, quarter, chip_send, chip_recv, chip)

    def to_last(origin):
        return pass_on(origin, chip, last_send, last_recv, core)

    for copy in own_columns:
        copy.wait()
    to_chip(rank).start()
    to_core(rank).start()

    def forward_columns(step, _):
        origin = lax.rem(rank + TEAM - step, TEAM)
        for copy in column_copies(origin, rank, origin):
            copy.wait_recv()
        to_chip(origin).start()
        to_core(origin).start()

    lax.fori_loop(1, TEAM, forward_columns, None)
    relay.start(1)

    def forward_chip(step, _):
        origin = lax.rem(rank + TEAM - step, TEAM)
        pass_on(origin, chip, chip_send, chip_recv, chip).wait_recv()
        to_last(origin).start()

    lax.fori_loop(0, TEAM, forward_chip, None)
    relay.start(2)

    def take_vectors(step, _):
        origin = lax.rem(rank + TEAM - step, TEAM)
        vector_copy(origin, rank, origin).wait_recv()

    lax.fori_loop(1, TEAM, take_vectors, None)
    for source in range(TEAM):
        for row in range(4):
            vectors[pl.ds(row, 1), pl.ds(source * rows, rows)] = vecs[source, pl.ds(row, 1), :]

    def last_columns(step, _):
        origin = lax.rem(rank + TEAM - step, TEAM)
        pass_on(origin, core, core_send, core_recv, core).wait_recv()
        pass_on(origin, chip_peer(core), last_send, last_recv, core).wait_recv()

    lax.fori_loop(0, TEAM, last_columns, None)
    stores = [
        pltpu.make_async_copy(weight, w_out, store_sem.at[0]),
        pltpu.make_async_copy(vecs, vec_out, store_sem.at[1]),
    ]
    for copy in stores:
        copy.start()

    strip = 32

    def work(which):
        def norm(index, _):
            chunk = pl.ds(pl.multiple_of(index * strip, strip), strip)
            unit, _ = normalize(held[which, chunk, :].astype(F32))
            ha[which, chunk, :] = (unit * vectors[0:1, :] + vectors[2:3, :]).astype(BF16)
            hm[which, chunk, :] = (unit * vectors[1:2, :] + vectors[3:4, :]).astype(BF16)

        lax.fori_loop(0, tokens // strip, norm, None)
        for kind in range(3):
            chunk = kind * TEAM + rank
            bias = vecs[lax.div(chunk, 3), pl.ds(8 + lax.rem(chunk, 3), 1), :]
            made = dot(ha[which], weight[:, pl.ds(kind * HEAD, HEAD)]) + bias
            if kind < 2:
                low = rotate_low(made[:, :128], cos_ref[...], above_ref[...], below_ref[...])
                qkv[which, kind, :, pl.ds(0, 128)] = low.astype(BF16)
                qkv[which, kind, :, pl.ds(128, HEAD - 128)] = made[:, 128:].astype(BF16)
            else:
                qkv[which, kind] = made.astype(BF16)
        spread.start(which)
        for start in range(0, hidden, 256):
            span = pl.ds(start, 256)
            up[which, :, span] = (
                dot(hm[which], weight[:, pl.ds(3 * HEAD + start, 256)]) + upb_ref[:, span]
            )

    for step, place in enumerate(near_first(line)):

        def one(other, _, step=step, place=place):
            @pl.when(other == 1)
            def _():
                if step == 0:
                    relay.start(3)
                relay.wait_over(place)

            work(place * 2 + side + other * (1 - 2 * side))

        lax.fori_loop(0, 2, one, None)

    for index, (src, dst) in enumerate(((held, x_out), (ha, ha_out), (hm, hm_out), (up, u_out))):
        stores.append(pltpu.make_async_copy(src, dst, store_sem.at[2 + index]))
        stores[-1].start()
    relay.finish()
    spread.finish()

    def sent(step, _):
        target = lax.rem(rank + step, TEAM)
        vector_copy(rank, target, target).wait_send()
        for copy in column_copies(rank, target, target):
            copy.wait_send()

    lax.fori_loop(1, TEAM, sent, None)

    def passed(origin, _):
        to_core(origin).wait_send()
        to_chip(origin).wait_send()
        to_last(origin).wait_send()

    lax.fori_loop(0, TEAM, passed, None)
    for copy in stores:
        copy.wait()


ANY = pl.BlockSpec(memory_space=pl.ANY)
VMEM = pl.BlockSpec(memory_space=pltpu.VMEM)
DMA = pltpu.SemaphoreType.DMA
LIMIT = 60 << 20


def first(x, w_qkv, w_up, vec, up_bias, tables):
    tokens, width = x.shape
    hidden = up_bias.shape[-1]
    span = 3 * HEAD + hidden
    shapes = [
        ((TEAM, tokens, width), BF16),
        ((TEAM, tokens, width), BF16),
        ((TEAM, tokens, width), BF16),
        ((TEAM, tokens, hidden), F32),
        ((width, span), BF16),
        ((2, 3, QUARTERS * tokens, HEAD), BF16),
        ((2, QUARTERS, 8, tokens), F32),
        ((TEAM, VECTOR_ROWS, vec.shape[-1]), F32),
    ]
    return pl.pallas_call(
        first_kernel,
        out_shape=[jax.ShapeDtypeStruct(*shape) for shape in shapes],
        in_specs=[VMEM, ANY, ANY, VMEM, VMEM, VMEM, VMEM, VMEM],
        out_specs=[ANY] * len(shapes),
        scratch_shapes=[
            pltpu.VMEM((TEAM, tokens, width), BF16),
            pltpu.VMEM((width, span), BF16),
            pltpu.VMEM((TEAM, VECTOR_ROWS, vec.shape[-1]), F32),
            pltpu.VMEM((TEAM, tokens, width), BF16),
            pltpu.VMEM((TEAM, tokens, width), BF16),
            pltpu.VMEM((TEAM, tokens, hidden), F32),
            pltpu.VMEM((TEAM, 3, tokens, HEAD), BF16),
            pltpu.VMEM((8, width), F32),
            DMA((2,)),
            DMA((6,)),
            DMA((4, TEAM)),
            DMA((4, TEAM)),
            DMA((4,)),
        ]
        + [DMA((TEAM,))] * 8
        + spread_sems(2)
        + RELAY_SEMS,
        compiler_params=pltpu.CompilerParams(
            collective_id=0, has_side_effects=True, vmem_limit_bytes=LIMIT
        ),
        name="gather_x",
    )(x, w_qkv, w_up, vec, up_bias, *tables)


def gelu_terms(values):
    chance = 0.5 * (1.0 + lax.erf(values * (0.5**0.5)))
    density = jnp.exp(-0.5 * values * values) * 0.3989422804014327
    return values * chance, chance + values * density


def second_kernel(
    dy_ref, wo_ref, wd_ref, u_ref, o_ref,
    dy_out, a_out, du_out, do_out, o_out, sum_out,
    held, up, act, grad, attended,
    own_sem, load_sem, store_sem, back_send, back_recv, spread_send, spread_recv, spread_own,
    *relay_sems,
):
    base, line, side, quarter = spot()
    rank = line * 2 + side
    tokens, width = dy_ref.shape
    hidden = up.shape[-1]
    relay = Relay(held, *relay_sems)
    spread = Spread(
        [
            (
                lambda s: attended.at[s],
                lambda j, origin: do_out.at[j, pl.ds(origin * tokens, tokens), :],
            )
        ],
        spread_send, spread_recv, spread_own,
    )
    loads = pltpu.make_async_copy(u_ref, up, load_sem)
    loads.start()
    greet_line(base, line, side, quarter)
    own = pltpu.make_async_copy(dy_ref, held.at[rank], own_sem.at[0])
    own.start()
    own.wait()
    relay.start(0)

    def back(to, origin):
        return send(
            o_ref.at[:, pl.ds(to * tokens, tokens), :], o_out.at[pl.ds(2 * origin, 2)],
            back_send.at[to], back_recv.at[origin], base + rank, to,
        )

    own_back = pltpu.make_async_copy(
        o_ref.at[:, pl.ds(quarter * tokens, tokens), :], o_out.at[pl.ds(2 * quarter, 2)],
        own_sem.at[1],
    )
    own_back.start()
    for step in range(1, QUARTERS):
        back(lax.rem(quarter + step, QUARTERS), quarter).start()
    loads.wait()
    sum_out[...] = jnp.zeros_like(sum_out)

    def work(which):
        attended[which] = contract_last(held[which], wo_ref[...]).astype(BF16)
        spread.start(which)
        for start in range(0, hidden, 256):
            span = pl.ds(start, 256)
            value, slope = gelu_terms(up[which, :, span])
            act[which, :, span] = value.astype(BF16)
            pulled = contract_last(held[which], wd_ref[span, :])
            grad[which, :, span] = (pulled * slope).astype(BF16)
        sum_out[0:1, :] += jnp.sum(held[which].astype(F32), 0, keepdims=True)

    for step, place in enumerate(near_first(line)):

        def one(other, _, step=step, place=place):
            @pl.when(other == 1)
            def _():
                if step < PAIRS - 1:
                    relay.start(step + 1)
                relay.wait_over(place)

            work(place * 2 + side + other * (1 - 2 * side))

        lax.fori_loop(0, 2, one, None)

    stores = []
    for index, (src, dst) in enumerate(((held, dy_out), (act, a_out), (grad, du_out))):
        stores.append(pltpu.make_async_copy(src, dst, store_sem.at[index]))
        stores[-1].start()
    relay.finish()
    spread.finish()
    for step in range(1, QUARTERS):
        back(lax.rem(quarter + step, QUARTERS), quarter).wait_send()
        origin = lax.rem(quarter + step, QUARTERS)
        back(origin, origin).wait_recv()
    own_back.wait()
    for copy in stores:
        copy.wait()


def second(dy, w_out, w_down, up_values, attended):
    tokens, width = dy.shape
    hidden = up_values.shape[-1]
    shapes = [
        ((TEAM, tokens, width), BF16),
        ((TEAM, tokens, hidden), BF16),
        ((TEAM, tokens, hidden), BF16),
        ((2, QUARTERS * tokens, HEAD), BF16),
        ((TEAM, tokens, HEAD), BF16),
        ((8, width), F32),
    ]
    return pl.pallas_call(
        second_kernel,
        out_shape=[jax.ShapeDtypeStruct(*shape) for shape in shapes],
        in_specs=[VMEM, VMEM, VMEM, ANY, ANY],
        out_specs=[ANY] * 5 + [VMEM],
        scratch_shapes=[
            pltpu.VMEM((TEAM, tokens, width), BF16),
            pltpu.VMEM((TEAM, tokens, hidden), F32),
            pltpu.VMEM((TEAM, tokens, hidden), BF16),
            pltpu.VMEM((TEAM, tokens, hidden), BF16),
            pltpu.VMEM((TEAM, tokens, HEAD), BF16),
            DMA((2,)),
            DMA,
            DMA((3,)),
            DMA((QUARTERS,)),
            DMA((QUARTERS,)),
        ]
        + spread_sems(1)
        + RELAY_SEMS,
        compiler_params=pltpu.CompilerParams(
            collective_id=1, has_side_effects=True, vmem_limit_bytes=LIMIT
        ),
        name="gather_dy",
    )(dy, w_out, w_down, up_values, attended)


def probabilities(start, block, q_ref, k_ref, col_ref, row_ref):
    rows, keys = pl.ds(start, block), pl.ds(0, start + block)
    scores = contract_last(q_ref[rows, :], k_ref[keys, :]) * HEAD ** (-0.5)
    shape = scores.shape
    query_pos = start + lax.broadcasted_iota(jnp.int32, shape, 0)
    key_pos = lax.broadcasted_iota(jnp.int32, shape, 1)
    allowed = (query_pos >= key_pos) & (col_ref[rows, :] == row_ref[:, keys])
    scores = jnp.where(allowed, scores, MASKED)
    expanded = jnp.exp(scores - jnp.max(scores, -1, keepdims=True))
    return expanded / jnp.sum(expanded, -1, keepdims=True)


def forward_kernel(block, qkv_ref, col_ref, row_ref, o_ref):
    q_ref, k_ref, v_ref = (qkv_ref.at[kind] for kind in range(3))
    for start in range(0, o_ref.shape[0], block):
        probs = probabilities(start, block, q_ref, k_ref, col_ref, row_ref)
        value_block = v_ref[pl.ds(0, start + block), :]
        o_ref[pl.ds(start, block), :] = dot(probs.astype(BF16), value_block).astype(BF16)


def backward_kernel(
    block, qkv_ref, do_ref, col_ref, row_ref, cos_ref, above_ref, below_ref, d_ref, dk_sum, dv_sum
):
    scale = HEAD ** (-0.5)
    q_ref, k_ref, v_ref = (qkv_ref.at[kind] for kind in range(3))
    length = q_ref.shape[0]

    def put(kind, rows, grads):
        low = unrotate_low(
            grads[:, :128], cos_ref[rows, :], above_ref[rows, :], below_ref[rows, :]
        )
        d_ref[kind, rows, pl.ds(0, 128)] = low.astype(BF16)
        d_ref[kind, rows, pl.ds(128, HEAD - 128)] = grads[:, 128:].astype(BF16)

    dk_sum[...] = jnp.zeros_like(dk_sum)
    dv_sum[...] = jnp.zeros_like(dv_sum)
    for start in range(0, length, block):
        rows, keys = pl.ds(start, block), pl.ds(0, start + block)
        probs = probabilities(start, block, q_ref, k_ref, col_ref, row_ref)
        grads = do_ref[rows, :]
        grad_probs = contract_last(grads, v_ref[keys, :])
        row_dot = jnp.sum(probs * grad_probs, -1, keepdims=True)
        grad_scores = (probs * (grad_probs - row_dot)).astype(BF16)
        put(0, rows, dot(grad_scores, k_ref[keys, :]) * scale)
        dk_sum[keys, :] += contract_first(grad_scores, q_ref[rows, :])
        dv_sum[keys, :] += contract_first(probs.astype(BF16), grads)
    put(1, pl.ds(0, length), dk_sum[...] * scale)
    d_ref[2] = dv_sum[...].astype(BF16)


def attention_specs(seqs, length):
    three = pl.BlockSpec((None, 3, length, HEAD), lambda s: (s, 0, 0, 0))
    one = pl.BlockSpec((None, length, HEAD), lambda s: (s, 0, 0))
    masks = [
        pl.BlockSpec((None, length, 1), lambda s: (s, 0, 0)),
        pl.BlockSpec((None, 1, length), lambda s: (s, 0, 0)),
    ]
    return three, one, masks


def attend(qkv, column, row):
    seqs, _, length, head = qkv.shape
    three, one, masks = attention_specs(seqs, length)
    return pl.pallas_call(
        partial(forward_kernel, min(256, length)),
        grid=(seqs,),
        in_specs=[three] + masks,
        out_specs=one,
        out_shape=jax.ShapeDtypeStruct((seqs, length, head), BF16),
        compiler_params=pltpu.CompilerParams(vmem_limit_bytes=48 << 20),
        name="attend",
    )(qkv, column, row)


def attend_back(qkv, grads, column, row, tables):
    seqs, _, length, head = qkv.shape
    three, one, masks = attention_specs(seqs, length)
    table = pl.BlockSpec((length, 128), lambda s: (0, 0))
    return pl.pallas_call(
        partial(backward_kernel, min(256, length)),
        grid=(seqs,),
        in_specs=[three, one] + masks + [table] * 3,
        out_specs=three,
        out_shape=jax.ShapeDtypeStruct(qkv.shape, BF16),
        scratch_shapes=[pltpu.VMEM((length, head), F32)] * 2,
        compiler_params=pltpu.CompilerParams(vmem_limit_bytes=48 << 20),
        name="attend_back",
    )(qkv, grads, column, row, *tables)


class Reduce:
    def __init__(self, own, side_out, side_in, line_out, line_in, sems):
        self.own, self.side_out, self.side_in = own, side_out, side_in
        self.line_out, self.line_in, self.sems = line_out, line_in, sems
        self.base, self.line, self.side, self.quarter = spot()
        self.order = near_first(self.line)

    def over(self, step):
        side_send, side_recv = self.sems[:2]
        place = self.base + self.line * 2 + 1 - self.side
        return send(
            self.side_out.at[step], self.side_in.at[step], side_send.at[step], side_recv.at[step],
            place, self.quarter,
        )

    def along(self, step, target, way):
        line_send, line_recv = self.sems[2:]
        move = 1 if way == RIGHT else -1
        slot = target if way == RIGHT else jnp.where(target == self.line - 1, PAIRS, target)
        place = self.base + (self.line + move) * 2 + self.side
        return send(
            self.line_out.at[step], self.line_in.at[slot], line_send.at[step], line_recv.at[slot],
            place, self.quarter,
        )

    def arrive(self, slot):
        line_send, line_recv = self.sems[2:]
        return send(
            self.line_out.at[0], self.line_in.at[slot], line_send.at[0], line_recv.at[slot],
            self.base + self.line * 2 + 1 - self.side, self.quarter,
        )

    def begin(self, step):
        self.over(step).start()

    def advance(self, step):
        target = self.order[step]
        self.over(step).wait_recv()

        def forward(way, upstream):
            @pl.when(upstream)
            def _():
                self.arrive(target).wait_recv()

            strip = 64

            def add(index, _):
                chunk = pl.ds(pl.multiple_of(index * strip, strip), strip)
                total = self.own[step, chunk, :] + self.side_in[step, chunk, :].astype(F32)
                held = self.line_in[target, chunk, :].astype(F32)
                total = jnp.where(upstream, total + held, total)
                self.line_out[step, chunk, :] = total.astype(BF16)

            lax.fori_loop(0, self.own.shape[1] // strip, add, None)
            self.along(step, target, way).start()

        @pl.when(target > self.line)
        def _():
            forward(RIGHT, self.line > 0)

        @pl.when(target < self.line)
        def _():
            forward(LEFT, self.line < PAIRS - 1)

    def last(self):
        self.over(0).wait_recv()
        pl.when(self.line > 0)(lambda: self.arrive(self.line).wait_recv())
        pl.when(self.line < PAIRS - 1)(lambda: self.arrive(PAIRS).wait_recv())

    def total(self, chunk):
        total = self.own[0, chunk, :] + self.side_in[0, chunk, :].astype(F32)
        left = self.line_in[self.line, chunk, :].astype(F32)
        right = self.line_in[PAIRS, chunk, :].astype(F32)
        total = jnp.where(self.line > 0, total + left, total)
        return jnp.where(self.line < PAIRS - 1, total + right, total)

    def finish(self):
        for step in range(PAIRS):
            self.over(step).wait_send()
        for step in range(1, PAIRS):
            target = self.order[step]
            pl.when(target > self.line)(lambda: self.along(step, target, RIGHT).wait_send())
            pl.when(target < self.line)(lambda: self.along(step, target, LEFT).wait_send())


def reduce_scratch(tokens, width):
    return [
        pltpu.VMEM((PAIRS, tokens, width), F32),
        pltpu.VMEM((PAIRS, tokens, width), BF16),
        pltpu.VMEM((PAIRS, tokens, width), BF16),
        pltpu.VMEM((PAIRS, tokens, width), BF16),
        pltpu.VMEM((PAIRS + 1, tokens, width), BF16),
        DMA((PAIRS,)),
        DMA((PAIRS,)),
        DMA((PAIRS,)),
        DMA((PAIRS + 1,)),
    ]


def third_kernel(
    x_ref, o_ref, a_ref, wo_ref, wd_ref, bias_ref, d_ref,
    result_ref, back_out,
    own_sem, back_send, back_recv, own, side_out, side_in, line_out, line_in, *sems,
):
    base, line, side, quarter = spot()
    rank = line * 2 + side
    tokens, width = x_ref.shape
    reduce = Reduce(own, side_out, side_in, line_out, line_in, sems)
    greet_line(base, line, side, quarter)

    def pieces(to, origin, kind):
        return (
            d_ref.at[:, kind, pl.ds(to * tokens, tokens), :],
            back_out.at[pl.ds(2 * origin, 2), :, pl.ds(kind * HEAD, HEAD)],
        )

    def back(to, origin, kind):
        src, dst = pieces(to, origin, kind)
        return send(
            src, dst, back_send.at[to, kind], back_recv.at[origin, kind], base + rank, to
        )

    own_back = [
        pltpu.make_async_copy(*pieces(quarter, quarter, kind), own_sem.at[kind])
        for kind in range(3)
    ]

    def make(which, put):
        for start in range(0, width, 512):
            span = pl.ds(start, 512)
            put(
                span,
                dot(o_ref[which], wo_ref[:, span]) + dot(a_ref[which], wd_ref[:, span]),
            )

    for step in reversed(range(PAIRS)):
        place = reduce.order[step]

        def put_out(span, value, step=step):
            side_out[step, :, span] = value.astype(BF16)

        def put_own(span, value, step=step):
            own[step, :, span] = value

        make(place * 2 + 1 - side, put_out)
        reduce.begin(step)
        make(place * 2 + side, put_own)
        if step == PAIRS - 1:
            for kind in range(3):
                own_back[kind].start()
                for hop in range(1, QUARTERS):
                    back(lax.rem(quarter + hop, QUARTERS), quarter, kind).start()

    for step in reversed(range(1, PAIRS)):
        reduce.advance(step)
    reduce.last()
    strip = 64

    def close(index, _):
        chunk = pl.ds(pl.multiple_of(index * strip, strip), strip)
        total = reduce.total(chunk) + bias_ref[0:1, :]
        result_ref[chunk, :] = (x_ref[chunk, :].astype(F32) + total).astype(BF16)

    lax.fori_loop(0, tokens // strip, close, None)
    reduce.finish()
    for kind in range(3):
        own_back[kind].wait()
        for hop in range(1, QUARTERS):
            origin = lax.rem(quarter + hop, QUARTERS)
            back(origin, quarter, kind).wait_send()
            back(origin, origin, kind).wait_recv()


def third(x, attended, activated, w_out, w_down, bias, grads):
    tokens, width = x.shape
    return pl.pallas_call(
        third_kernel,
        out_shape=[
            jax.ShapeDtypeStruct((tokens, width), BF16),
            jax.ShapeDtypeStruct((TEAM, tokens, 3 * HEAD), BF16),
        ],
        in_specs=[VMEM] * 6 + [ANY],
        out_specs=[VMEM, ANY],
        scratch_shapes=[DMA((3,)), DMA((QUARTERS, 3)), DMA((QUARTERS, 3))]
        + reduce_scratch(tokens, width),
        compiler_params=pltpu.CompilerParams(
            collective_id=2, has_side_effects=True, vmem_limit_bytes=LIMIT
        ),
        name="scatter_result",
    )(x, attended, activated, w_out, w_down, bias, grads)


def fourth_kernel(
    x_ref, dy_ref, xs_ref, dqkv_ref, du_ref, w_ref, vec_ref,
    grad_ref, sums_ref,
    weight, xs, load_sem, own, side_out, side_in, line_out, line_in, *sems,
):
    base, line, side, quarter = spot()
    tokens, width = x_ref.shape
    reduce = Reduce(own, side_out, side_in, line_out, line_in, sems)
    loads = [
        pltpu.make_async_copy(w_ref, weight, load_sem.at[0]),
        pltpu.make_async_copy(xs_ref, xs, load_sem.at[1]),
    ]
    for copy in loads:
        copy.start()
    greet_line(base, line, side, quarter)
    sums_ref[...] = jnp.zeros_like(sums_ref)
    for copy in loads:
        copy.wait()

    def make(which, put):
        rows = xs[which].astype(F32)
        average = jnp.mean(rows, -1, keepdims=True)
        variance = jnp.mean(jnp.square(rows - average), -1, keepdims=True)
        inverse = lax.rsqrt(variance + EPSILON)
        for start in range(0, width, 512):
            span = pl.ds(start, 512)
            attn = contract_last(dqkv_ref[which], weight[span, : 3 * HEAD])
            mlp = contract_last(du_ref[which], weight[span, 3 * HEAD :])
            unit = (xs[which, :, span].astype(F32) - average) * inverse
            sums_ref[0:1, span] += jnp.sum(attn * unit, 0, keepdims=True)
            sums_ref[1:2, span] += jnp.sum(mlp * unit, 0, keepdims=True)
            sums_ref[2:3, span] += jnp.sum(attn, 0, keepdims=True)
            sums_ref[3:4, span] += jnp.sum(mlp, 0, keepdims=True)
            put(span, attn * vec_ref[0:1, span] + mlp * vec_ref[1:2, span])

    for step in reversed(range(PAIRS)):
        place = reduce.order[step]

        def put_out(span, value, step=step):
            side_out[step, :, span] = value.astype(BF16)

        def put_own(span, value, step=step):
            own[step, :, span] = value

        make(place * 2 + 1 - side, put_out)
        reduce.begin(step)
        make(place * 2 + side, put_own)

    for step in reversed(range(1, PAIRS)):
        reduce.advance(step)
    reduce.last()
    strip = 64

    def close(index, _):
        chunk = pl.ds(pl.multiple_of(index * strip, strip), strip)
        total = reduce.total(chunk)
        unit, inverse = normalize(x_ref[chunk, :].astype(F32))
        pulled = (
            total
            - jnp.mean(total, -1, keepdims=True)
            - unit * jnp.mean(total * unit, -1, keepdims=True)
        )
        grad_ref[chunk, :] = (dy_ref[chunk, :].astype(F32) + inverse * pulled).astype(BF16)

    lax.fori_loop(0, tokens // strip, close, None)
    reduce.finish()


def fourth(x, dy, everyone, grad_qkv, grad_up, weight, vectors):
    tokens, width = x.shape
    return pl.pallas_call(
        fourth_kernel,
        out_shape=[
            jax.ShapeDtypeStruct((tokens, width), BF16),
            jax.ShapeDtypeStruct((8, width), F32),
        ],
        in_specs=[VMEM, VMEM, ANY, VMEM, VMEM, ANY, VMEM],
        out_specs=[VMEM, VMEM],
        scratch_shapes=[
            pltpu.VMEM(weight.shape, BF16),
            pltpu.VMEM(everyone.shape, BF16),
            DMA((2,)),
        ]
        + reduce_scratch(tokens, width),
        compiler_params=pltpu.CompilerParams(
            collective_id=3, has_side_effects=True, vmem_limit_bytes=LIMIT
        ),
        name="scatter_grad",
    )(x, dy, everyone, grad_qkv, grad_up, weight, vectors)


def on_device(
    dp,
    ctx,
    inputs,
    segments,
    ln_gain,
    ln_bias,
    qkv_weight,
    qkv_bias,
    out_weight,
    out_bias,
    up_weight,
    up_bias,
    down_weight,
    down_bias,
    cotangent,
):
    assert dp % TEAM == 0 and ctx == QUARTERS
    teams = dp // TEAM
    together = None if teams == 1 else [[g * TEAM + i for i in range(TEAM)] for g in range(teams)]
    across = None if teams == 1 else [[g * TEAM + i for g in range(teams)] for i in range(TEAM)]
    place = lax.axis_index("dp")
    rank = place % TEAM
    _, tokens, width = inputs.shape
    hidden = up_weight.shape[1] // TEAM
    shard = width // dp

    def team_order(values):
        if teams == 1:
            return values
        lead = values.shape[:-1]
        return values.reshape(*lead, teams, TEAM, shard).swapaxes(-3, -2).reshape(*lead, width)

    def plain_order(values):
        if teams == 1:
            return values
        lead = values.shape[:-1]
        return values.reshape(*lead, TEAM, teams, shard).swapaxes(-3, -2).reshape(*lead, width)

    if teams == 1:
        w_qkv, w_up, w_out, w_down = qkv_weight, up_weight, out_weight, down_weight
        gain, shift, b_qkv, b_up = ln_gain, ln_bias, qkv_bias, up_bias
        b_rows = [out_bias, down_bias]
    else:
        line_up = partial(lax.all_gather, axis_name="dp", axis_index_groups=across, tiled=True)
        whole = partial(lax.all_gather, axis_name="dp", axis=0, tiled=True)

        def cut(values):
            size = values.shape[0] // TEAM
            return lax.dynamic_slice_in_dim(values, rank * size, size, 0)

        w_qkv, w_up = line_up(qkv_weight, axis=0), line_up(up_weight, axis=0)
        gain, shift = line_up(ln_gain, axis=1), line_up(ln_bias, axis=1)
        w_out, w_down = cut(whole(out_weight)), cut(whole(down_weight))
        b_qkv, b_up = cut(whole(qkv_bias)), cut(whole(up_bias))
        b_rows = [cut(whole(out_bias)), cut(whole(down_bias))]
    rows = w_qkv.shape[0]
    packet = jnp.concatenate(
        [
            gain.astype(F32),
            shift.astype(F32),
            jnp.stack(b_rows).astype(F32),
            jnp.zeros((2, rows), F32),
            b_qkv.astype(F32).reshape(3, rows),
            jnp.zeros((5, rows), F32),
            jnp.broadcast_to(segments.astype(F32), (8, tokens)),
        ]
    )
    mine = inputs.reshape(tokens, width)
    grad_mine = cotangent.reshape(tokens, width)
    mine_team = team_order(mine)
    positions = jnp.arange(ctx * tokens, dtype=jnp.int32)
    tables = rotary_tables(positions.astype(F32))
    own_tables = [
        lax.dynamic_slice_in_dim(table, lax.axis_index("ctx") * tokens, tokens, 0)
        for table in tables
    ]
    everyone, attn_input, mlp_input, up_values, weight, qkv, marks, vectors = first(
        mine_team, w_qkv, w_up, packet, b_up.astype(F32).reshape(1, hidden), own_tables
    )
    marks = marks[:, :, 0, :].reshape(2, ctx * tokens)
    column, row = marks[:, :, None], marks[:, None, :]
    attended = attend(qkv, column, row)
    grad_rows, activated, grad_up, grad_attended, attended, dy_sum = second(
        grad_mine, w_out, w_down, up_values, attended
    )
    grads = attend_back(qkv, grad_attended, column, row, tables)
    branch_bias = (vectors[:, 4] + vectors[:, 5]).reshape(1, width)
    result, grad_qkv = third(
        mine, attended, activated, w_out, w_down, branch_bias, grads
    )
    gains = vectors[:, :2].transpose(1, 0, 2).reshape(2, width)
    grad_inputs, sums = fourth(
        mine_team, team_order(grad_mine), everyone, grad_qkv, grad_up, weight, gains
    )
    grad_inputs = plain_order(grad_inputs)

    flat = (TEAM * tokens, -1)
    attn_input, mlp_input = attn_input.reshape(flat), mlp_input.reshape(flat)
    grad_rows, grad_qkv, grad_up = (
        values.reshape(flat) for values in (grad_rows, grad_qkv, grad_up)
    )
    attended, activated = attended.reshape(flat), activated.reshape(flat)
    qkv_bias_sum = lax.dynamic_update_slice_in_dim(
        jnp.zeros((3, HEADS, HEAD), F32),
        jnp.sum(grad_qkv.astype(F32), 0).reshape(3, 1, HEAD), rank, 1,
    )
    up_bias_sum = lax.dynamic_update_slice_in_dim(
        jnp.zeros((TEAM, hidden), F32), jnp.sum(grad_up.astype(F32), 0)[None], rank, 0
    )
    vector = jnp.concatenate(
        [
            plain_order(sums[:4]).reshape(-1),
            qkv_bias_sum.reshape(-1),
            dy_sum[0] * jnp.where(rank == 0, 1.0, 0.0),
            up_bias_sum.reshape(-1),
        ]
    )
    vector = lax.psum(vector, ("dp", "ctx"))

    def own(start, size):
        return lax.dynamic_slice_in_dim(vector, start + place * (size // dp), size // dp, 0)

    grad_gain = jnp.stack([own(0, width), own(width, width)])
    grad_shift = jnp.stack([own(2 * width, width), own(3 * width, width)])
    grad_qkv_b = own(4 * width, 3 * width)
    grad_out_b = own(7 * width, width)
    grad_up_b = own(8 * width, TEAM * hidden)

    term_out = contract_first(attended, grad_rows).astype(BF16)
    term_down = contract_first(activated, grad_rows).astype(BF16)
    term_columns = jnp.concatenate(
        [
            contract_first(attn_input, grad_qkv).astype(BF16),
            contract_first(mlp_input, grad_up).astype(BF16),
        ],
        -1,
    )
    span = term_columns.shape[-1]
    if teams > 1:
        def scatter_rows(term):
            size = term.shape[0]
            full = jnp.zeros((TEAM, size, width), BF16)
            full = lax.dynamic_update_slice_in_dim(full, term[None], rank, 0)
            return lax.psum_scatter(
                full.reshape(TEAM * size, width), "dp", scatter_dimension=0, tiled=True
            )

        term_out, term_down = scatter_rows(term_out), scatter_rows(term_down)
        term_columns = term_columns.reshape(TEAM, teams, shard, span).swapaxes(0, 1)
        term_columns = lax.psum_scatter(
            term_columns.reshape(width, span), "dp", scatter_dimension=0,
            axis_index_groups=across, tiled=True,
        )
    grad_out_w = lax.psum(term_out, "ctx").astype(F32)
    grad_down_w = lax.psum(term_down, "ctx").astype(F32)
    term_columns = term_columns.reshape(TEAM, shard, span)
    term_columns = lax.psum_scatter(term_columns, "ctx", scatter_dimension=1, tiled=True)
    term_columns = lax.all_to_all(
        term_columns, "dp", 0, 0, axis_index_groups=together, tiled=True
    )
    term_columns = lax.all_gather(term_columns, "ctx", axis=1, tiled=True)
    grad_qkv_w = (
        term_columns[:, :, : 3 * HEAD].reshape(TEAM, shard, 3, HEAD).transpose(1, 2, 0, 3)
        .reshape(shard, 3 * width).astype(F32)
    )
    grad_up_w = (
        term_columns[:, :, 3 * HEAD :].transpose(1, 0, 2).reshape(shard, TEAM * hidden).astype(F32)
    )
    return (
        result.reshape(inputs.shape),
        grad_inputs.reshape(inputs.shape),
        grad_gain,
        grad_shift,
        grad_qkv_w,
        grad_qkv_b,
        grad_out_w,
        grad_out_b,
        grad_up_w,
        grad_up_b,
        grad_down_w,
        grad_out_b,
    )


def solution(mesh):
    placed = (
        P("dp", "ctx", None),
        P("dp", "ctx"),
        P(None, "dp"),
        P(None, "dp"),
        P("dp", None),
        P("dp"),
        P("dp", None),
        P("dp"),
        P("dp", None),
        P("dp"),
        P("dp", None),
        P("dp"),
        P("dp", "ctx", None),
    )
    return jax.shard_map(
        partial(on_device, mesh.shape["dp"], mesh.shape["ctx"]),
        mesh=mesh,
        in_specs=placed,
        out_specs=(
            P("dp", "ctx", None),
            P("dp", "ctx", None),
            P(None, "dp"),
            P(None, "dp"),
            P("dp", None),
            P("dp"),
            P("dp", None),
            P("dp"),
            P("dp", None),
            P("dp"),
            P("dp", None),
            P("dp"),
        ),
        check_vma=False,
    )
```

time: 1310 us -> 927 us (0.71)
  Pallas kernels: 10.5 us -> 502 us
  waiting for transfers between devices: 713 us -> 256 us
  blocking collectives: 186 us -> 0 us
  matrix products: 168 us -> 45.8 us
  local copies, waits for them, and re-layouts: 124 us -> 65 us
  other arithmetic: 68.8 us -> 31.1 us
    pallas_call x1 -> x6, Pallas kernels: 10.5 us -> 502 us  [the longest x1 153 us: first(): pl.pallas_call(first_kernel, out_shape=[jax.ShapeDtypeStruct(*shape) for...]
    reduce_scatter x2 -> x0, waiting for transfers between devices: 293 us -> none  [the longest x1 150 us: on_device(): lax.psum_scatter(branches, 'dp', scatter_dimension=0, axis_index_groups=t...]
    all_gather x3 -> x0, waiting for transfers between devices: 224 us -> none  [the longest x1 117 us: on_device(): everyone = gather(inputs, axis=0).reshape(team * tokens, width)]
    dot_general x8 -> x0, matrix products: 126 us -> none  [the longest x4 74.6 us: contract_last(): lax.dot_general(left, right, (((1,), (1,)), ((), ())), preferred_element_...]
    all_gather x3 -> x0, blocking collectives: 93.3 us -> none  [the longest x1 48.2 us: on_device(): segments_all = lax.all_gather(segments, 'ctx', axis=1, tiled=True)]
    all_to_all x2 -> x0, blocking collectives: 93 us -> none  [the longest x1 48.5 us: on_device(): lax.all_to_all(term_columns, 'dp', 0, 0, axis_index_groups=together, tile...]
    psum x1, waiting for transfers between devices: 39.9 us -> 75.4 us  [on_device(): vector = lax.psum(vector, ('dp', 'ctx'))]
    all_to_all x2 -> x1, waiting for transfers between devices: 0.01 us -> 32.7 us  [on_device(): lax.all_to_all(term_columns, 'dp', 0, 0, axis_index_groups=together, tile...]
  transfers between devices with their start and end apart: 11 -> 5, of which waited for: 8 -> 4; matrix products, arithmetic and copies ran while one was open for 19% -> 5% of each run, Pallas kernels for 0% -> 12%
where the time goes in v2:
time: 927 us; the launch traced here: 922 us
  Pallas kernels  502 us (54%)
  waiting for transfers between devices  256 us (28%)
  local copies, waits for them, and re-layouts  65 us (7%)
  matrix products  45.8 us (5%)
  other arithmetic  31.1 us (3%)
  between operations  16.2 us (2%)
    pallas_call x1, Pallas kernels, first(): pl.pallas_call(first_kernel, out_shape=[jax.ShapeDtypeStruct(*shape) for...  153 us
    pallas_call x1, Pallas kernels, third(): pl.pallas_call(third_kernel, out_shape=[jax.ShapeDtypeStruct((tokens, wid...  116 us
    pallas_call x1, Pallas kernels, second(): pl.pallas_call(second_kernel, out_shape=[jax.ShapeDtypeStruct(*shape) for...  109 us
    pallas_call x1, Pallas kernels, fourth(): pl.pallas_call(fourth_kernel, out_shape=[jax.ShapeDtypeStruct((tokens, wi...  108 us
    psum x1, waiting for transfers between devices, on_device(): grad_out_w = lax.psum(term_out, 'ctx').astype(F32)  102 us
    psum x1, waiting for transfers between devices, on_device(): vector = lax.psum(vector, ('dp', 'ctx'))  75.4 us
    dot_general x4, matrix products, contract_first(): lax.dot_general(left, right, (((0,), (0,)), ((), ())), preferred_element_...  45.8 us
    all_gather x1, waiting for transfers between devices, on_device(): term_columns = lax.all_gather(term_columns, 'ctx', axis=1, tiled=True)  45.7 us
  transfers between devices with their start and end apart: 5, of which 4 were waited for; matrix products, arithmetic and copies ran while one was open for 5% of the time, Pallas kernels for 12%

profile of v2, /device:TPU:19, one launch (start us, length us, event | category | flops | bytes accessed | tf_op | source)
XLA Modules:
  0.0 922.2 jit_solution(2762559966672789352)
XLA Ops:
  8.1 0.1 pad.15.clone
  8.2 0.1 pad.18.clone
  8.3 0.7 convert_element_type.90
  9.0 0.7 stack.27
  9.6 0.7 stack.28
  10.3 0.7 reshape.129
  11.0 1.3 reshape.130
  12.2 1.9 multiply_sine_fusion
  14.2 0.5 maximum_maximum_fusion.2
  14.7 0.7 constant_dynamic-slice_fusion.below_ref
  15.3 0.7 constant_dynamic-slice_fusion.1.above_ref
  16.0 0.7 constant_dynamic-slice_fusion.2.cos_ref
  16.7 1.8 concatenate.18.vec_ref
  18.6 153.3 %gather_x.1 = (bf16[8,256,2048]{2,1,0:T(8,128)(2,1)}, bf16[8,256,2048]{2,1,0:T(8,128)(2,1)}, bf16[8,256,2048]{2,1,0:T(8,128)(2,1)}, f32[8,256,1024]{2,1,0:T(8,12...) custom-call(bf16[256,2048]{1,0:T(8,128)(2,1)} %bitcast.64, ...), custom_call_target="tpu_custom_call" | custom-call | tf_op jit(solution)/shard_map/gather_x/pallas_call | solution.py:502
  171.8 1.5 slice_add_fusion
  173.4 0.9 fusion.3
  174.2 0.9 broadcast_in_dim_reshape_squeeze.8.col_ref
  175.1 1.9 copy-done
  177.0 4.5 attend.1.o_ref
  181.6 1.0 copy-done.1
  182.5 109.3 %gather_dy.1 = (bf16[8,256,2048]{2,1,0:T(8,128)(2,1)}, bf16[8,256,1024]{2,1,0:T(8,128)(2,1)}, bf16[8,256,1024]{2,1,0:T(8,128)(2,1)}, bf16[2,1024,256]{2,1,0:T(8,...) custom-call(bf16[256,2048]{1,0:T(8,128)(2,1)} %bitcast.69, bf16[256,2048]{1,0:T(8,128)(2,1)} %wo_ref.3, ...), custom_call_target="tpu_custom_call" | custom-call | tf_op jit(solution)/shard_map/gather_dy/pallas_call | solution.py:633
  291.9 1.2 copy-done.2
  293.1 10.7 %attend_back.1.d_ref = bf16[2,3,1024,256]{3,2,1,0:T(8,128)(2,1)} custom-call(bf16[2,3,1024,256]{3,2,1,0:T(8,128)(2,1)} %get-tuple-element.31.qkv_ref, bf16[2,1024,256]{2,1,0:T(8,128)(2,1)S(1)} %copy-done.2, f32[2,1024,1]{2,1,0:T(8,128)S(1)} %broadcast_in_dim_reshape_squeeze.8.col_ref, f32[2,1,1024]{2,1,0:T(1,128)S(1)} %bitcast.58, ...), custom_call_target="tpu_custom_call" | custom-call | tf_op jit(solution)/shard_map/attend_back/pallas_call | solution.py:737
  303.8 12.8 %bitcast_convert_fusion.1 = bf16[2048,1024]{0,1:T(8,128)(2,1)} fusion(bf16[8,256,2048]{2,1,0:T(8,128)(2,1)} %get-tuple-element.46, bf16[8,256,1024]{2,1,0:T(8,128)(2,1)S(1)} %copy-done.3), kind=kOutput, calls=%fused_computation.1 | convolution fusion | flops 8592031744 | bytes 16777216 | tf_op jit(solution)/shard_map/dot_general | solution.py:34
  316.7 116.0 %scatter_result.1 = (bf16[256,2048]{1,0:T(8,128)(2,1)}, bf16[8,256,768]{2,1,0:T(8,128)(2,1)}) custom-call(bf16[256,2048]{1,0:T(8,128)(2,1)} %bitcast.65, bf16[8,256,256]{2,1,0:T(8,128)(2,1)} %get-tuple-element.33.o_ref, bf16[8,256,1024]{2,1,0:T(8,128)(2,1)} %get-tuple-element.34.a_ref, bf16[256,2048]{1,0:T(8,128)(2,1)} %wo_ref.3, bf16[1024,2048]{1,0:T(8,128)(2,1)} %wd_ref.3, ...), custom_call_target="tpu_custom_call" | custom-call | tf_op jit(solution)/shard_map/scatter_result/pallas_call | solution.py:924
  432.7 12.2 %bitcast_convert_fusion.2 = bf16[2048,768]{0,1:T(8,128)(2,1)} fusion(bf16[8,256,2048]{2,1,0:T(8,128)(2,1)} %get-tuple-element.45, bf16[8,256,768]{2,1,0:T(8,128)(2,1)} %get-tuple-element.39.dqkv_ref), kind=kOutput, calls=%fused_computation.4 | convolution fusion | flops 6444023808 | bytes 14680064 | tf_op jit(solution)/shard_map/dot_general | solution.py:34
  444.9 6.0 pad_maximum_fusion
  450.9 9.3 %copy.55 = bf16[224,8,8,256]{3,2,1,0:T(8,128)(2,1)} copy(bf16[224,8,8,256]{3,1,2,0:T(8,128)(2,1)} %bitcast.60) | data formatting | bytes 14680064
  460.2 11.6 %copy.43 = bf16[8,256,1792]{2,0,1:T(8,128)(2,1)} copy(bf16[8,256,1792]{1,0,2:T(8,128)(2,1)} %bitcast.61) | data formatting | bytes 14680064 | tf_op jit(solution)/shard_map/reshape | solution.py:1188
  471.9 0.0 all-reduce.4.cloned.1.call-start
  472.0 1.6 slice.27
  473.6 2.9 convert_reduce_fusion
  476.4 0.1 dynamic_update_slice.7
  476.6 0.5 convert_reduce_fusion.1
  477.1 0.1 dynamic_update_slice.6
  477.2 108.4 %scatter_grad.1 = (bf16[256,2048]{1,0:T(8,128)(2,1)}, f32[8,2048]{1,0:T(8,128)}) custom-call(bf16[256,2048]{1,0:T(8,128)(2,1)} %bitcast.66, bf16[256,2048]{1,0:T(8,128)(2,1)} %bitcast.70, bf16[8,256,2048]{2,1,0:T(8,128)(2,1)} %get-tuple-element.38.xs_ref, bf16[8,256,768]{2,1,0:T(8,128)(2,1)} %get-tuple-element.39.dqkv_ref, ...), custom_call_target="tpu_custom_call" | custom-call | tf_op jit(solution)/shard_map/scatter_grad/pallas_call | solution.py:1011
  585.6 0.8 slice_bitcast_fusion
  586.5 0.8 slice_multiply_fusion
  587.3 0.6 pad_maximum_fusion.1
  588.0 14.0 %bitcast_convert_fusion = bf16[1024,2048]{1,0:T(8,128)(2,1)} fusion(bf16[8,256,1024]{2,1,0:T(8,128)(2,1)} %get-tuple-element.34.a_ref, bf16[8,256,2048]{2,1,0:T(8,128)(2,1)} %get-tuple-element.47), kind=kOutput, calls=%fused_computation | convolution fusion | flops 8592031744 | bytes 16777216 | tf_op jit(solution)/shard_map/dot_general | solution.py:34
  602.0 3.1 copy.44
  605.2 5.3 all-to-all-start
  610.4 6.7 fusion
  617.2 0.2 all-gather.2.cloned.1.call-start
  617.4 32.7 %all-to-all-done = bf16[8,64,1792]{2,1,0:T(8,128)(2,1)S(1)} async-done(((bf16[8,64,1792]{2,1,0:T(8,128)(2,1)}), bf16[8,64,1792]{2,1,0:T(8,128)(2,1)S(1)}, u32[]{:S(2)}, u32[]{:S(2)}) %all-to-all-start) | async-done | bytes 1835040 | tf_op jit(solution)/shard_map/all_to_all | solution.py:1190
  650.2 2.2 copy.45
  652.4 75.4 %all-reduce.4.cloned.1.call-done = f32[24576]{0:T(1024)} async-done(((f32[24576]{0:T(1024)}), f32[24576]{0:T(1024)}) %all-reduce.4.cloned.1.call-update) | async-done | bytes 98320 | tf_op jit(solution)/shard_map/psum | solution.py:1150
  727.8 0.8 fusion.2
  728.6 1.4 dynamic_slice.37
  730.0 1.3 dynamic_slice.39
  731.3 0.6 pad_maximum_fusion.3
  731.9 0.6 pad_maximum_fusion.2
  732.4 102.4 %all-reduce.6.cloned.1.call-done = (bf16[256,2048]{1,0:T(8,128)(2,1)}, bf16[1024,2048]{1,0:T(8,128)(2,1)}) async-done(((bf16[256,2048]{1,0:T(8,128)(2,1)}, bf16[1024,2048]{1,0:T(8,128)(2,1)}), (bf16[256,2048]{1,0:T(8,128)(2,1)}, bf16[1024,2048]{1,0:T(8,128)(2,1)})) %all-reduce.6.cloned.1.call-update) | async-done | bytes 5242896 | tf_op jit(solution)/shard_map/psum | solution.py:1186
  834.8 2.8 convert_element_type.102
  837.6 6.7 convert_element_type.107
  844.3 45.7 %all-gather.2.cloned.1.call-done = bf16[8,256,1792]{2,0,1:T(8,128)(2,1)} async-done(((bf16[8,64,1792]{2,0,1:T(8,128)(2,1)}), bf16[8,256,1792]{2,0,1:T(8,128)(2,1)}) %all-gather.2.cloned.1.call-update) | async-done | bytes 7340048 | tf_op jit(solution)/shard_map/all_gather | solution.py:1193
  890.0 3.2 slice_convert_fusion
  893.2 11.0 %copy.57 = f32[32,8,8,1024]{3,1,2,0:T(8,128)} copy(f32[32,8,8,1024]{3,2,1,0:T(8,128)S(1)} %bitcast.59) | data formatting | bytes 16777216
  904.2 1.9 slice-done
  906.1 0.5 convert.7
  906.6 5.3 copy.56
  911.9 0.6 copy.68
  912.5 1.0 copy.69
  913.5 1.0 copy.70
  (44 shorter events, 0.3 us)
Async XLA Ops:
  8.0 8.7 copy-start.11
  8.0 8.7 copy-start.10
  8.0 594.0 %reduce-scatter.2.cloned.1.call-start = ((), (), s32[]{:S(2)}) async-start(), calls=%async_computation.3 | async-start | bytes 9175040 | tf_op jit(solution)/shard_map/reduce_scatter | solution.py:1189
  175.1 1.9 copy-start
  181.6 1.0 copy-start.1
  291.9 1.2 copy-start.2
  293.1 10.7 %copy-start.3 = (bf16[8,256,1024]{2,1,0:T(8,128)(2,1)S(1)}, bf16[8,256,1024]{2,1,0:T(8,128)(2,1)}, u32[]{:S(2)}) copy-start(bf16[8,256,1024]{2,1,0:T(8,128)(2,1)} %get-tuple-element.40.du_ref) | copy-start | bytes 12582916
  432.7 12.2 %copy-start.5 = (bf16[2048,1024]{0,1:T(8,128)(2,1)S(1)}, bf16[2048,1024]{0,1:T(8,128)(2,1)}, u32[]{:S(2)}) copy-start(bf16[2048,1024]{0,1:T(8,128)(2,1)} %bitcast_convert_fusion.1) | copy-start | bytes 12582916
  471.9 4.7 copy-start.4
  471.9 255.9 %all-reduce.4.cloned.1.call-start = ((), (), s32[]{:S(2)}) async-start(), calls=%async_computation.2 | async-start | bytes 196608 | tf_op jit(solution)/shard_map/psum | solution.py:1150
  602.0 8.4 copy-start.6
  605.2 45.0 %all-to-all-start = ((bf16[8,64,1792]{2,1,0:T(8,128)(2,1)}), bf16[8,64,1792]{2,1,0:T(8,128)(2,1)S(1)}, u32[]{:S(2)}, u32[]{:S(2)}) async-start(bf16[8,64,1792]{2,1,0:T(8,128)(2,1)} %copy.44), calls=%async_computation.1 | async-start | bytes 3670016 | tf_op jit(solution)/shard_map/all_to_all | solution.py:1190
  610.4 224.4 %all-reduce.6.cloned.1.call-start = ((), (), s32[]{:S(2)}) async-start(), calls=%async_computation.5 | async-start | bytes 10485760 | tf_op jit(solution)/shard_map/psum | solution.py:1186
  617.2 272.8 %all-gather.2.cloned.1.call-start = ((), (), s32[]{:S(2)}) async-start(), calls=%async_computation.4 | async-start | bytes 9175040 | tf_op jit(solution)/shard_map/all_gather | solution.py:1193
  728.6 183.3 %copy-start.9 = (f32[256]{0:T(256)}, f32[256]{0:T(256)S(1)}, u32[]{:S(2)}) copy-start(f32[256]{0:T(256)S(1)} %get-tuple-element.106) | copy-start | bytes 3076
  904.2 1.9 slice-start
  906.6 5.9 copy-start.7
  906.6 6.9 copy-start.8
Sparse Core Ops, SparseCore 0:
  472.0 69.2 reduce-scatter.1
Sparse Core Ops, SparseCore 1:
  588.1 139.7 all-reduce.3
  730.7 104.1 all-reduce.5
  836.9 53.0 all-gather.1

commit v3 on v2

--- a/solution.py
+++ b/solution.py
@@ -747,9 +747,9 @@
 
 
 class Reduce:
-    def __init__(self, own, side_out, side_in, line_out, line_in, sems):
-        self.own, self.side_out, self.side_in = own, side_out, side_in
-        self.line_out, self.line_in, self.sems = line_out, line_in, sems
+    def __init__(self, own, side_out, side_in, line_in, sems):
+        self.own, self.side_out, self.side_in, self.line_in = own, side_out, side_in, line_in
+        self.sems = sems
         self.base, self.line, self.side, self.quarter = spot()
         self.order = near_first(self.line)
 
@@ -767,74 +767,69 @@
         slot = target if way == RIGHT else jnp.where(target == self.line - 1, PAIRS, target)
         place = self.base + (self.line + move) * 2 + self.side
         return send(
-            self.line_out.at[step], self.line_in.at[slot], line_send.at[step], line_recv.at[slot],
+            self.side_out.at[step], self.line_in.at[slot], line_send.at[step], line_recv.at[slot],
             place, self.quarter,
         )
 
     def arrive(self, slot):
         line_send, line_recv = self.sems[2:]
         return send(
-            self.line_out.at[0], self.line_in.at[slot], line_send.at[0], line_recv.at[slot],
+            self.side_out.at[0], self.line_in.at[slot], line_send.at[0], line_recv.at[slot],
             self.base + self.line * 2 + 1 - self.side, self.quarter,
         )
 
     def begin(self, step):
         self.over(step).start()
+
+    def mine(self, step, chunk):
+        slot = step if self.own.shape[0] > 1 else 0
+        return self.own[slot, chunk, :].astype(F32) + self.side_in[step, chunk, :].astype(F32)
 
     def advance(self, step):
         target = self.order[step]
         self.over(step).wait_recv()
+        self.over(step).wait_send()
 
         def forward(way, upstream):
-            @pl.when(upstream)
-            def _():
-                self.arrive(target).wait_recv()
-
+            pl.when(upstream)(lambda: self.arrive(target).wait_recv())
             strip = 64
 
             def add(index, _):
                 chunk = pl.ds(pl.multiple_of(index * strip, strip), strip)
-                total = self.own[step, chunk, :] + self.side_in[step, chunk, :].astype(F32)
-                held = self.line_in[target, chunk, :].astype(F32)
-                total = jnp.where(upstream, total + held, total)
-                self.line_out[step, chunk, :] = total.astype(BF16)
+                total = self.mine(step, chunk)
+                passing = self.line_in[target, chunk, :].astype(F32)
+                total = jnp.where(upstream, total + passing, total)
+                self.side_out[step, chunk, :] = total.astype(BF16)
 
             lax.fori_loop(0, self.own.shape[1] // strip, add, None)
             self.along(step, target, way).start()
 
-        @pl.when(target > self.line)
-        def _():
-            forward(RIGHT, self.line > 0)
-
-        @pl.when(target < self.line)
-        def _():
-            forward(LEFT, self.line < PAIRS - 1)
+        pl.when(target > self.line)(lambda: forward(RIGHT, self.line > 0))
+        pl.when(target < self.line)(lambda: forward(LEFT, self.line < PAIRS - 1))
 
     def last(self):
         self.over(0).wait_recv()
+        self.over(0).wait_send()
         pl.when(self.line > 0)(lambda: self.arrive(self.line).wait_recv())
         pl.when(self.line < PAIRS - 1)(lambda: self.arrive(PAIRS).wait_recv())
 
     def total(self, chunk):
-        total = self.own[0, chunk, :] + self.side_in[0, chunk, :].astype(F32)
+        total = self.mine(0, chunk)
         left = self.line_in[self.line, chunk, :].astype(F32)
         right = self.line_in[PAIRS, chunk, :].astype(F32)
         total = jnp.where(self.line > 0, total + left, total)
         return jnp.where(self.line < PAIRS - 1, total + right, total)
 
     def finish(self):
-        for step in range(PAIRS):
-            self.over(step).wait_send()
         for step in range(1, PAIRS):
             target = self.order[step]
             pl.when(target > self.line)(lambda: self.along(step, target, RIGHT).wait_send())
             pl.when(target < self.line)(lambda: self.along(step, target, LEFT).wait_send())
 
 
-def reduce_scratch(tokens, width):
+def reduce_scratch(tokens, width, slots, dtype):
     return [
-        pltpu.VMEM((PAIRS, tokens, width), F32),
-        pltpu.VMEM((PAIRS, tokens, width), BF16),
+        pltpu.VMEM((slots, tokens, width), dtype),
         pltpu.VMEM((PAIRS, tokens, width), BF16),
         pltpu.VMEM((PAIRS, tokens, width), BF16),
         pltpu.VMEM((PAIRS + 1, tokens, width), BF16),
@@ -845,15 +840,109 @@
     ]
 
 
+class Quarters:
+    def __init__(self, keep, away, came, far, core_send, core_recv, chip_send, chip_recv):
+        self.keep, self.away, self.came, self.far = keep, away, came, far
+        self.sems = core_send, core_recv, chip_send, chip_recv
+        base, line, side, self.quarter = spot()
+        self.place = base + line * 2 + side
+        self.core, self.chip = lax.rem(self.quarter, 2), lax.div(self.quarter, 2)
+        self.tiles = keep.shape[0]
+
+    def to_core(self, tile):
+        return send(
+            self.away.at[tile], self.came.at[tile], self.sems[0].at[tile], self.sems[1].at[tile],
+            self.place, core_peer(self.quarter),
+        )
+
+    def to_chip(self, tile):
+        return send(
+            self.away.at[tile, 0], self.far.at[tile], self.sems[2].at[tile], self.sems[3].at[tile],
+            self.place, chip_peer(self.quarter),
+        )
+
+    def put(self, tile, quarter_of):
+        for chip in range(2):
+            self.keep[tile, chip] = quarter_of(2 * chip + self.core).astype(BF16)
+            self.away[tile, chip] = quarter_of(2 * chip + 1 - self.core).astype(BF16)
+        self.to_core(tile).start()
+
+    def over_cores(self):
+        def one(tile, _):
+            self.to_core(tile).wait_recv()
+            self.to_core(tile).wait_send()
+            other = 1 - self.chip
+            passed = self.keep[tile, other].astype(F32) + self.came[tile, other].astype(F32)
+            self.away[tile, 0] = passed.astype(BF16)
+            self.to_chip(tile).start()
+            kept = self.keep[tile, self.chip].astype(F32)
+            kept = kept + self.came[tile, self.chip].astype(F32)
+            self.keep[tile, self.chip] = kept.astype(BF16)
+
+        lax.fori_loop(0, self.tiles, one, None)
+
+    def over_chips(self, then):
+        def one(tile, _):
+            self.to_chip(tile).wait_recv()
+            total = self.keep[tile, self.chip].astype(F32) + self.far[tile].astype(F32)
+            self.keep[tile, self.chip] = total.astype(BF16)
+            then(tile)
+
+        lax.fori_loop(0, self.tiles, one, None)
+
+    def total(self, tile):
+        return self.keep.at[tile, self.chip]
+
+    def finish(self):
+        lax.fori_loop(0, self.tiles, lambda tile, _: self.to_chip(tile).wait_send(), None)
+
+
+def quarters_scratch(tiles, rows, columns):
+    return [
+        pltpu.VMEM((tiles, 2, rows, columns), BF16),
+        pltpu.VMEM((tiles, 2, rows, columns), BF16),
+        pltpu.VMEM((tiles, 2, rows, columns), BF16),
+        pltpu.VMEM((tiles, rows, columns), BF16),
+    ] + [DMA((tiles,))] * 4
+
+
+class Stream:
+    def __init__(self, source, slots, sems):
+        self.source, self.slots, self.sems = source, slots, sems
+
+    def copy(self, tile):
+        size = self.slots.shape[-1]
+        start = pl.multiple_of(tile * size, size)
+        slot = lax.rem(tile, 2)
+        return pltpu.make_async_copy(
+            self.source.at[:, pl.ds(start, size)], self.slots.at[slot], self.sems.at[slot]
+        )
+
+    def run(self, tiles, use):
+        def one(tile, _):
+            self.copy(tile).wait()
+            use(tile, self.slots.at[lax.rem(tile, 2)])
+            pl.when(tile + 2 < tiles)(lambda: self.copy(tile + 2).start())
+
+        lax.fori_loop(0, tiles, one, None)
+
+
 def third_kernel(
-    x_ref, o_ref, a_ref, wo_ref, wd_ref, bias_ref, d_ref,
-    result_ref, back_out,
-    own_sem, back_send, back_recv, own, side_out, side_in, line_out, line_in, *sems,
+    x_ref, o_ref, a_ref, wo_ref, wd_ref, bias_ref, du_ref, d_ref, hm_ref, dy_ref,
+    result_ref, back_out, up_out, rows_out,
+    own_sem, back_send, back_recv, load_sem, store_sem, hm_tiles, tile_sum, dy, *rest,
 ):
     base, line, side, quarter = spot()
     rank = line * 2 + side
     tokens, width = x_ref.shape
-    reduce = Reduce(own, side_out, side_in, line_out, line_in, sems)
+    part = width // TEAM // QUARTERS
+    reduce = Reduce(*rest[:4], rest[4:8])
+    ups, downs = Quarters(*rest[8:16]), Quarters(*rest[16:24])
+    stream = Stream(hm_ref, hm_tiles, load_sem)
+    load_dy = pltpu.make_async_copy(dy_ref, dy, own_sem.at[3])
+    load_dy.start()
+    for tile in range(2):
+        stream.copy(tile).start()
     greet_line(base, line, side, quarter)
 
     def pieces(to, origin, kind):
@@ -874,33 +963,71 @@
     ]
 
     def make(which, put):
+        rows = pl.ds(pl.multiple_of(which * tokens, tokens), tokens)
         for start in range(0, width, 512):
             span = pl.ds(start, 512)
             put(
                 span,
-                dot(o_ref[which], wo_ref[:, span]) + dot(a_ref[which], wd_ref[:, span]),
+                dot(o_ref[rows, :], wo_ref[:, span]) + dot(a_ref[rows, :], wd_ref[:, span]),
             )
 
+    def put_own(span, value):
+        reduce.own[0, :, span] = value
+
     for step in reversed(range(PAIRS)):
-        place = reduce.order[step]
 
         def put_out(span, value, step=step):
-            side_out[step, :, span] = value.astype(BF16)
-
-        def put_own(span, value, step=step):
-            own[step, :, span] = value
-
-        make(place * 2 + 1 - side, put_out)
+            reduce.side_out[step, :, span] = value.astype(BF16)
+
+        make(reduce.order[step] * 2 + 1 - side, put_out)
         reduce.begin(step)
-        make(place * 2 + side, put_own)
         if step == PAIRS - 1:
             for kind in range(3):
                 own_back[kind].start()
                 for hop in range(1, QUARTERS):
                     back(lax.rem(quarter + hop, QUARTERS), quarter, kind).start()
 
-    for step in reversed(range(1, PAIRS)):
-        reduce.advance(step)
+    def up_tile(tile, held):
+        for start in range(0, tile_sum.shape[1], 512):
+            span = pl.ds(start, 512)
+            tile_sum[:, span] = contract_first(held[...], du_ref[:, span])
+        ups.put(tile, lambda q: tile_sum[pl.ds(pl.multiple_of(q * part, part), part), :])
+
+    stream.run(TEAM, up_tile)
+    make(reduce.order[3] * 2 + side, put_own)
+    reduce.advance(3)
+    ups.over_cores()
+    load_dy.wait()
+    share = width // QUARTERS
+
+    def down_tile(source, first, tile, _):
+        columns = pl.ds(pl.multiple_of(tile * 128, 128), 128)
+        rows = source[:, columns]
+
+        def quarter_of(q):
+            span = pl.ds(pl.multiple_of(q * share, share), share)
+            return contract_first(rows, dy[:, span])
+
+        downs.put(first + tile, quarter_of)
+
+    hidden = a_ref.shape[1] // 128
+    lax.fori_loop(0, hidden, partial(down_tile, a_ref, 0), None)
+    lax.fori_loop(0, HEAD // 128, partial(down_tile, o_ref, hidden), None)
+    make(reduce.order[2] * 2 + side, put_own)
+    reduce.advance(2)
+    downs.over_cores()
+    make(reduce.order[1] * 2 + side, put_own)
+    reduce.advance(1)
+    make(rank, put_own)
+
+    def store_up(tile):
+        return pltpu.make_async_copy(ups.total(tile), up_out.at[tile], store_sem.at[0])
+
+    def store_down(tile):
+        rows = pl.ds(pl.multiple_of(tile * 128, 128), 128)
+        return pltpu.make_async_copy(downs.total(tile), rows_out.at[rows, :], store_sem.at[1])
+
+    ups.over_chips(lambda tile: store_up(tile).start())
     reduce.last()
     strip = 64
 
@@ -910,6 +1037,7 @@
         result_ref[chunk, :] = (x_ref[chunk, :].astype(F32) + total).astype(BF16)
 
     lax.fori_loop(0, tokens // strip, close, None)
+    downs.over_chips(lambda tile: store_down(tile).start())
     reduce.finish()
     for kind in range(3):
         own_back[kind].wait()
@@ -917,116 +1045,504 @@
             origin = lax.rem(quarter + hop, QUARTERS)
             back(origin, quarter, kind).wait_send()
             back(origin, origin, kind).wait_recv()
-
-
-def third(x, attended, activated, w_out, w_down, bias, grads):
+    ups.finish()
+    downs.finish()
+    lax.fori_loop(0, ups.tiles, lambda tile, _: store_up(tile).wait(), None)
+    lax.fori_loop(0, downs.tiles, lambda tile, _: store_down(tile).wait(), None)
+
+
+def third(x, attended, activated, w_out, w_down, bias, grad_up, grads, mlp_input, grad_rows):
     tokens, width = x.shape
+    hidden = activated.shape[-1]
+    part, share = width // TEAM // QUARTERS, width // QUARTERS
+    tiles = (hidden + HEAD) // 128
+    shapes = [
+        (tokens, width),
+        (TEAM, tokens, 3 * HEAD),
+        (TEAM, part, hidden),
+        (tiles * 128, share),
+    ]
     return pl.pallas_call(
         third_kernel,
-        out_shape=[
-            jax.ShapeDtypeStruct((tokens, width), BF16),
-            jax.ShapeDtypeStruct((TEAM, tokens, 3 * HEAD), BF16),
-        ],
-        in_specs=[VMEM] * 6 + [ANY],
-        out_specs=[VMEM, ANY],
-        scratch_shapes=[DMA((3,)), DMA((QUARTERS, 3)), DMA((QUARTERS, 3))]
-        + reduce_scratch(tokens, width),
+        out_shape=[jax.ShapeDtypeStruct(shape, BF16) for shape in shapes],
+        in_specs=[VMEM] * 7 + [ANY] * 3,
+        out_specs=[VMEM, ANY, ANY, ANY],
+        scratch_shapes=[
+            DMA((4,)),
+            DMA((QUARTERS, 3)),
+            DMA((QUARTERS, 3)),
+            DMA((2,)),
+            DMA((2,)),
+            pltpu.VMEM((2, TEAM * tokens, width // TEAM), BF16),
+            pltpu.VMEM((width // TEAM, hidden), F32),
+            pltpu.VMEM((TEAM * tokens, width), BF16),
+        ]
+        + reduce_scratch(tokens, width, 1, F32)
+        + quarters_scratch(TEAM, part, hidden)
+        + quarters_scratch(tiles, 128, share),
         compiler_params=pltpu.CompilerParams(
             collective_id=2, has_side_effects=True, vmem_limit_bytes=LIMIT
         ),
         name="scatter_result",
-    )(x, attended, activated, w_out, w_down, bias, grads)
+    )(x, attended, activated, w_out, w_down, bias, grad_up, grads, mlp_input, grad_rows)
+
+
+class Columns:
+    def __init__(self, kind, source_of, landed, start, size, sems):
+        self.kind, self.source_of, self.landed = kind, source_of, landed
+        self.start_lane, self.size, self.sems = start, size, sems
+        self.base, line, side, self.quarter = spot()
+        self.rank = line * 2 + side
+        self.part = landed.shape[1] // QUARTERS
+
+    def region(self, source, slice_of):
+        rows = pl.ds(pl.multiple_of(slice_of * self.part, 16), self.part)
+        return self.landed.at[source, rows, pl.ds(self.start_lane, self.size)]
+
+    def deal(self, source, target, peer):
+        sends, recvs = self.sems[:2]
+        return send(
+            self.source_of(target), self.region(source, self.quarter),
+            sends.at[self.kind, target], recvs.at[self.kind, source],
+            self.base + peer, self.quarter,
+        )
+
+    def own(self):
+        return pltpu.make_async_copy(
+            self.source_of(self.rank), self.region(self.rank, self.quarter),
+            self.sems[8].at[self.kind],
+        )
+
+    def start(self):
+        self.own().start()
+
+        def one(step, _):
+            target = lax.rem(self.rank + step, TEAM)
+            self.deal(self.rank, target, target).start()
+
+        lax.fori_loop(1, TEAM, one, None)
+
+    def pass_on(self, which, source, slice_of, to):
+        block = self.region(source, slice_of)
+        sends, recvs = self.sems[2 + 2 * which : 4 + 2 * which]
+        return send(
+            block, block, sends.at[self.kind, source], recvs.at[self.kind, source],
+            self.base + self.rank, to,
+        )
+
+    def to_core(self, source):
+        return self.pass_on(0, source, self.quarter, core_peer(self.quarter))
+
+    def to_chip(self, source):
+        return self.pass_on(1, source, self.quarter, chip_peer(self.quarter))
+
+    def to_last(self, source):
+        return self.pass_on(2, source, chip_peer(self.quarter), core_peer(self.quarter))
+
+    def forward(self):
+        self.own().wait()
+        self.to_chip(self.rank).start()
+        self.to_core(self.rank).start()
+
+        def one(step, _):
+            source = lax.rem(self.rank + TEAM - step, TEAM)
+            self.deal(source, self.rank, source).wait_recv()
+            self.to_chip(source).start()
+            self.to_core(source).start()
+
+        lax.fori_loop(1, TEAM, one, None)
+
+    def forward_last(self):
+        def one(step, _):
+            source = lax.rem(self.rank + TEAM - step, TEAM)
+            self.pass_on(
+                1, source, chip_peer(self.quarter), chip_peer(self.quarter)
+            ).wait_recv()
+            self.to_last(source).start()
+
+        lax.fori_loop(0, TEAM, one, None)
+
+    def finish(self):
+        core = core_peer(self.quarter)
+
+        def one(source, _):
+            self.pass_on(0, source, core, core).wait_recv()
+            self.pass_on(2, source, chip_peer(core), core).wait_recv()
+            self.to_core(source).wait_send()
+            self.to_chip(source).wait_send()
+            self.to_last(source).wait_send()
+
+        lax.fori_loop(0, TEAM, one, None)
+
+        def sent(step, _):
+            target = lax.rem(self.rank + step, TEAM)
+            self.deal(self.rank, target, target).wait_send()
+
+        lax.fori_loop(1, TEAM, sent, None)
+
+
+COLUMN_SEMS = [DMA((2, TEAM))] * 8 + [DMA((2,))]
 
 
 def fourth_kernel(
-    x_ref, dy_ref, xs_ref, dqkv_ref, du_ref, w_ref, vec_ref,
-    grad_ref, sums_ref,
-    weight, xs, load_sem, own, side_out, side_in, line_out, line_in, *sems,
+    x_ref, dy_ref, dqkv_ref, du_ref, vec_ref, dy_sum_ref, xs_ref, w_ref, ha_ref, up_ref, rows_ref,
+    grad_ref, landed, rows_out, vector_ref,
+    weight, xs, load_sem, tile_load, ha_tiles, tile_sum, sums, packets, packets_in, ring, ring_in,
+    row_own, row_send, row_recv, pack_send, pack_recv, ring_send, ring_recv, *rest,
 ):
     base, line, side, quarter = spot()
+    rank = line * 2 + side
     tokens, width = x_ref.shape
-    reduce = Reduce(own, side_out, side_in, line_out, line_in, sems)
+    hidden = du_ref.shape[1]
+    part = width // TEAM // QUARTERS
+    block = width // TEAM
+    core, chip = core_peer(quarter), chip_peer(quarter)
+    reduce = Reduce(*rest[:4], rest[4:8])
+    qkvs = Quarters(*rest[8:16])
+    sems = rest[16:25]
+    up_columns = Columns(0, lambda n: up_ref.at[n], landed, 3 * HEAD, hidden, sems)
+    qkv_columns = Columns(1, lambda n: qkvs.total(n), landed, 0, 3 * HEAD, sems)
+    stream = Stream(ha_ref, ha_tiles, tile_load)
     loads = [
         pltpu.make_async_copy(w_ref, weight, load_sem.at[0]),
         pltpu.make_async_copy(xs_ref, xs, load_sem.at[1]),
     ]
     for copy in loads:
         copy.start()
-    greet_line(base, line, side, quarter)
-    sums_ref[...] = jnp.zeros_like(sums_ref)
+    for tile in range(2):
+        stream.copy(tile).start()
+    greet_team(base, line, side, quarter)
+
+    def rows_copy(which, slice_of, to):
+        src = rows_ref if which < 2 else rows_out.at[slice_of]
+        return send(
+            src, rows_out.at[slice_of], row_send.at[which], row_recv.at[which], base + rank, to
+        )
+
+    own_rows = pltpu.make_async_copy(rows_ref, rows_out.at[quarter], row_own)
+    own_rows.start()
+    rows_copy(0, quarter, core).start()
+    rows_copy(1, quarter, chip).start()
+    up_columns.start()
+    sums[...] = jnp.zeros_like(sums)
     for copy in loads:
         copy.wait()
 
     def make(which, put):
-        rows = xs[which].astype(F32)
-        average = jnp.mean(rows, -1, keepdims=True)
-        variance = jnp.mean(jnp.square(rows - average), -1, keepdims=True)
+        rows = pl.ds(pl.multiple_of(which * tokens, tokens), tokens)
+        values = xs[which].astype(F32)
+        average = jnp.mean(values, -1, keepdims=True)
+        variance = jnp.mean(jnp.square(values - average), -1, keepdims=True)
         inverse = lax.rsqrt(variance + EPSILON)
         for start in range(0, width, 512):
             span = pl.ds(start, 512)
-            attn = contract_last(dqkv_ref[which], weight[span, : 3 * HEAD])
-            mlp = contract_last(du_ref[which], weight[span, 3 * HEAD :])
+            attn = contract_last(dqkv_ref[rows, :], weight[span, : 3 * HEAD])
+            mlp = contract_last(du_ref[rows, :], weight[span, 3 * HEAD :])
             unit = (xs[which, :, span].astype(F32) - average) * inverse
-            sums_ref[0:1, span] += jnp.sum(attn * unit, 0, keepdims=True)
-            sums_ref[1:2, span] += jnp.sum(mlp * unit, 0, keepdims=True)
-            sums_ref[2:3, span] += jnp.sum(attn, 0, keepdims=True)
-            sums_ref[3:4, span] += jnp.sum(mlp, 0, keepdims=True)
+            sums[0:1, span] += jnp.sum(attn * unit, 0, keepdims=True)
+            sums[1:2, span] += jnp.sum(mlp * unit, 0, keepdims=True)
+            sums[2:3, span] += jnp.sum(attn, 0, keepdims=True)
+            sums[3:4, span] += jnp.sum(mlp, 0, keepdims=True)
             put(span, attn * vec_ref[0:1, span] + mlp * vec_ref[1:2, span])
+        sums[4:5, pl.ds(0, hidden)] += jnp.sum(du_ref[rows, :].astype(F32), 0, keepdims=True)
+        sums[5:6, pl.ds(0, 3 * HEAD)] += jnp.sum(
+            dqkv_ref[rows, :].astype(F32), 0, keepdims=True
+        )
 
     for step in reversed(range(PAIRS)):
-        place = reduce.order[step]
 
         def put_out(span, value, step=step):
-            side_out[step, :, span] = value.astype(BF16)
+            reduce.side_out[step, :, span] = value.astype(BF16)
+
+        make(reduce.order[step] * 2 + 1 - side, put_out)
+        reduce.begin(step)
+
+    def qkv_tile(tile, held):
+        tile_sum[...] = contract_first(held[...], dqkv_ref[...])
+        qkvs.put(tile, lambda q: tile_sum[pl.ds(pl.multiple_of(q * part, part), part), :])
+
+    stream.run(TEAM, qkv_tile)
+    qkvs.over_cores()
+    for step in reversed(range(PAIRS)):
 
         def put_own(span, value, step=step):
-            own[step, :, span] = value
-
-        make(place * 2 + 1 - side, put_out)
-        reduce.begin(step)
-        make(place * 2 + side, put_own)
-
-    for step in reversed(range(1, PAIRS)):
-        reduce.advance(step)
+            reduce.own[step, :, span] = value.astype(BF16)
+
+        make(reduce.order[step] * 2 + side, put_own)
+        if step == PAIRS - 1:
+            reduce.advance(step)
+
+    def pack(target, _):
+        span = pl.ds(pl.multiple_of(target * block, block), block)
+        packets[target, pl.ds(0, 4), :] = sums[pl.ds(0, 4), span]
+        packets[target, pl.ds(4, 1), :] = jnp.where(target == rank, dy_sum_ref[0:1, span], 0.0)
+        for index in range(3):
+            chunk = 3 * target + index
+            kind = lax.div(chunk, HEADS)
+            lanes = pl.ds(pl.multiple_of(kind * HEAD, HEAD), HEAD)
+            packets[target, pl.ds(5 + index, 1), :] = jnp.where(
+                lax.rem(chunk, HEADS) == rank, sums[5:6, lanes], 0.0
+            )
+
+    lax.fori_loop(0, TEAM, pack, None)
+
+    def pack_copy(source, target, peer):
+        return send(
+            packets.at[target], packets_in.at[source], pack_send.at[target], pack_recv.at[source],
+            base + peer, quarter,
+        )
+
+    def deal_packets(step, _):
+        target = lax.rem(rank + step, TEAM)
+        pack_copy(rank, target, target).start()
+
+    lax.fori_loop(1, TEAM, deal_packets, None)
+    packets_in[rank] = packets[rank]
+
+    up_columns.forward()
+    reduce.advance(2)
+    rows_copy(1, chip, chip).wait_recv()
+    rows_copy(2, chip, core).start()
+    qkvs.over_chips(lambda tile: None)
+    qkv_columns.start()
+    up_columns.forward_last()
+    reduce.advance(1)
+
+    def take_packets(step, _):
+        source = lax.rem(rank + TEAM - step, TEAM)
+        pack_copy(source, rank, source).wait_recv()
+
+    lax.fori_loop(1, TEAM, take_packets, None)
+    total = packets_in[0]
+    for source in range(1, TEAM):
+        total = total + packets_in[source]
+    ring[pl.ds(0, 8), :] = total
+    for index in range(hidden // block):
+        ring[pl.ds(8 + index, 1), :] = sums[4:5, pl.ds(index * block, block)]
+
+    def ring_copy(to, origin, peer):
+        return send(
+            ring, ring_in.at[origin], ring_send.at[to], ring_recv.at[origin], base + rank, peer
+        )
+
+    for hop in range(1, QUARTERS):
+        to = lax.rem(quarter + hop, QUARTERS)
+        ring_copy(to, quarter, to).start()
+    ring_in[quarter] = ring[...]
+    qkv_columns.forward()
     reduce.last()
     strip = 64
 
     def close(index, _):
         chunk = pl.ds(pl.multiple_of(index * strip, strip), strip)
-        total = reduce.total(chunk)
+        pulled = reduce.total(chunk)
         unit, inverse = normalize(x_ref[chunk, :].astype(F32))
         pulled = (
-            total
-            - jnp.mean(total, -1, keepdims=True)
-            - unit * jnp.mean(total * unit, -1, keepdims=True)
+            pulled
+            - jnp.mean(pulled, -1, keepdims=True)
+            - unit * jnp.mean(pulled * unit, -1, keepdims=True)
         )
         grad_ref[chunk, :] = (dy_ref[chunk, :].astype(F32) + inverse * pulled).astype(BF16)
 
     lax.fori_loop(0, tokens // strip, close, None)
+    qkv_columns.forward_last()
+    for hop in range(1, QUARTERS):
+        origin = lax.rem(quarter + hop, QUARTERS)
+        ring_copy(quarter, origin, origin).wait_recv()
+    vector_ref[...] = (ring_in[0] + ring_in[1]) + (ring_in[2] + ring_in[3])
+
     reduce.finish()
-
-
-def fourth(x, dy, everyone, grad_qkv, grad_up, weight, vectors):
+    qkvs.finish()
+    own_rows.wait()
+    rows_copy(0, core, core).wait_recv()
+    rows_copy(2, chip_peer(core), core).wait_recv()
+    rows_copy(0, quarter, core).wait_send()
+    rows_copy(1, quarter, chip).wait_send()
+    rows_copy(2, chip, core).wait_send()
+    up_columns.finish()
+    qkv_columns.finish()
+
+    def sent_packets(step, _):
+        target = lax.rem(rank + step, TEAM)
+        pack_copy(rank, target, target).wait_send()
+
+    lax.fori_loop(1, TEAM, sent_packets, None)
+    for hop in range(1, QUARTERS):
+        to = lax.rem(quarter + hop, QUARTERS)
+        ring_copy(to, quarter, to).wait_send()
+
+
+def fourth(
+    x, dy, grad_qkv, grad_up, gains, dy_sum, everyone, weight, attn_input, up_sums, row_sums
+):
     tokens, width = x.shape
+    hidden = grad_up.shape[-1]
+    part, block = width // TEAM // QUARTERS, width // TEAM
+    shapes = [
+        ((tokens, width), BF16),
+        ((TEAM, block, 3 * HEAD + hidden), BF16),
+        ((QUARTERS, *row_sums.shape), BF16),
+        ((16, block), F32),
+    ]
     return pl.pallas_call(
         fourth_kernel,
-        out_shape=[
-            jax.ShapeDtypeStruct((tokens, width), BF16),
-            jax.ShapeDtypeStruct((8, width), F32),
-        ],
-        in_specs=[VMEM, VMEM, ANY, VMEM, VMEM, ANY, VMEM],
-        out_specs=[VMEM, VMEM],
+        out_shape=[jax.ShapeDtypeStruct(*shape) for shape in shapes],
+        in_specs=[VMEM] * 6 + [ANY] * 5,
+        out_specs=[VMEM, ANY, ANY, VMEM],
         scratch_shapes=[
             pltpu.VMEM(weight.shape, BF16),
             pltpu.VMEM(everyone.shape, BF16),
             DMA((2,)),
+            DMA((2,)),
+            pltpu.VMEM((2, TEAM * tokens, block), BF16),
+            pltpu.VMEM((block, 3 * HEAD), F32),
+            pltpu.VMEM((8, width), F32),
+            pltpu.VMEM((TEAM, 8, block), F32),
+            pltpu.VMEM((TEAM, 8, block), F32),
+            pltpu.VMEM((16, block), F32),
+            pltpu.VMEM((QUARTERS, 16, block), F32),
+            DMA,
+            DMA((3,)),
+            DMA((3,)),
+            DMA((TEAM,)),
+            DMA((TEAM,)),
+            DMA((QUARTERS,)),
+            DMA((QUARTERS,)),
         ]
-        + reduce_scratch(tokens, width),
+        + reduce_scratch(tokens, width, PAIRS, BF16)
+        + quarters_scratch(TEAM, part, 3 * HEAD)
+        + COLUMN_SEMS,
         compiler_params=pltpu.CompilerParams(
             collective_id=3, has_side_effects=True, vmem_limit_bytes=LIMIT
         ),
         name="scatter_grad",
-    )(x, dy, everyone, grad_qkv, grad_up, weight, vectors)
+    )(x, dy, grad_qkv, grad_up, gains, dy_sum, everyone, weight, attn_input, up_sums, row_sums)
+
+
+def settle_kernel(
+    columns_ref, rows_ref, result_ref, grad_ref,
+    qkv_out, up_out, down_out, out_out, result_out, grad_out,
+    low, wide, low_rows, wide_rows, passing, load_sem, store_sem, rows_load, rows_store, copy_sem,
+):
+    team, block, span = columns_ref.shape
+    quarters, tall, share = rows_ref.shape
+    width = team * HEAD
+    hidden = span - 3 * HEAD
+    plain = [
+        (
+            pltpu.make_async_copy(src, passing.at[index], copy_sem.at[index, 0]),
+            pltpu.make_async_copy(passing.at[index], dst, copy_sem.at[index, 1]),
+        )
+        for index, (src, dst) in enumerate(((result_ref, result_out), (grad_ref, grad_out)))
+    ]
+    for load_in, _ in plain:
+        load_in.start()
+
+    def load(source):
+        slot = lax.rem(source, 2)
+        return pltpu.make_async_copy(columns_ref.at[source], low.at[slot], load_sem.at[slot])
+
+    def stores(source):
+        slot = lax.rem(source, 2)
+        pairs = []
+        for kind in range(3):
+            start = pl.multiple_of(kind * width + source * HEAD, HEAD)
+            pairs.append((pl.ds(kind * HEAD, HEAD), qkv_out.at[:, pl.ds(start, HEAD)]))
+        start = pl.multiple_of(source * hidden, hidden)
+        pairs.append((pl.ds(3 * HEAD, hidden), up_out.at[:, pl.ds(start, hidden)]))
+        return [
+            pltpu.make_async_copy(wide.at[slot, :, lanes], dst, store_sem.at[slot, index])
+            for index, (lanes, dst) in enumerate(pairs)
+        ]
+
+    def load_rows(quarter):
+        slot = lax.rem(quarter, 2)
+        return pltpu.make_async_copy(rows_ref.at[quarter], low_rows.at[slot], rows_load.at[slot])
+
+    def stores_rows(quarter):
+        slot = lax.rem(quarter, 2)
+        lanes = pl.ds(pl.multiple_of(quarter * share, share), share)
+        size = tall - HEAD
+        return [
+            pltpu.make_async_copy(
+                wide_rows.at[slot, pl.ds(0, size), :], down_out.at[:, lanes], rows_store.at[slot, 0]
+            ),
+            pltpu.make_async_copy(
+                wide_rows.at[slot, pl.ds(size, HEAD), :], out_out.at[:, lanes],
+                rows_store.at[slot, 1],
+            ),
+        ]
+
+    def run(count, load, stores, low, wide, strip):
+        def one(index, _):
+            slot = lax.rem(index, 2)
+            load(index).wait()
+
+            @pl.when(index >= 2)
+            def _():
+                for copy in stores(index - 2):
+                    copy.wait()
+
+            def widen(step, _):
+                chunk = pl.ds(pl.multiple_of(step * strip, strip), strip)
+                wide[slot, chunk, :] = low[slot, chunk, :].astype(F32)
+
+            lax.fori_loop(0, low.shape[1] // strip, widen, None)
+            for copy in stores(index):
+                copy.start()
+            pl.when(index + 2 < count)(lambda: load(index + 2).start())
+
+        lax.fori_loop(0, count, one, None)
+
+    for index in range(2):
+        load_rows(index).start()
+        load(index).start()
+    for load_in, store_out in plain:
+        load_in.wait()
+        store_out.start()
+    run(quarters, load_rows, stores_rows, low_rows, wide_rows, 64)
+    run(team, load, stores, low, wide, min(64, block))
+    for index in (quarters - 2, quarters - 1):
+        for copy in stores_rows(index):
+            copy.wait()
+    for index in (team - 2, team - 1):
+        for copy in stores(index):
+            copy.wait()
+    for _, store_out in plain:
+        store_out.wait()
+
+
+def settle(columns, row_sums, result, grad_inputs):
+    team, block, span = columns.shape
+    quarters, tall, share = row_sums.shape
+    shapes = [
+        ((block, team * 3 * HEAD), F32),
+        ((block, team * (span - 3 * HEAD)), F32),
+        ((tall - HEAD, quarters * share), F32),
+        ((HEAD, quarters * share), F32),
+        (result.shape, BF16),
+        (grad_inputs.shape, BF16),
+    ]
+    return pl.pallas_call(
+        settle_kernel,
+        out_shape=[jax.ShapeDtypeStruct(*shape) for shape in shapes],
+        in_specs=[ANY] * 4,
+        out_specs=[ANY] * 6,
+        scratch_shapes=[
+            pltpu.VMEM((2, block, span), BF16),
+            pltpu.VMEM((2, block, span), F32),
+            pltpu.VMEM((2, tall, share), BF16),
+            pltpu.VMEM((2, tall, share), F32),
+            pltpu.VMEM((2, *result.shape), BF16),
+            DMA((2,)),
+            DMA((2, 4)),
+            DMA((2,)),
+            DMA((2, 2)),
+            DMA((2, 2)),
+        ],
+        compiler_params=pltpu.CompilerParams(vmem_limit_bytes=LIMIT),
+        name="settle",
+    )(columns, row_sums, result, grad_inputs)
 
 
 def on_device(
@@ -1116,88 +1632,56 @@
         grad_mine, w_out, w_down, up_values, attended
     )
     grads = attend_back(qkv, grad_attended, column, row, tables)
+    flat = (TEAM * tokens, -1)
+    attn_input, mlp_input, grad_rows, activated, grad_up, attended = (
+        values.reshape(flat)
+        for values in (attn_input, mlp_input, grad_rows, activated, grad_up, attended)
+    )
     branch_bias = (vectors[:, 4] + vectors[:, 5]).reshape(1, width)
-    result, grad_qkv = third(
-        mine, attended, activated, w_out, w_down, branch_bias, grads
+    result, grad_qkv, up_sums, row_sums = third(
+        mine, attended, activated, w_out, w_down, branch_bias, grad_up, grads, mlp_input, grad_rows
     )
     gains = vectors[:, :2].transpose(1, 0, 2).reshape(2, width)
-    grad_inputs, sums = fourth(
-        mine_team, team_order(grad_mine), everyone, grad_qkv, grad_up, weight, gains
+    grad_inputs, columns, row_sums, vector = fourth(
+        mine_team, team_order(grad_mine), grad_qkv.reshape(flat), grad_up, gains, dy_sum, everyone,
+        weight, attn_input, up_sums, row_sums,
     )
     grad_inputs = plain_order(grad_inputs)
-
-    flat = (TEAM * tokens, -1)
-    attn_input, mlp_input = attn_input.reshape(flat), mlp_input.reshape(flat)
-    grad_rows, grad_qkv, grad_up = (
-        values.reshape(flat) for values in (grad_rows, grad_qkv, grad_up)
-    )
-    attended, activated = attended.reshape(flat), activated.reshape(flat)
-    qkv_bias_sum = lax.dynamic_update_slice_in_dim(
-        jnp.zeros((3, HEADS, HEAD), F32),
-        jnp.sum(grad_qkv.astype(F32), 0).reshape(3, 1, HEAD), rank, 1,
-    )
-    up_bias_sum = lax.dynamic_update_slice_in_dim(
-        jnp.zeros((TEAM, hidden), F32), jnp.sum(grad_up.astype(F32), 0)[None], rank, 0
-    )
-    vector = jnp.concatenate(
-        [
-            plain_order(sums[:4]).reshape(-1),
-            qkv_bias_sum.reshape(-1),
-            dy_sum[0] * jnp.where(rank == 0, 1.0, 0.0),
-            up_bias_sum.reshape(-1),
-        ]
-    )
-    vector = lax.psum(vector, ("dp", "ctx"))
-
-    def own(start, size):
-        return lax.dynamic_slice_in_dim(vector, start + place * (size // dp), size // dp, 0)
-
-    grad_gain = jnp.stack([own(0, width), own(width, width)])
-    grad_shift = jnp.stack([own(2 * width, width), own(3 * width, width)])
-    grad_qkv_b = own(4 * width, 3 * width)
-    grad_out_b = own(7 * width, width)
-    grad_up_b = own(8 * width, TEAM * hidden)
-
-    term_out = contract_first(attended, grad_rows).astype(BF16)
-    term_down = contract_first(activated, grad_rows).astype(BF16)
-    term_columns = jnp.concatenate(
-        [
-            contract_first(attn_input, grad_qkv).astype(BF16),
-            contract_first(mlp_input, grad_up).astype(BF16),
-        ],
-        -1,
-    )
-    span = term_columns.shape[-1]
-    if teams > 1:
+    if teams == 1:
+        grad_gain, grad_shift, grad_out_b = vector[0:2], vector[2:4], vector[4]
+        grad_qkv_b, grad_up_b = vector[5:8].reshape(-1), vector[8 : 8 + hidden // rows].reshape(-1)
+    else:
+        near = partial(lax.all_gather, axis_name="dp", axis_index_groups=together, tiled=True)
+
+        def own(values):
+            size = values.shape[0] // dp
+            total = lax.psum(values, "dp", axis_index_groups=across)
+            return lax.dynamic_slice_in_dim(total, place * size, size, 0)
+
+        ends = lax.psum_scatter(
+            vector[:4], "dp", scatter_dimension=1, axis_index_groups=across, tiled=True
+        )
+        grad_gain, grad_shift = ends[0:2], ends[2:4]
+        grad_out_b = own(near(vector[4], axis=0))
+        grad_qkv_b = own(near(vector[5:8].reshape(-1), axis=0))
+        grad_up_b = own(near(vector[8 : 8 + hidden // rows].reshape(-1), axis=0))
+
         def scatter_rows(term):
             size = term.shape[0]
             full = jnp.zeros((TEAM, size, width), BF16)
-            full = lax.dynamic_update_slice_in_dim(full, term[None], rank, 0)
+            full = lax.dynamic_update_slice_in_dim(full, term.astype(BF16)[None], rank, 0)
             return lax.psum_scatter(
                 full.reshape(TEAM * size, width), "dp", scatter_dimension=0, tiled=True
-            )
-
-        term_out, term_down = scatter_rows(term_out), scatter_rows(term_down)
-        term_columns = term_columns.reshape(TEAM, teams, shard, span).swapaxes(0, 1)
-        term_columns = lax.psum_scatter(
-            term_columns.reshape(width, span), "dp", scatter_dimension=0,
-            axis_index_groups=across, tiled=True,
-        )
-    grad_out_w = lax.psum(term_out, "ctx").astype(F32)
-    grad_down_w = lax.psum(term_down, "ctx").astype(F32)
-    term_columns = term_columns.reshape(TEAM, shard, span)
-    term_columns = lax.psum_scatter(term_columns, "ctx", scatter_dimension=1, tiled=True)
-    term_columns = lax.all_to_all(
-        term_columns, "dp", 0, 0, axis_index_groups=together, tiled=True
+            ).astype(F32)
+
+        columns = lax.psum_scatter(
+            columns, "dp", scatter_dimension=1, axis_index_groups=across, tiled=True
+        )
+    grad_qkv_w, grad_up_w, grad_down_w, grad_out_w, result, grad_inputs = settle(
+        columns, row_sums, result, grad_inputs
     )
-    term_columns = lax.all_gather(term_columns, "ctx", axis=1, tiled=True)
-    grad_qkv_w = (
-        term_columns[:, :, : 3 * HEAD].reshape(TEAM, shard, 3, HEAD).transpose(1, 2, 0, 3)
-        .reshape(shard, 3 * width).astype(F32)
-    )
-    grad_up_w = (
-        term_columns[:, :, 3 * HEAD :].transpose(1, 0, 2).reshape(shard, TEAM * hidden).astype(F32)
-    )
+    if teams > 1:
+        grad_out_w, grad_down_w = scatter_rows(grad_out_w), scatter_rows(grad_down_w)
     return (
         result.reshape(inputs.shape),
         grad_inputs.reshape(inputs.shape),

time: 927 us -> 591 us (0.64)
  waiting for transfers between devices: 256 us -> 0 us
  Pallas kernels: 502 us -> 559 us
  matrix products: 45.8 us -> 0 us
  local copies, waits for them, and re-layouts: 65 us -> 19.2 us
  other arithmetic: 31.1 us -> 5.88 us
  between operations: 16.2 us -> 1.22 us
    psum x2 -> x0, waiting for transfers between devices: 178 us -> none  [the longest x1 102 us: on_device(): grad_out_w = lax.psum(term_out, 'ctx').astype(F32)]
    pallas_call x2 -> x3, Pallas kernels: 224 us -> 281 us  [the longest x1 145 us: fourth(): pl.pallas_call(fourth_kernel, out_shape=[jax.ShapeDtypeStruct(*shape) for...]
    dot_general x4 -> x0, matrix products: 45.8 us -> none  [contract_first(): lax.dot_general(left, right, (((0,), (0,)), ((), ())), preferred_element_...]
    all_gather x1 -> x0, waiting for transfers between devices: 45.7 us -> none  [on_device(): term_columns = lax.all_gather(term_columns, 'ctx', axis=1, tiled=True)]
    all_to_all x1 -> x0, waiting for transfers between devices: 32.7 us -> none  [on_device(): lax.all_to_all(term_columns, 'dp', 0, 0, axis_index_groups=together, tile...]
    unnamed x34 -> x11, local copies, waits for them, and re-layouts: 33.1 us -> 5.93 us
    convert_element_type x4 -> x0, other arithmetic: 13.1 us -> none  [the longest x1 6.65 us: on_device(): grad_down_w = lax.psum(term_down, 'ctx').astype(F32)]
    reshape x2 -> x1, local copies, waits for them, and re-layouts: 11.6 us -> 0.6 us  [on_device(): vector[5:8].reshape(-1)]
  transfers between devices with their start and end apart: 5 -> 0, of which waited for: 4 -> 0; matrix products, arithmetic and copies ran while one was open for 5% -> 0% of each run, Pallas kernels for 12% -> 0%
where the time goes in v3:
time: 591 us; the launch traced here: 585 us
  Pallas kernels  559 us (95%)
  local copies, waits for them, and re-layouts  19.2 us (3%)
    pallas_call x1, Pallas kernels, first(): pl.pallas_call(first_kernel, out_shape=[jax.ShapeDtypeStruct(*shape) for...  153 us
    pallas_call x1, Pallas kernels, fourth(): pl.pallas_call(fourth_kernel, out_shape=[jax.ShapeDtypeStruct(*shape) for...  145 us
    pallas_call x1, Pallas kernels, third(): pl.pallas_call(third_kernel, out_shape=[jax.ShapeDtypeStruct(shape, BF16)...  121 us
    pallas_call x1, Pallas kernels, second(): pl.pallas_call(second_kernel, out_shape=[jax.ShapeDtypeStruct(*shape) for...  110 us
    pallas_call x1, Pallas kernels, settle(): pl.pallas_call(settle_kernel, out_shape=[jax.ShapeDtypeStruct(*shape) for...  15.2 us

profile of v3, /device:TPU:19, one launch (start us, length us, event | category | flops | bytes accessed | tf_op | source)
XLA Modules:
  0.0 585.4 jit_solution(9826529272506504124)
XLA Ops:
  0.7 0.1 pad.5.clone
  0.7 0.1 pad.8.clone
  0.8 0.7 convert_element_type.43
  1.5 0.7 stack.9
  2.2 0.7 stack.10
  2.8 0.7 reshape.127
  3.5 1.3 reshape.128
  4.8 2.5 concatenate.12.vec_ref
  7.3 1.9 multiply_sine_fusion
  9.3 0.5 maximum_maximum_fusion.2
  9.8 0.7 constant_dynamic-slice_fusion.below_ref
  10.4 0.7 constant_dynamic-slice_fusion.1.above_ref
  11.1 0.7 constant_dynamic-slice_fusion.2.cos_ref
  11.8 153.0 %gather_x.1 = (bf16[8,256,2048]{2,1,0:T(8,128)(2,1)}, bf16[8,256,2048]{2,1,0:T(8,128)(2,1)}, bf16[8,256,2048]{2,1,0:T(8,128)(2,1)}, f32[8,256,1024]{2,1,0:T(8,12...) custom-call(bf16[256,2048]{1,0:T(8,128)(2,1)} %bitcast.26, ...), custom_call_target="tpu_custom_call" | custom-call | tf_op jit(solution)/shard_map/gather_x/pallas_call | solution.py:502
  164.8 1.5 slice_add_fusion
  166.3 1.4 slice.30
  167.8 0.9 fusion.1
  168.6 0.9 broadcast_in_dim_reshape_squeeze.8.col_ref
  169.5 0.0 copy-start
  169.5 1.9 copy-done
  171.4 4.5 attend.1.o_ref
  176.0 0.0 copy-start.1
  176.0 1.0 copy-done.1
  176.9 109.5 %gather_dy.1 = (bf16[8,256,2048]{2,1,0:T(8,128)(2,1)}, bf16[8,256,1024]{2,1,0:T(8,128)(2,1)}, bf16[8,256,1024]{2,1,0:T(8,128)(2,1)}, bf16[2,1024,256]{2,1,0:T(8,...) custom-call(bf16[256,2048]{1,0:T(8,128)(2,1)} %bitcast.33, bf16[256,2048]{1,0:T(8,128)(2,1)} %wo_ref.3, ...), custom_call_target="tpu_custom_call" | custom-call | tf_op jit(solution)/shard_map/gather_dy/pallas_call | solution.py:633
  286.5 0.0 copy-start.2
  286.5 1.2 copy-done.2
  287.7 10.6 %attend_back.1.d_ref = bf16[2,3,1024,256]{3,2,1,0:T(8,128)(2,1)} custom-call(bf16[2,3,1024,256]{3,2,1,0:T(8,128)(2,1)} %get-tuple-element.41.qkv_ref, bf16[2,1024,256]{2,1,0:T(8,128)(2,1)S(1)} %copy-done.2, f32[2,1024,1]{2,1,0:T(8,128)S(1)} %broadcast_in_dim_reshape_squeeze.8.col_ref, f32[2,1,1024]{2,1,0:T(1,128)S(1)} %bitcast.23, ...), custom_call_target="tpu_custom_call" | custom-call | tf_op jit(solution)/shard_map/attend_back/pallas_call | solution.py:737
  298.3 121.3 %scatter_result.1 = (bf16[256,2048]{1,0:T(8,128)(2,1)}, bf16[8,256,768]{2,1,0:T(8,128)(2,1)}, bf16[8,64,1024]{2,1,0:T(8,128)(2,1)}, bf16[1280,512]{1,0:T(8,128)(2,1)}) custom-call(bf16[256,2048]{1,0:T(8,128)(2,1)} %bitcast.27, bf16[2048,256]{1,0:T(8,128)(2,1)} %bitcast.36, bf16[2048,1024]{1,0:T(8,128)(2,1)} %bitcast.32, bf16[256,2048]{1,0:T(8,128)(2,1)} %wo_ref.3, ...), custom_call_target="tpu_custom_call" | custom-call | tf_op jit(solution)/shard_map/scatter_result/pallas_call | solution.py:1065
  419.6 145.0 %scatter_grad.1 = (bf16[256,2048]{1,0:T(8,128)(2,1)}, bf16[8,256,1792]{2,1,0:T(8,128)(2,1)}, bf16[4,1280,512]{2,1,0:T(8,128)(2,1)}, f32[16,256]{1,0:T(8,128)}) custom-call(bf16[256,2048]{1,0:T(8,128)(2,1)} %bitcast.28, bf16[256,2048]{1,0:T(8,128)(2,1)} %bitcast.34, bf16[2048,768]{1,0:T(8,128)(2,1)} %bitcast.35, bf16[2048,1024]{1,0:T(8,128)(2,1)} %bitcast.25, ...), custom_call_target="tpu_custom_call" | custom-call | tf_op jit(solution)/shard_map/scatter_grad/pallas_call | solution.py:1387
  564.6 0.7 slice.34
  565.3 0.0 copy-start.3
  565.3 0.7 slice.33
  566.0 0.6 reshape.124
  566.6 0.7 slice_bitcast_fusion
  567.3 1.4 fusion.2
  568.6 0.6 copy.27
  569.2 15.2 %settle.1 = (f32[256,6144]{1,0:T(8,128)}, f32[256,8192]{1,0:T(8,128)}, f32[1024,2048]{1,0:T(8,128)}, f32[256,2048]{1,0:T(8,128)}, bf16[256,2048]{1,0:T(8,128)(2,1)}, /*index=5*/bf16[256,2048]{1,0:T(8,128)(2,1)}) custom-call(bf16[8,256,1792]{2,1,0:T(8,128)(2,1)} %get-tuple-element.57.columns_ref, bf16[4,1280,512]{2,1,0:T(8,128)(2,1)} %get-tuple-element.58.rows_ref, ...), custom_call_target="tpu_custom_call" | custom-call | tf_op jit(solution)/shard_map/settle/pallas_call | solution.py:1526
  584.4 0.0 copy-done.3
  584.4 0.6 copy.29
  (9 shorter events, 0.1 us)
Async XLA Ops:
  169.5 1.9 copy-start
  176.0 1.0 copy-start.1
  286.5 1.2 copy-start.2
  565.3 19.1 %copy-start.3 = (f32[1,256]{1,0:T(1,128)}, f32[1,256]{1,0:T(1,128)S(1)}, u32[]{:S(2)}) copy-start(f32[1,256]{1,0:T(1,128)S(1)} %slice.34) | copy-start | bytes 3076

commit v4 on v3

--- a/solution.py
+++ b/solution.py
@@ -111,24 +111,43 @@
 
 
 class Relay:
-    def __init__(self, held, line_send, line_recv, side_send, side_recv):
+    def __init__(self, held, line_send, line_recv, side_send, side_recv, half_send, half_recv):
         self.held = held
-        self.sems = line_send, line_recv, side_send, side_recv
+        self.sems = line_send, line_recv, side_send, side_recv, half_send, half_recv
         self.base, self.line, self.side, self.quarter = spot()
+        self.half = held.shape[1] // 2
+
+    def neighbour(self, way):
+        return self.base + self.line * 2 + self.side + (2 if way == RIGHT else -2)
 
     def along(self, source, way):
-        line_send, line_recv, _, _ = self.sems
         block = self.held.at[source * 2 + self.side]
-        place = self.base + self.line * 2 + self.side + (2 if way == RIGHT else -2)
         return send(
-            block, block, line_send.at[way, source], line_recv.at[source], place, self.quarter
-        )
-
-    def over(self, source, side):
-        _, _, side_send, side_recv = self.sems
+            block, block, self.sems[0].at[way, source], self.sems[1].at[source],
+            self.neighbour(way), self.quarter,
+        )
+
+    def along_half(self, way):
+        source = 0 if way == RIGHT else PAIRS - 1
+        block = self.held.at[source * 2 + 1 - self.side, pl.ds(0, self.half)]
+        return send(
+            block, block, self.sems[4].at[way], self.sems[5].at[way], self.neighbour(way),
+            self.quarter,
+        )
+
+    def over(self, source, side, low):
         block = self.held.at[source * 2 + side]
+        if low:
+            block = self.held.at[source * 2 + side, pl.ds(self.half, self.half)]
         place = self.base + self.line * 2 + 1 - self.side
-        return send(block, block, side_send.at[source], side_recv.at[source], place, self.quarter)
+        return send(
+            block, block, self.sems[2].at[source], self.sems[3].at[source], place, self.quarter
+        )
+
+    def crossing(self, source, side, act):
+        parted = (source != self.line) & (lax.rem(source, PAIRS - 1) == 0)
+        pl.when(parted)(lambda: act(self.over(source, side, True)))
+        pl.when(jnp.logical_not(parted))(lambda: act(self.over(source, side, False)))
 
     def each(self, step, act):
         line = self.line
@@ -157,24 +176,51 @@
             if way == "arrive":
                 self.along(source, RIGHT).wait_recv()
             elif way is None:
-                self.over(source, self.side).start()
+                self.crossing(source, self.side, lambda copy: copy.start())
             else:
                 self.along(source, way).start()
 
         self.each(step, act)
+
+    def start_halves(self):
+        for end, way in ((0, RIGHT), (PAIRS - 1, LEFT)):
+
+            @pl.when(self.line == end)
+            def _(end=end, way=way):
+                self.over(self.line, 1 - self.side, False).wait_recv()
+                self.along_half(way).start()
+
+    def pass_halves(self, step):
+        for end, way in ((0, RIGHT), (PAIRS - 1, LEFT)):
+            here = step if way == RIGHT else PAIRS - 1 - step
+
+            @pl.when(self.line == here)
+            def _(way=way):
+                self.along_half(way).wait_recv()
+                if step < PAIRS - 1:
+                    self.along_half(way).start()
+
+    def wait_over(self, step, source):
+        def take(copy):
+            copy.wait_recv()
+
+        if step == 0:
+            inner = (self.line > 0) & (self.line < PAIRS - 1)
+            pl.when(inner)(lambda: take(self.over(source, 1 - self.side, False)))
+        else:
+            self.crossing(source, 1 - self.side, take)
 
     def finish(self):
         def act(source, way):
             if way is None:
-                self.over(source, self.side).wait_send()
+                self.crossing(source, self.side, lambda copy: copy.wait_send())
             elif way != "arrive":
                 self.along(source, way).wait_send()
 
         for step in range(PAIRS):
             self.each(step, act)
-
-    def wait_over(self, source):
-        self.over(source, 1 - self.side).wait_recv()
+        pl.when(self.line < PAIRS - 1)(lambda: self.along_half(RIGHT).wait_send())
+        pl.when(self.line > 0)(lambda: self.along_half(LEFT).wait_send())
 
 
 RELAY_SEMS = [
@@ -182,6 +228,8 @@
     pltpu.SemaphoreType.DMA((PAIRS,)),
     pltpu.SemaphoreType.DMA((PAIRS,)),
     pltpu.SemaphoreType.DMA((PAIRS,)),
+    pltpu.SemaphoreType.DMA((2,)),
+    pltpu.SemaphoreType.DMA((2,)),
 ]
 
 
@@ -274,21 +322,124 @@
     ]
 
 
+class Columns:
+    def __init__(self, pieces, place, lane, lanes, sems):
+        self.pieces, self.place, self.lane, self.lanes, self.sems = pieces, place, lane, lanes, sems
+        self.base, line, side, self.quarter = spot()
+        self.rank = line * 2 + side
+
+    def deal(self, source, target, peer):
+        sends, recvs = self.sems[:2]
+        return [
+            send(
+                src, self.place(source, self.quarter, lane, lanes),
+                sends.at[index, target], recvs.at[index, source], self.base + peer, self.quarter,
+            )
+            for index, (src, lane, lanes) in enumerate(self.pieces(target))
+        ]
+
+    def own(self):
+        return [
+            pltpu.make_async_copy(
+                src, self.place(self.rank, self.quarter, lane, lanes), self.sems[2].at[index]
+            )
+            for index, (src, lane, lanes) in enumerate(self.pieces(self.rank))
+        ]
+
+    def start(self):
+        for copy in self.own():
+            copy.start()
+
+        def one(step, _):
+            target = lax.rem(self.rank + step, TEAM)
+            for copy in self.deal(self.rank, target, target):
+                copy.start()
+
+        lax.fori_loop(1, TEAM, one, None)
+
+    def pass_on(self, which, source, slice_of, to):
+        block = self.place(source, slice_of, self.lane, self.lanes)
+        sends, recvs = self.sems[3 + 2 * which : 5 + 2 * which]
+        return send(
+            block, block, sends.at[source], recvs.at[source], self.base + self.rank, to
+        )
+
+    def to_core(self, source):
+        return self.pass_on(0, source, self.quarter, core_peer(self.quarter))
+
+    def to_chip(self, source):
+        return self.pass_on(1, source, self.quarter, chip_peer(self.quarter))
+
+    def to_last(self, source):
+        return self.pass_on(2, source, chip_peer(self.quarter), core_peer(self.quarter))
+
+    def forward(self):
+        for copy in self.own():
+            copy.wait()
+        self.to_chip(self.rank).start()
+        self.to_core(self.rank).start()
+
+        def one(step, _):
+            source = lax.rem(self.rank + TEAM - step, TEAM)
+            for copy in self.deal(source, self.rank, source):
+                copy.wait_recv()
+            self.to_chip(source).start()
+            self.to_core(source).start()
+
+        lax.fori_loop(1, TEAM, one, None)
+
+    def forward_last(self):
+        chip = chip_peer(self.quarter)
+
+        def one(step, _):
+            source = lax.rem(self.rank + TEAM - step, TEAM)
+            self.pass_on(1, source, chip, chip).wait_recv()
+            self.to_last(source).start()
+
+        lax.fori_loop(0, TEAM, one, None)
+
+    def arrive(self):
+        core = core_peer(self.quarter)
+
+        def one(source, _):
+            self.pass_on(0, source, core, core).wait_recv()
+            self.pass_on(2, source, chip_peer(core), core).wait_recv()
+
+        lax.fori_loop(0, TEAM, one, None)
+
+    def finish(self):
+        def one(source, _):
+            self.to_core(source).wait_send()
+            self.to_chip(source).wait_send()
+            self.to_last(source).wait_send()
+
+        lax.fori_loop(0, TEAM, one, None)
+
+        def sent(step, _):
+            target = lax.rem(self.rank + step, TEAM)
+            for copy in self.deal(self.rank, target, target):
+                copy.wait_send()
+
+        lax.fori_loop(1, TEAM, sent, None)
+
+
+def column_sems(count):
+    dma = pltpu.SemaphoreType.DMA
+    return [dma((count, TEAM))] * 2 + [dma((count,))] + [dma((TEAM,))] * 6
+
+
 def first_kernel(
-    x_ref, wq_ref, wu_ref, vec_ref, upb_ref, cos_ref, above_ref, below_ref,
-    x_out, ha_out, hm_out, u_out, w_out, qkv_out, seg_out, vec_out,
-    held, weight, vecs, ha, hm, up, qkv, vectors,
-    own_sem, store_sem, w_send, w_recv, w_own, core_send, core_recv, chip_send, chip_recv,
-    last_send, last_recv, v_send, v_recv, spread_send, spread_recv, spread_own, *relay_sems,
+    x_ref, wq_ref, vec_ref, cos_ref, above_ref, below_ref,
+    x_out, ha_out, hm_out, w_out, qkv_out, seg_out, vec_out,
+    held, weight, vecs, ha, hm, qkv, vectors,
+    own_sem, store_sem, last_store, v_send, v_recv, spread_send, spread_recv, spread_own, *sems,
 ):
     base, line, side, quarter = spot()
     rank = line * 2 + side
     tokens, width = x_ref.shape
     rows = wq_ref.shape[0]
     part = rows // QUARTERS
-    hidden = up.shape[-1]
-    core, chip = core_peer(quarter), chip_peer(quarter)
-    relay = Relay(held, *relay_sems)
+    relay = Relay(held, *sems[:6])
     spread = Spread(
         [
             (
@@ -299,123 +450,73 @@
         ],
         spread_send, spread_recv, spread_own,
     )
+    columns = Columns(
+        lambda target: [
+            (
+                wq_ref.at[
+                    pl.ds(pl.multiple_of(quarter * part, 16), part),
+                    pl.ds(pl.multiple_of(kind * width + target * HEAD, HEAD), HEAD),
+                ],
+                kind * HEAD,
+                HEAD,
+            )
+            for kind in range(3)
+        ],
+        lambda source, slice_of, lane, lanes: weight.at[
+            pl.ds(pl.multiple_of(source * rows + slice_of * part, 16), part), pl.ds(lane, lanes)
+        ],
+        0, 3 * HEAD, sems[6:15],
+    )
     greet_team(base, line, side, quarter)
+
+    def vector_copy(source, target, peer):
+        return send(
+            vec_ref, vecs.at[source], v_send.at[target], v_recv.at[source], base + peer, quarter
+        )
 
     own_x = pltpu.make_async_copy(x_ref, held.at[rank], own_sem.at[0])
     own_x.start()
     own_v = pltpu.make_async_copy(vec_ref, vecs.at[rank], own_sem.at[1])
     own_v.start()
 
-    def band(origin, slice_of):
-        return pl.ds(pl.multiple_of(origin * rows + slice_of * part, 16), part)
-
-    def columns(source, target):
-        mine = pl.ds(pl.multiple_of(quarter * part, 16), part)
-        pieces = []
-        for kind in range(3):
-            start = pl.multiple_of(kind * width + target * HEAD, HEAD)
-            pieces.append(
-                (
-                    wq_ref.at[mine, pl.ds(start, HEAD)],
-                    weight.at[band(source, quarter), pl.ds(kind * HEAD, HEAD)],
-                )
-            )
-        start = pl.multiple_of(target * hidden, hidden)
-        pieces.append(
-            (
-                wu_ref.at[mine, pl.ds(start, hidden)],
-                weight.at[band(source, quarter), pl.ds(3 * HEAD, hidden)],
-            )
-        )
-        return pieces
-
-    def column_copies(source, target, peer):
-        return [
-            send(src, dst, w_send.at[kind, target], w_recv.at[kind, source], base + peer, quarter)
-            for kind, (src, dst) in enumerate(columns(source, target))
-        ]
-
-    def vector_copy(source, target, peer):
-        return send(
-            vec_ref, vecs.at[source], v_send.at[target], v_recv.at[source], base + peer, quarter
-        )
-
-    def send_columns(step, _):
+    def send_vector(step, _):
         target = lax.rem(rank + step, TEAM)
         vector_copy(rank, target, target).start()
-        for copy in column_copies(rank, target, target):
-            copy.start()
-
-    lax.fori_loop(1, TEAM, send_columns, None)
-    own_columns = [
-        pltpu.make_async_copy(src, dst, w_own.at[kind])
-        for kind, (src, dst) in enumerate(columns(rank, rank))
-    ]
-    for copy in own_columns:
-        copy.start()
+
+    lax.fori_loop(1, TEAM, send_vector, None)
+    columns.start()
     own_x.wait()
     own_v.wait()
     relay.start(0)
-
-    def pass_on(origin, slice_of, sends, recvs, to):
-        block = weight.at[band(origin, slice_of), :]
-        return send(block, block, sends.at[origin], recvs.at[origin], base + rank, to)
-
-    def to_core(origin):
-        return pass_on(origin, quarter, core_send, core_recv, core)
-
-    def to_chip(origin):
-        return pass_on(origin, quarter, chip_send, chip_recv, chip)
-
-    def to_last(origin):
-        return pass_on(origin, chip, last_send, last_recv, core)
-
-    for copy in own_columns:
-        copy.wait()
-    to_chip(rank).start()
-    to_core(rank).start()
-
-    def forward_columns(step, _):
-        origin = lax.rem(rank + TEAM - step, TEAM)
-        for copy in column_copies(origin, rank, origin):
-            copy.wait_recv()
-        to_chip(origin).start()
-        to_core(origin).start()
-
-    lax.fori_loop(1, TEAM, forward_columns, None)
+    columns.forward()
+    relay.start_halves()
     relay.start(1)
-
-    def forward_chip(step, _):
-        origin = lax.rem(rank + TEAM - step, TEAM)
-        pass_on(origin, chip, chip_send, chip_recv, chip).wait_recv()
-        to_last(origin).start()
-
-    lax.fori_loop(0, TEAM, forward_chip, None)
-    relay.start(2)
-
-    def take_vectors(step, _):
+    columns.forward_last()
+
+    def take_vector(step, _):
         origin = lax.rem(rank + TEAM - step, TEAM)
         vector_copy(origin, rank, origin).wait_recv()
 
-    lax.fori_loop(1, TEAM, take_vectors, None)
+    lax.fori_loop(1, TEAM, take_vector, None)
     for source in range(TEAM):
         for row in range(4):
             vectors[pl.ds(row, 1), pl.ds(source * rows, rows)] = vecs[source, pl.ds(row, 1), :]
-
-    def last_columns(step, _):
-        origin = lax.rem(rank + TEAM - step, TEAM)
-        pass_on(origin, core, core_send, core_recv, core).wait_recv()
-        pass_on(origin, chip_peer(core), last_send, last_recv, core).wait_recv()
-
-    lax.fori_loop(0, TEAM, last_columns, None)
-    stores = [
-        pltpu.make_async_copy(weight, w_out, store_sem.at[0]),
-        pltpu.make_async_copy(vecs, vec_out, store_sem.at[1]),
+    columns.arrive()
+    last_stores = [
+        pltpu.make_async_copy(weight, w_out, last_store.at[0]),
+        pltpu.make_async_copy(vecs, vec_out, last_store.at[1]),
     ]
-    for copy in stores:
+    for copy in last_stores:
         copy.start()
 
     strip = 32
+    own_rows = pl.ds(pl.multiple_of(quarter * tokens, tokens), tokens)
+
+    def stores(which):
+        return [
+            pltpu.make_async_copy(src.at[which], dst.at[which], store_sem.at[index, which])
+            for index, (src, dst) in enumerate(((held, x_out), (ha, ha_out), (hm, hm_out)))
+        ]
 
     def work(which):
         def norm(index, _):
@@ -430,52 +531,49 @@
             bias = vecs[lax.div(chunk, 3), pl.ds(8 + lax.rem(chunk, 3), 1), :]
             made = dot(ha[which], weight[:, pl.ds(kind * HEAD, HEAD)]) + bias
             if kind < 2:
-                low = rotate_low(made[:, :128], cos_ref[...], above_ref[...], below_ref[...])
+                low = rotate_low(
+                    made[:, :128], cos_ref[own_rows, :], above_ref[own_rows, :],
+                    below_ref[own_rows, :],
+                )
                 qkv[which, kind, :, pl.ds(0, 128)] = low.astype(BF16)
                 qkv[which, kind, :, pl.ds(128, HEAD - 128)] = made[:, 128:].astype(BF16)
             else:
                 qkv[which, kind] = made.astype(BF16)
         spread.start(which)
-        for start in range(0, hidden, 256):
-            span = pl.ds(start, 256)
-            up[which, :, span] = (
-                dot(hm[which], weight[:, pl.ds(3 * HEAD + start, 256)]) + upb_ref[:, span]
-            )
+        for copy in stores(which):
+            copy.start()
 
     for step, place in enumerate(near_first(line)):
 
         def one(other, _, step=step, place=place):
             @pl.when(other == 1)
             def _():
-                if step == 0:
-                    relay.start(3)
-                relay.wait_over(place)
+                if 0 < step < PAIRS - 1:
+                    relay.start(step + 1)
+                if step > 0:
+                    relay.pass_halves(step)
+                relay.wait_over(step, place)
 
             work(place * 2 + side + other * (1 - 2 * side))
 
         lax.fori_loop(0, 2, one, None)
 
-    for index, (src, dst) in enumerate(((held, x_out), (ha, ha_out), (hm, hm_out), (up, u_out))):
-        stores.append(pltpu.make_async_copy(src, dst, store_sem.at[2 + index]))
-        stores[-1].start()
     relay.finish()
     spread.finish()
+    columns.finish()
 
     def sent(step, _):
         target = lax.rem(rank + step, TEAM)
         vector_copy(rank, target, target).wait_send()
-        for copy in column_copies(rank, target, target):
-            copy.wait_send()
 
     lax.fori_loop(1, TEAM, sent, None)
 
-    def passed(origin, _):
-        to_core(origin).wait_send()
-        to_chip(origin).wait_send()
-        to_last(origin).wait_send()
-
-    lax.fori_loop(0, TEAM, passed, None)
-    for copy in stores:
+    def stored(which, _):
+        for copy in stores(which):
+            copy.wait()
+
+    lax.fori_loop(0, TEAM, stored, None)
+    for copy in last_stores:
         copy.wait()
 
 
@@ -485,16 +583,13 @@
 LIMIT = 60 << 20
 
 
-def first(x, w_qkv, w_up, vec, up_bias, tables):
+def first(x, w_qkv, vec, tables):
     tokens, width = x.shape
-    hidden = up_bias.shape[-1]
-    span = 3 * HEAD + hidden
     shapes = [
         ((TEAM, tokens, width), BF16),
         ((TEAM, tokens, width), BF16),
         ((TEAM, tokens, width), BF16),
-        ((TEAM, tokens, hidden), F32),
-        ((width, span), BF16),
+        ((width, 3 * HEAD), BF16),
         ((2, 3, QUARTERS * tokens, HEAD), BF16),
         ((2, QUARTERS, 8, tokens), F32),
         ((TEAM, VECTOR_ROWS, vec.shape[-1]), F32),
@@ -502,158 +597,36 @@
     return pl.pallas_call(
         first_kernel,
         out_shape=[jax.ShapeDtypeStruct(*shape) for shape in shapes],
-        in_specs=[VMEM, ANY, ANY, VMEM, VMEM, VMEM, VMEM, VMEM],
+        in_specs=[VMEM, ANY, VMEM, VMEM, VMEM, VMEM],
         out_specs=[ANY] * len(shapes),
         scratch_shapes=[
             pltpu.VMEM((TEAM, tokens, width), BF16),
-            pltpu.VMEM((width, span), BF16),
+            pltpu.VMEM((width, 3 * HEAD), BF16),
             pltpu.VMEM((TEAM, VECTOR_ROWS, vec.shape[-1]), F32),
             pltpu.VMEM((TEAM, tokens, width), BF16),
             pltpu.VMEM((TEAM, tokens, width), BF16),
-            pltpu.VMEM((TEAM, tokens, hidden), F32),
             pltpu.VMEM((TEAM, 3, tokens, HEAD), BF16),
             pltpu.VMEM((8, width), F32),
             DMA((2,)),
-            DMA((6,)),
-            DMA((4, TEAM)),
-            DMA((4, TEAM)),
-            DMA((4,)),
+            DMA((3, TEAM)),
+            DMA((2,)),
+            DMA((TEAM,)),
+            DMA((TEAM,)),
         ]
-        + [DMA((TEAM,))] * 8
         + spread_sems(2)
-        + RELAY_SEMS,
+        + RELAY_SEMS
+        + column_sems(3),
         compiler_params=pltpu.CompilerParams(
             collective_id=0, has_side_effects=True, vmem_limit_bytes=LIMIT
         ),
         name="gather_x",
-    )(x, w_qkv, w_up, vec, up_bias, *tables)
+    )(x, w_qkv, vec, *tables)
 
 
 def gelu_terms(values):
     chance = 0.5 * (1.0 + lax.erf(values * (0.5**0.5)))
     density = jnp.exp(-0.5 * values * values) * 0.3989422804014327
     return values * chance, chance + values * density
-
-
-def second_kernel(
-    dy_ref, wo_ref, wd_ref, u_ref, o_ref,
-    dy_out, a_out, du_out, do_out, o_out, sum_out,
-    held, up, act, grad, attended,
-    own_sem, load_sem, store_sem, back_send, back_recv, spread_send, spread_recv, spread_own,
-    *relay_sems,
-):
-    base, line, side, quarter = spot()
-    rank = line * 2 + side
-    tokens, width = dy_ref.shape
-    hidden = up.shape[-1]
-    relay = Relay(held, *relay_sems)
-    spread = Spread(
-        [
-            (
-                lambda s: attended.at[s],
-                lambda j, origin: do_out.at[j, pl.ds(origin * tokens, tokens), :],
-            )
-        ],
-        spread_send, spread_recv, spread_own,
-    )
-    loads = pltpu.make_async_copy(u_ref, up, load_sem)
-    loads.start()
-    greet_line(base, line, side, quarter)
-    own = pltpu.make_async_copy(dy_ref, held.at[rank], own_sem.at[0])
-    own.start()
-    own.wait()
-    relay.start(0)
-
-    def back(to, origin):
-        return send(
-            o_ref.at[:, pl.ds(to * tokens, tokens), :], o_out.at[pl.ds(2 * origin, 2)],
-            back_send.at[to], back_recv.at[origin], base + rank, to,
-        )
-
-    own_back = pltpu.make_async_copy(
-        o_ref.at[:, pl.ds(quarter * tokens, tokens), :], o_out.at[pl.ds(2 * quarter, 2)],
-        own_sem.at[1],
-    )
-    own_back.start()
-    for step in range(1, QUARTERS):
-        back(lax.rem(quarter + step, QUARTERS), quarter).start()
-    loads.wait()
-    sum_out[...] = jnp.zeros_like(sum_out)
-
-    def work(which):
-        attended[which] = contract_last(held[which], wo_ref[...]).astype(BF16)
-        spread.start(which)
-        for start in range(0, hidden, 256):
-            span = pl.ds(start, 256)
-            value, slope = gelu_terms(up[which, :, span])
-            act[which, :, span] = value.astype(BF16)
-            pulled = contract_last(held[which], wd_ref[span, :])
-            grad[which, :, span] = (pulled * slope).astype(BF16)
-        sum_out[0:1, :] += jnp.sum(held[which].astype(F32), 0, keepdims=True)
-
-    for step, place in enumerate(near_first(line)):
-
-        def one(other, _, step=step, place=place):
-            @pl.when(other == 1)
-            def _():
-                if step < PAIRS - 1:
-                    relay.start(step + 1)
-                relay.wait_over(place)
-
-            work(place * 2 + side + other * (1 - 2 * side))
-
-        lax.fori_loop(0, 2, one, None)
-
-    stores = []
-    for index, (src, dst) in enumerate(((held, dy_out), (act, a_out), (grad, du_out))):
-        stores.append(pltpu.make_async_copy(src, dst, store_sem.at[index]))
-        stores[-1].start()
-    relay.finish()
-    spread.finish()
-    for step in range(1, QUARTERS):
-        back(lax.rem(quarter + step, QUARTERS), quarter).wait_send()
-        origin = lax.rem(quarter + step, QUARTERS)
-        back(origin, origin).wait_recv()
-    own_back.wait()
-    for copy in stores:
-        copy.wait()
-
-
-def second(dy, w_out, w_down, up_values, attended):
-    tokens, width = dy.shape
-    hidden = up_values.shape[-1]
-    shapes = [
-        ((TEAM, tokens, width), BF16),
-        ((TEAM, tokens, hidden), BF16),
-        ((TEAM, tokens, hidden), BF16),
-        ((2, QUARTERS * tokens, HEAD), BF16),
-        ((TEAM, tokens, HEAD), BF16),
-        ((8, width), F32),
-    ]
-    return pl.pallas_call(
-        second_kernel,
-        out_shape=[jax.ShapeDtypeStruct(*shape) for shape in shapes],
-        in_specs=[VMEM, VMEM, VMEM, ANY, ANY],
-        out_specs=[ANY] * 5 + [VMEM],
-        scratch_shapes=[
-            pltpu.VMEM((TEAM, tokens, width), BF16),
-            pltpu.VMEM((TEAM, tokens, hidden), F32),
-            pltpu.VMEM((TEAM, tokens, hidden), BF16),
-            pltpu.VMEM((TEAM, tokens, hidden), BF16),
-            pltpu.VMEM((TEAM, tokens, HEAD), BF16),
-            DMA((2,)),
-            DMA,
-            DMA((3,)),
-            DMA((QUARTERS,)),
-            DMA((QUARTERS,)),
-        ]
-        + spread_sems(1)
-        + RELAY_SEMS,
-        compiler_params=pltpu.CompilerParams(
-            collective_id=1, has_side_effects=True, vmem_limit_bytes=LIMIT
-        ),
-        name="gather_dy",
-    )(dy, w_out, w_down, up_values, attended)
 
 
 def probabilities(start, block, q_ref, k_ref, col_ref, row_ref):
@@ -668,12 +641,189 @@
     return expanded / jnp.sum(expanded, -1, keepdims=True)
 
 
-def forward_kernel(block, qkv_ref, col_ref, row_ref, o_ref):
-    q_ref, k_ref, v_ref = (qkv_ref.at[kind] for kind in range(3))
-    for start in range(0, o_ref.shape[0], block):
-        probs = probabilities(start, block, q_ref, k_ref, col_ref, row_ref)
-        value_block = v_ref[pl.ds(0, start + block), :]
-        o_ref[pl.ds(start, block), :] = dot(probs.astype(BF16), value_block).astype(BF16)
+def second_kernel(
+    dy_ref, wo_ref, wd_ref, upb_ref, col_ref, row_ref, wu_ref, hm_ref, qkv_ref,
+    dy_out, a_out, du_out, do_out, o_out, w_out, sum_out,
+    held, hm, weight, qkv, mixed, act, grad, attended,
+    own_sem, load_sem, store_sem, w_store, back_send, back_recv,
+    spread_send, spread_recv, spread_own, *sems,
+):
+    base, line, side, quarter = spot()
+    rank = line * 2 + side
+    tokens, width = dy_ref.shape
+    hidden = act.shape[-1]
+    rows = wu_ref.shape[0]
+    part = rows // QUARTERS
+    relay = Relay(held, *sems[:6])
+    spread = Spread(
+        [
+            (
+                lambda s: attended.at[s],
+                lambda j, origin: do_out.at[j, pl.ds(origin * tokens, tokens), :],
+            )
+        ],
+        spread_send, spread_recv, spread_own,
+    )
+    columns = Columns(
+        lambda target: [
+            (
+                wu_ref.at[
+                    pl.ds(pl.multiple_of(quarter * part, 16), part),
+                    pl.ds(pl.multiple_of(target * hidden, hidden), hidden),
+                ],
+                0,
+                hidden,
+            )
+        ],
+        lambda source, slice_of, lane, lanes: weight.at[
+            pl.ds(pl.multiple_of(source * rows + slice_of * part, 16), part), pl.ds(lane, lanes)
+        ],
+        0, hidden, sems[6:15],
+    )
+    load_qkv = pltpu.make_async_copy(qkv_ref, qkv, load_sem.at[0])
+    load_hm = pltpu.make_async_copy(hm_ref, hm, load_sem.at[1])
+    load_qkv.start()
+    load_hm.start()
+    greet_team(base, line, side, quarter)
+    own = pltpu.make_async_copy(dy_ref, held.at[rank], own_sem.at[0])
+    own.start()
+    columns.start()
+    own.wait()
+    relay.start(0)
+
+    load_qkv.wait()
+    length = QUARTERS * tokens
+
+    def attend(sequence, _):
+        q, k, v = (qkv.at[sequence, kind] for kind in range(3))
+        for start in range(0, length, tokens):
+            probs = probabilities(
+                start, tokens, q, k, col_ref.at[sequence], row_ref.at[sequence]
+            )
+            value_block = v[pl.ds(0, start + tokens), :]
+            mixed[sequence, pl.ds(start, tokens), :] = dot(
+                probs.astype(BF16), value_block
+            ).astype(BF16)
+
+    lax.fori_loop(0, 2, attend, None)
+
+    def back(to, origin):
+        return send(
+            mixed.at[:, pl.ds(to * tokens, tokens), :], o_out.at[pl.ds(2 * origin, 2)],
+            back_send.at[to], back_recv.at[origin], base + rank, to,
+        )
+
+    own_back = pltpu.make_async_copy(
+        mixed.at[:, pl.ds(quarter * tokens, tokens), :], o_out.at[pl.ds(2 * quarter, 2)],
+        own_sem.at[1],
+    )
+    own_back.start()
+    for step in range(1, QUARTERS):
+        to = lax.rem(quarter + step, QUARTERS)
+        back(to, quarter).start()
+    columns.forward()
+    sum_out[...] = jnp.zeros_like(sum_out)
+    relay.start_halves()
+    relay.start(1)
+    columns.forward_last()
+    columns.arrive()
+    store_weight = pltpu.make_async_copy(weight, w_out, w_store)
+    store_weight.start()
+    load_hm.wait()
+
+    def stores(which):
+        return [
+            pltpu.make_async_copy(src.at[which], dst.at[which], store_sem.at[index, which])
+            for index, (src, dst) in enumerate(((held, dy_out), (act, a_out), (grad, du_out)))
+        ]
+
+    def work(which):
+        attended[which] = contract_last(held[which], wo_ref[...]).astype(BF16)
+        spread.start(which)
+        for start in range(0, hidden, 256):
+            span = pl.ds(start, 256)
+            up = dot(hm[which], weight[:, span]) + upb_ref[:, span]
+            value, slope = gelu_terms(up)
+            act[which, :, span] = value.astype(BF16)
+            pulled = contract_last(held[which], wd_ref[span, :])
+            grad[which, :, span] = (pulled * slope).astype(BF16)
+        for copy in stores(which):
+            copy.start()
+        sum_out[0:1, :] += jnp.sum(held[which].astype(F32), 0, keepdims=True)
+
+    for step, place in enumerate(near_first(line)):
+
+        def one(other, _, step=step, place=place):
+            @pl.when(other == 1)
+            def _():
+                if 0 < step < PAIRS - 1:
+                    relay.start(step + 1)
+                if step > 0:
+                    relay.pass_halves(step)
+                relay.wait_over(step, place)
+
+            work(place * 2 + side + other * (1 - 2 * side))
+
+        lax.fori_loop(0, 2, one, None)
+
+    relay.finish()
+    spread.finish()
+    columns.finish()
+    for step in range(1, QUARTERS):
+        other = lax.rem(quarter + step, QUARTERS)
+        back(other, quarter).wait_send()
+        back(other, other).wait_recv()
+    own_back.wait()
+    store_weight.wait()
+
+    def stored(which, _):
+        for copy in stores(which):
+            copy.wait()
+
+    lax.fori_loop(0, TEAM, stored, None)
+
+
+def second(dy, w_out, w_down, up_bias, column, row, w_up, mlp_input, qkv):
+    tokens, width = dy.shape
+    hidden = up_bias.shape[-1]
+    shapes = [
+        ((TEAM, tokens, width), BF16),
+        ((TEAM, tokens, hidden), BF16),
+        ((TEAM, tokens, hidden), BF16),
+        ((2, QUARTERS * tokens, HEAD), BF16),
+        ((TEAM, tokens, HEAD), BF16),
+        ((width, hidden), BF16),
+        ((8, width), F32),
+    ]
+    return pl.pallas_call(
+        second_kernel,
+        out_shape=[jax.ShapeDtypeStruct(*shape) for shape in shapes],
+        in_specs=[VMEM] * 6 + [ANY] * 3,
+        out_specs=[ANY] * 6 + [VMEM],
+        scratch_shapes=[
+            pltpu.VMEM((TEAM, tokens, width), BF16),
+            pltpu.VMEM((TEAM, tokens, width), BF16),
+            pltpu.VMEM((width, hidden), BF16),
+            pltpu.VMEM(qkv.shape, BF16),
+            pltpu.VMEM((2, QUARTERS * tokens, HEAD), BF16),
+            pltpu.VMEM((TEAM, tokens, hidden), BF16),
+            pltpu.VMEM((TEAM, tokens, hidden), BF16),
+            pltpu.VMEM((TEAM, tokens, HEAD), BF16),
+            DMA((2,)),
+            DMA((2,)),
+            DMA((3, TEAM)),
+            DMA,
+            DMA((QUARTERS,)),
+            DMA((QUARTERS,)),
+        ]
+        + spread_sems(1)
+        + RELAY_SEMS
+        + column_sems(1),
+        compiler_params=pltpu.CompilerParams(
+            collective_id=1, has_side_effects=True, vmem_limit_bytes=LIMIT
+        ),
+        name="gather_dy",
+    )(dy, w_out, w_down, up_bias, column, row, w_up, mlp_input, qkv)
 
 
 def backward_kernel(
@@ -716,20 +866,6 @@
     return three, one, masks
 
 
-def attend(qkv, column, row):
-    seqs, _, length, head = qkv.shape
-    three, one, masks = attention_specs(seqs, length)
-    return pl.pallas_call(
-        partial(forward_kernel, min(256, length)),
-        grid=(seqs,),
-        in_specs=[three] + masks,
-        out_specs=one,
-        out_shape=jax.ShapeDtypeStruct((seqs, length, head), BF16),
-        compiler_params=pltpu.CompilerParams(vmem_limit_bytes=48 << 20),
-        name="attend",
-    )(qkv, column, row)
-
-
 def attend_back(qkv, grads, column, row, tables):
     seqs, _, length, head = qkv.shape
     three, one, masks = attention_specs(seqs, length)
@@ -928,9 +1064,9 @@
 
 
 def third_kernel(
-    x_ref, o_ref, a_ref, wo_ref, wd_ref, bias_ref, du_ref, d_ref, hm_ref, dy_ref,
+    x_ref, o_ref, a_ref, wo_ref, wd_ref, vec_ref, du_ref, d_ref, hm_ref, dy_ref,
     result_ref, back_out, up_out, rows_out,
-    own_sem, back_send, back_recv, load_sem, store_sem, hm_tiles, tile_sum, dy, *rest,
+    own_sem, back_send, back_recv, load_sem, store_sem, hm_tiles, tile_sum, dy, bias, *rest,
 ):
     base, line, side, quarter = spot()
     rank = line * 2 + side
@@ -1028,12 +1164,15 @@
         return pltpu.make_async_copy(downs.total(tile), rows_out.at[rows, :], store_sem.at[1])
 
     ups.over_chips(lambda tile: store_up(tile).start())
+    block = width // TEAM
+    for source in range(TEAM):
+        bias[0:1, pl.ds(source * block, block)] = vec_ref[source, 4:5, :] + vec_ref[source, 5:6, :]
     reduce.last()
     strip = 64
 
     def close(index, _):
         chunk = pl.ds(pl.multiple_of(index * strip, strip), strip)
-        total = reduce.total(chunk) + bias_ref[0:1, :]
+        total = reduce.total(chunk) + bias[0:1, :]
         result_ref[chunk, :] = (x_ref[chunk, :].astype(F32) + total).astype(BF16)
 
     lax.fori_loop(0, tokens // strip, close, None)
@@ -1051,7 +1190,7 @@
     lax.fori_loop(0, downs.tiles, lambda tile, _: store_down(tile).wait(), None)
 
 
-def third(x, attended, activated, w_out, w_down, bias, grad_up, grads, mlp_input, grad_rows):
+def third(x, attended, activated, w_out, w_down, vectors, grad_up, grads, mlp_input, grad_rows):
     tokens, width = x.shape
     hidden = activated.shape[-1]
     part, share = width // TEAM // QUARTERS, width // QUARTERS
@@ -1076,6 +1215,7 @@
             pltpu.VMEM((2, TEAM * tokens, width // TEAM), BF16),
             pltpu.VMEM((width // TEAM, hidden), F32),
             pltpu.VMEM((TEAM * tokens, width), BF16),
+            pltpu.VMEM((8, width), F32),
         ]
         + reduce_scratch(tokens, width, 1, F32)
         + quarters_scratch(TEAM, part, hidden)
@@ -1084,110 +1224,13 @@
             collective_id=2, has_side_effects=True, vmem_limit_bytes=LIMIT
         ),
         name="scatter_result",
-    )(x, attended, activated, w_out, w_down, bias, grad_up, grads, mlp_input, grad_rows)
-
-
-class Columns:
-    def __init__(self, kind, source_of, landed, start, size, sems):
-        self.kind, self.source_of, self.landed = kind, source_of, landed
-        self.start_lane, self.size, self.sems = start, size, sems
-        self.base, line, side, self.quarter = spot()
-        self.rank = line * 2 + side
-        self.part = landed.shape[1] // QUARTERS
-
-    def region(self, source, slice_of):
-        rows = pl.ds(pl.multiple_of(slice_of * self.part, 16), self.part)
-        return self.landed.at[source, rows, pl.ds(self.start_lane, self.size)]
-
-    def deal(self, source, target, peer):
-        sends, recvs = self.sems[:2]
-        return send(
-            self.source_of(target), self.region(source, self.quarter),
-            sends.at[self.kind, target], recvs.at[self.kind, source],
-            self.base + peer, self.quarter,
-        )
-
-    def own(self):
-        return pltpu.make_async_copy(
-            self.source_of(self.rank), self.region(self.rank, self.quarter),
-            self.sems[8].at[self.kind],
-        )
-
-    def start(self):
-        self.own().start()
-
-        def one(step, _):
-            target = lax.rem(self.rank + step, TEAM)
-            self.deal(self.rank, target, target).start()
-
-        lax.fori_loop(1, TEAM, one, None)
-
-    def pass_on(self, which, source, slice_of, to):
-        block = self.region(source, slice_of)
-        sends, recvs = self.sems[2 + 2 * which : 4 + 2 * which]
-        return send(
-            block, block, sends.at[self.kind, source], recvs.at[self.kind, source],
-            self.base + self.rank, to,
-        )
-
-    def to_core(self, source):
-        return self.pass_on(0, source, self.quarter, core_peer(self.quarter))
-
-    def to_chip(self, source):
-        return self.pass_on(1, source, self.quarter, chip_peer(self.quarter))
-
-    def to_last(self, source):
-        return self.pass_on(2, source, chip_peer(self.quarter), core_peer(self.quarter))
-
-    def forward(self):
-        self.own().wait()
-        self.to_chip(self.rank).start()
-        self.to_core(self.rank).start()
-
-        def one(step, _):
-            source = lax.rem(self.rank + TEAM - step, TEAM)
-            self.deal(source, self.rank, source).wait_recv()
-            self.to_chip(source).start()
-            self.to_core(source).start()
-
-        lax.fori_loop(1, TEAM, one, None)
-
-    def forward_last(self):
-        def one(step, _):
-            source = lax.rem(self.rank + TEAM - step, TEAM)
-            self.pass_on(
-                1, source, chip_peer(self.quarter), chip_peer(self.quarter)
-            ).wait_recv()
-            self.to_last(source).start()
-
-        lax.fori_loop(0, TEAM, one, None)
-
-    def finish(self):
-        core = core_peer(self.quarter)
-
-        def one(source, _):
-            self.pass_on(0, source, core, core).wait_recv()
-            self.pass_on(2, source, chip_peer(core), core).wait_recv()
-            self.to_core(source).wait_send()
-            self.to_chip(source).wait_send()
-            self.to_last(source).wait_send()
-
-        lax.fori_loop(0, TEAM, one, None)
-
-        def sent(step, _):
-            target = lax.rem(self.rank + step, TEAM)
-            self.deal(self.rank, target, target).wait_send()
-
-        lax.fori_loop(1, TEAM, sent, None)
-
-
-COLUMN_SEMS = [DMA((2, TEAM))] * 8 + [DMA((2,))]
+    )(x, attended, activated, w_out, w_down, vectors, grad_up, grads, mlp_input, grad_rows)
 
 
 def fourth_kernel(
-    x_ref, dy_ref, dqkv_ref, du_ref, vec_ref, dy_sum_ref, xs_ref, w_ref, ha_ref, up_ref, rows_ref,
+    x_ref, dy_ref, dqkv_ref, du_ref, vec_ref, dy_sum_ref, xs_ref, wq_ref, wu_ref, ha_ref, up_ref, rows_ref,
     grad_ref, landed, rows_out, vector_ref,
-    weight, xs, load_sem, tile_load, ha_tiles, tile_sum, sums, packets, packets_in, ring, ring_in,
+    wq, wu, xs, gains, load_sem, tile_load, ha_tiles, tile_sum, sums, packets, packets_in, ring, ring_in,
     row_own, row_send, row_recv, pack_send, pack_recv, ring_send, ring_recv, *rest,
 ):
     base, line, side, quarter = spot()
@@ -1199,13 +1242,22 @@
     core, chip = core_peer(quarter), chip_peer(quarter)
     reduce = Reduce(*rest[:4], rest[4:8])
     qkvs = Quarters(*rest[8:16])
-    sems = rest[16:25]
-    up_columns = Columns(0, lambda n: up_ref.at[n], landed, 3 * HEAD, hidden, sems)
-    qkv_columns = Columns(1, lambda n: qkvs.total(n), landed, 0, 3 * HEAD, sems)
+
+    def place(source, slice_of, lane, lanes):
+        rows = pl.ds(pl.multiple_of(slice_of * part, 16), part)
+        return landed.at[source, rows, pl.ds(lane, lanes)]
+
+    up_columns = Columns(
+        lambda n: [(up_ref.at[n], 3 * HEAD, hidden)], place, 3 * HEAD, hidden, rest[16:25]
+    )
+    qkv_columns = Columns(
+        lambda n: [(qkvs.total(n), 0, 3 * HEAD)], place, 0, 3 * HEAD, rest[25:34]
+    )
     stream = Stream(ha_ref, ha_tiles, tile_load)
     loads = [
-        pltpu.make_async_copy(w_ref, weight, load_sem.at[0]),
-        pltpu.make_async_copy(xs_ref, xs, load_sem.at[1]),
+        pltpu.make_async_copy(wq_ref, wq, load_sem.at[0]),
+        pltpu.make_async_copy(wu_ref, wu, load_sem.at[1]),
+        pltpu.make_async_copy(xs_ref, xs, load_sem.at[2]),
     ]
     for copy in loads:
         copy.start()
@@ -1225,6 +1277,8 @@
     rows_copy(1, quarter, chip).start()
     up_columns.start()
     sums[...] = jnp.zeros_like(sums)
+    for source in range(TEAM):
+        gains[0:2, pl.ds(source * block, block)] = vec_ref[source, 0:2, :]
     for copy in loads:
         copy.wait()
 
@@ -1236,14 +1290,14 @@
         inverse = lax.rsqrt(variance + EPSILON)
         for start in range(0, width, 512):
             span = pl.ds(start, 512)
-            attn = contract_last(dqkv_ref[rows, :], weight[span, : 3 * HEAD])
-            mlp = contract_last(du_ref[rows, :], weight[span, 3 * HEAD :])
+            attn = contract_last(dqkv_ref[rows, :], wq[span, :])
+            mlp = contract_last(du_ref[rows, :], wu[span, :])
             unit = (xs[which, :, span].astype(F32) - average) * inverse
             sums[0:1, span] += jnp.sum(attn * unit, 0, keepdims=True)
             sums[1:2, span] += jnp.sum(mlp * unit, 0, keepdims=True)
             sums[2:3, span] += jnp.sum(attn, 0, keepdims=True)
             sums[3:4, span] += jnp.sum(mlp, 0, keepdims=True)
-            put(span, attn * vec_ref[0:1, span] + mlp * vec_ref[1:2, span])
+            put(span, attn * gains[0:1, span] + mlp * gains[1:2, span])
         sums[4:5, pl.ds(0, hidden)] += jnp.sum(du_ref[rows, :].astype(F32), 0, keepdims=True)
         sums[5:6, pl.ds(0, 3 * HEAD)] += jnp.sum(
             dqkv_ref[rows, :].astype(F32), 0, keepdims=True
@@ -1359,8 +1413,9 @@
     rows_copy(0, quarter, core).wait_send()
     rows_copy(1, quarter, chip).wait_send()
     rows_copy(2, chip, core).wait_send()
-    up_columns.finish()
-    qkv_columns.finish()
+    for columns in (up_columns, qkv_columns):
+        columns.arrive()
+        columns.finish()
 
     def sent_packets(step, _):
         target = lax.rem(rank + step, TEAM)
@@ -1373,7 +1428,7 @@
 
 
 def fourth(
-    x, dy, grad_qkv, grad_up, gains, dy_sum, everyone, weight, attn_input, up_sums, row_sums
+    x, dy, grad_qkv, grad_up, vectors, dy_sum, everyone, w_qkv, w_up, attn_input, up_sums, row_sums
 ):
     tokens, width = x.shape
     hidden = grad_up.shape[-1]
@@ -1387,12 +1442,14 @@
     return pl.pallas_call(
         fourth_kernel,
         out_shape=[jax.ShapeDtypeStruct(*shape) for shape in shapes],
-        in_specs=[VMEM] * 6 + [ANY] * 5,
+        in_specs=[VMEM] * 6 + [ANY] * 6,
         out_specs=[VMEM, ANY, ANY, VMEM],
         scratch_shapes=[
-            pltpu.VMEM(weight.shape, BF16),
+            pltpu.VMEM(w_qkv.shape, BF16),
+            pltpu.VMEM(w_up.shape, BF16),
             pltpu.VMEM(everyone.shape, BF16),
-            DMA((2,)),
+            pltpu.VMEM((8, width), F32),
+            DMA((3,)),
             DMA((2,)),
             pltpu.VMEM((2, TEAM * tokens, block), BF16),
             pltpu.VMEM((block, 3 * HEAD), F32),
@@ -1411,12 +1468,15 @@
         ]
         + reduce_scratch(tokens, width, PAIRS, BF16)
         + quarters_scratch(TEAM, part, 3 * HEAD)
-        + COLUMN_SEMS,
+        + column_sems(1) * 2,
         compiler_params=pltpu.CompilerParams(
             collective_id=3, has_side_effects=True, vmem_limit_bytes=LIMIT
         ),
         name="scatter_grad",
-    )(x, dy, grad_qkv, grad_up, gains, dy_sum, everyone, weight, attn_input, up_sums, row_sums)
+    )(
+        x, dy, grad_qkv, grad_up, vectors, dy_sum, everyone, w_qkv, w_up, attn_input, up_sums,
+        row_sums,
+    )
 
 
 def settle_kernel(
@@ -1618,18 +1678,14 @@
     mine_team = team_order(mine)
     positions = jnp.arange(ctx * tokens, dtype=jnp.int32)
     tables = rotary_tables(positions.astype(F32))
-    own_tables = [
-        lax.dynamic_slice_in_dim(table, lax.axis_index("ctx") * tokens, tokens, 0)
-        for table in tables
-    ]
-    everyone, attn_input, mlp_input, up_values, weight, qkv, marks, vectors = first(
-        mine_team, w_qkv, w_up, packet, b_up.astype(F32).reshape(1, hidden), own_tables
+    everyone, attn_input, mlp_input, w_head, qkv, marks, vectors = first(
+        mine_team, w_qkv, packet, tables
     )
     marks = marks[:, :, 0, :].reshape(2, ctx * tokens)
     column, row = marks[:, :, None], marks[:, None, :]
-    attended = attend(qkv, column, row)
-    grad_rows, activated, grad_up, grad_attended, attended, dy_sum = second(
-        grad_mine, w_out, w_down, up_values, attended
+    grad_rows, activated, grad_up, grad_attended, attended, w_units, dy_sum = second(
+        grad_mine, w_out, w_down, b_up.astype(F32).reshape(1, hidden), column, row, w_up, mlp_input,
+        qkv,
     )
     grads = attend_back(qkv, grad_attended, column, row, tables)
     flat = (TEAM * tokens, -1)
@@ -1637,14 +1693,12 @@
         values.reshape(flat)
         for values in (attn_input, mlp_input, grad_rows, activated, grad_up, attended)
     )
-    branch_bias = (vectors[:, 4] + vectors[:, 5]).reshape(1, width)
     result, grad_qkv, up_sums, row_sums = third(
-        mine, attended, activated, w_out, w_down, branch_bias, grad_up, grads, mlp_input, grad_rows
-    )
-    gains = vectors[:, :2].transpose(1, 0, 2).reshape(2, width)
+        mine, attended, activated, w_out, w_down, vectors, grad_up, grads, mlp_input, grad_rows
+    )
     grad_inputs, columns, row_sums, vector = fourth(
-        mine_team, team_order(grad_mine), grad_qkv.reshape(flat), grad_up, gains, dy_sum, everyone,
-        weight, attn_input, up_sums, row_sums,
+        mine_team, team_order(grad_mine), grad_qkv.reshape(flat), grad_up, vectors, dy_sum, everyone,
+        w_head, w_units, attn_input, up_sums, row_sums,
     )
     grad_inputs = plain_order(grad_inputs)
     if teams == 1:

time: 591 us -> 548 us (0.927)
  Pallas kernels: 559 us -> 523 us
    pallas_call x1, Pallas kernels: 153 us -> 105 us  [first(): pl.pallas_call(first_kernel, out_shape=[jax.ShapeDtypeStruct(*shape) for...]
    pallas_call x1, Pallas kernels: 121 us -> 132 us  [third(): pl.pallas_call(third_kernel, out_shape=[jax.ShapeDtypeStruct(shape, BF16)...]
where the time goes in v4:
time: 548 us; the launch traced here: 544 us
  Pallas kernels  523 us (95%)
  local copies, waits for them, and re-layouts  14.5 us (3%)
    pallas_call x1, Pallas kernels, fourth(): pl.pallas_call(fourth_kernel, out_shape=[jax.ShapeDtypeStruct(*shape) for...  146 us
    pallas_call x1, Pallas kernels, third(): pl.pallas_call(third_kernel, out_shape=[jax.ShapeDtypeStruct(shape, BF16)...  132 us
    pallas_call x1, Pallas kernels, second(): pl.pallas_call(second_kernel, out_shape=[jax.ShapeDtypeStruct(*shape) for...  114 us
    pallas_call x1, Pallas kernels, first(): pl.pallas_call(first_kernel, out_shape=[jax.ShapeDtypeStruct(*shape) for...  105 us
    pallas_call x1, Pallas kernels, settle(): pl.pallas_call(settle_kernel, out_shape=[jax.ShapeDtypeStruct(*shape) for...  15.2 us

profile of v4, /device:TPU:19, one launch (start us, length us, event | category | flops | bytes accessed | tf_op | source)
XLA Modules:
  0.0 544.4 jit_solution(2736781122412262473)
XLA Ops:
  0.7 0.1 pad.5.clone
  0.7 0.1 pad.8.clone
  0.8 0.7 convert_element_type.43
  1.5 0.7 stack.9
  2.2 0.7 stack.10
  2.8 0.7 reshape.106
  3.5 1.3 reshape.103
  4.8 2.5 concatenate.12.vec_ref
  7.3 1.9 multiply_sine_fusion
  9.3 1.6 maximum_maximum_fusion.2
  10.9 105.3 %gather_x.1 = (bf16[8,256,2048]{2,1,0:T(8,128)(2,1)}, bf16[8,256,2048]{2,1,0:T(8,128)(2,1)}, bf16[8,256,2048]{2,1,0:T(8,128)(2,1)}, bf16[2048,768]{1,0:T(8,128)(...) custom-call(bf16[256,2048]{1,0:T(8,128)(2,1)} %bitcast.23, ...), custom_call_target="tpu_custom_call" | custom-call | tf_op jit(solution)/shard_map/gather_x/pallas_call | solution.py:597
  116.2 1.4 fusion.1
  117.7 1.9 broadcast_in_dim_reshape_squeeze.8.col_ref
  119.5 0.0 copy-start
  119.5 0.0 copy-start.1
  119.5 0.0 copy-start.2
  119.5 0.0 copy-start.3
  119.5 0.0 copy-start.5
  119.5 114.3 %gather_dy.1 = (bf16[8,256,2048]{2,1,0:T(8,128)(2,1)}, bf16[8,256,1024]{2,1,0:T(8,128)(2,1)}, bf16[8,256,1024]{2,1,0:T(8,128)(2,1)}, bf16[2,1024,256]{2,1,0:T(8,...) custom-call(bf16[256,2048]{1,0:T(8,128)(2,1)} %bitcast.29, ...), custom_call_target="tpu_custom_call" | custom-call | tf_op jit(solution)/shard_map/gather_dy/pallas_call | solution.py:798
  233.8 0.0 copy-done
  233.8 0.0 copy-done.1
  233.9 0.0 copy-done.2
  233.9 0.0 copy-done.3
  233.9 0.0 copy-done.5
  233.9 0.0 copy-start.4
  233.9 1.2 copy-done.4
  235.1 10.7 %attend_back.1.d_ref = bf16[2,3,1024,256]{3,2,1,0:T(8,128)(2,1)} custom-call(bf16[2,3,1024,256]{3,2,1,0:T(8,128)(2,1)} %get-tuple-element.42.qkv_ref, bf16[2,1024,256]{2,1,0:T(8,128)(2,1)S(1)} %copy-done.4, f32[2,1024,1]{2,1,0:T(8,128)S(1)} %copy-done, f32[2,1,1024]{2,1,0:T(1,128)S(1)} %bitcast.19, f32[1024,128]{1,0:T(8,128)S(1)} %copy-done.3, ...), custom_call_target="tpu_custom_call" | custom-call | tf_op jit(solution)/shard_map/attend_back/pallas_call | solution.py:873
  245.8 132.1 %scatter_result.1 = (bf16[256,2048]{1,0:T(8,128)(2,1)}, bf16[8,256,768]{2,1,0:T(8,128)(2,1)}, bf16[8,64,1024]{2,1,0:T(8,128)(2,1)}, bf16[1280,512]{1,0:T(8,128)(2,1)}) custom-call(bf16[256,2048]{1,0:T(8,128)(2,1)} %bitcast.24, bf16[2048,256]{1,0:T(8,128)(2,1)} %bitcast.32, bf16[2048,1024]{1,0:T(8,128)(2,1)} %bitcast.28, bf16[256,2048]{1,0:T(8,128)(2,1)} %wo_ref.3, ...), custom_call_target="tpu_custom_call" | custom-call | tf_op jit(solution)/shard_map/scatter_result/pallas_call | solution.py:1204
  378.0 145.9 %scatter_grad.1 = (bf16[256,2048]{1,0:T(8,128)(2,1)}, bf16[8,256,1792]{2,1,0:T(8,128)(2,1)}, bf16[4,1280,512]{2,1,0:T(8,128)(2,1)}, f32[16,256]{1,0:T(8,128)}) custom-call(bf16[256,2048]{1,0:T(8,128)(2,1)} %bitcast.25, bf16[256,2048]{1,0:T(8,128)(2,1)} %bitcast.30, bf16[2048,768]{1,0:T(8,128)(2,1)} %bitcast.31, bf16[2048,1024]{1,0:T(8,128)(2,1)} %bitcast.22, ...), custom_call_target="tpu_custom_call" | custom-call | tf_op jit(solution)/shard_map/scatter_grad/pallas_call | solution.py:1442
  523.8 0.7 slice.22
  524.5 0.0 copy-start.6
  524.5 0.7 slice.21
  525.2 0.6 reshape.101
  525.8 0.7 slice_bitcast_fusion
  526.5 1.4 fusion.2
  527.9 0.6 copy.27
  528.5 15.2 %settle.1 = (f32[256,6144]{1,0:T(8,128)}, f32[256,8192]{1,0:T(8,128)}, f32[1024,2048]{1,0:T(8,128)}, f32[256,2048]{1,0:T(8,128)}, bf16[256,2048]{1,0:T(8,128)(2,1)}, /*index=5*/bf16[256,2048]{1,0:T(8,128)(2,1)}) custom-call(bf16[8,256,1792]{2,1,0:T(8,128)(2,1)} %get-tuple-element.57.columns_ref, bf16[4,1280,512]{2,1,0:T(8,128)(2,1)} %get-tuple-element.58.rows_ref, ...), custom_call_target="tpu_custom_call" | custom-call | tf_op jit(solution)/shard_map/settle/pallas_call | solution.py:1586
  543.6 0.0 copy-done.6
  543.6 0.6 copy.29
  (9 shorter events, 0.1 us)
Async XLA Ops:
  119.5 114.3 %copy-start = (f32[2,1024,1]{2,1,0:T(8,128)S(1)}, f32[2,1024,1]{2,1,0:T(8,128)}, u32[]{:S(2)}) copy-start(f32[2,1024,1]{2,1,0:T(8,128)} %broadcast_in_dim_reshape_squeeze.8.col_ref) | copy-start | bytes 24580
  119.5 114.3 %copy-start.1 = (f32[1024,128]{1,0:T(8,128)S(1)}, f32[1024,128]{1,0:T(8,128)}, u32[]{:S(2)}) copy-start(f32[1024,128]{1,0:T(8,128)} %get-tuple-element.68.below_ref) | copy-start | bytes 1572868
  119.5 114.3 %copy-start.2 = (f32[1024,128]{1,0:T(8,128)S(1)}, f32[1024,128]{1,0:T(8,128)}, u32[]{:S(2)}) copy-start(f32[1024,128]{1,0:T(8,128)} %get-tuple-element.69.above_ref) | copy-start | bytes 1572868
  119.5 114.3 %copy-start.3 = (f32[1024,128]{1,0:T(8,128)S(1)}, f32[1024,128]{1,0:T(8,128)}, u32[]{:S(2)}) copy-start(f32[1024,128]{1,0:T(8,128)} %get-tuple-element.77.cos_ref) | copy-start | bytes 1572868
  119.5 114.3 %copy-start.5 = (f32[2,4,1,256]{3,2,1,0:T(1,128)S(1)}, f32[2,4,1,256]{3,2,1,0:T(1,128)}, u32[]{:S(2)}) copy-start(f32[2,4,1,256]{3,2,1,0:T(1,128)} %get-tuple-element.70) | copy-start | bytes 24580
  233.9 1.2 copy-start.4
  524.5 19.1 %copy-start.6 = (f32[1,256]{1,0:T(1,128)}, f32[1,256]{1,0:T(1,128)S(1)}, u32[]{:S(2)}) copy-start(f32[1,256]{1,0:T(1,128)S(1)} %slice.22) | copy-start | bytes 3076

commit v5 on v4

--- a/solution.py
+++ b/solution.py
@@ -115,7 +115,7 @@
         self.held = held
         self.sems = line_send, line_recv, side_send, side_recv, half_send, half_recv
         self.base, self.line, self.side, self.quarter = spot()
-        self.half = held.shape[1] // 2
+        self.half = held.shape[1] * 3 // 8
 
     def neighbour(self, way):
         return self.base + self.line * 2 + self.side + (2 if way == RIGHT else -2)
@@ -138,7 +138,7 @@
     def over(self, source, side, low):
         block = self.held.at[source * 2 + side]
         if low:
-            block = self.held.at[source * 2 + side, pl.ds(self.half, self.half)]
+            block = self.held.at[source * 2 + side, pl.ds(self.half, self.held.shape[1] - self.half)]
         place = self.base + self.line * 2 + 1 - self.side
         return send(
             block, block, self.sems[2].at[source], self.sems[3].at[source], place, self.quarter
@@ -255,61 +255,66 @@
     )
 
 
+def reader(sequence):
+    return 2 * lax.rem(sequence, 2) + lax.rem(lax.div(sequence, 2), 2)
+
+
+def reader_slot(sequence):
+    return lax.div(sequence, QUARTERS)
+
+
+def among(quarter):
+    return 2 * lax.rem(quarter, 2) + lax.div(quarter, 2)
+
+
 class Spread:
     def __init__(self, pieces, send_sem, recv_sem, own_sem):
         self.pieces, self.sems = pieces, (send_sem, recv_sem, own_sem)
         base, line, side, self.quarter = spot()
         self.place = base + line * 2 + side
 
-    def _remote(self, index, sequence, to, origin):
+    def _remote(self, index, sequence, slot, to, origin):
         src, dst = self.pieces[index]
         send_sem, recv_sem, _ = self.sems
         return send(
-            src(sequence), dst(lax.rem(sequence, 2), origin), send_sem.at[index, sequence],
-            recv_sem.at[index, origin, lax.rem(sequence, 2)], self.place, to,
+            src(sequence), dst(slot, origin), send_sem.at[index, sequence],
+            recv_sem.at[index, origin, slot], self.place, to,
         )
 
     def _own(self, index, sequence):
         src, dst = self.pieces[index]
+        slot = reader_slot(sequence)
         return pltpu.make_async_copy(
-            src(sequence), dst(lax.rem(sequence, 2), self.quarter),
-            self.sems[2].at[index, lax.rem(sequence, 2)],
-        )
-
-    def start(self, sequence):
-        to = lax.div(sequence, 2)
+            src(sequence), dst(slot, self.quarter), self.sems[2].at[index, slot]
+        )
+
+    def each(self, sequence, own, other):
+        to, slot = reader(sequence), reader_slot(sequence)
 
         @pl.when(to == self.quarter)
         def _():
             for index in range(len(self.pieces)):
-                self._own(index, sequence).start()
+                own(self._own(index, sequence))
 
         @pl.when(to != self.quarter)
         def _():
             for index in range(len(self.pieces)):
-                self._remote(index, sequence, to, self.quarter).start()
+                other(self._remote(index, sequence, slot, to, self.quarter))
+
+    def start(self, sequence):
+        self.each(sequence, lambda copy: copy.start(), lambda copy: copy.start())
 
     def finish(self):
         def sent(sequence, _):
-            to = lax.div(sequence, 2)
-
-            @pl.when(to == self.quarter)
-            def _():
-                for index in range(len(self.pieces)):
-                    self._own(index, sequence).wait()
-
-            @pl.when(to != self.quarter)
-            def _():
-                for index in range(len(self.pieces)):
-                    self._remote(index, sequence, to, self.quarter).wait_send()
+            self.each(sequence, lambda copy: copy.wait(), lambda copy: copy.wait_send())
 
         lax.fori_loop(0, TEAM, sent, None)
 
         def landed(step, _):
             origin = lax.rem(self.quarter + 1 + lax.div(step, 2), QUARTERS)
-            sequence = lax.rem(step, 2)
+            slot = lax.rem(step, 2)
             for index in range(len(self.pieces)):
-                self._remote(index, sequence, origin, origin).wait_recv()
+                self._remote(index, 0, slot, origin, origin).wait_recv()
 
         lax.fori_loop(0, 2 * (QUARTERS - 1), landed, None)
 
@@ -428,280 +433,235 @@
     return [dma((count, TEAM))] * 2 + [dma((count,))] + [dma((TEAM,))] * 6
 
 
-def first_kernel(
-    x_ref, wq_ref, vec_ref, cos_ref, above_ref, below_ref,
-    x_out, ha_out, hm_out, w_out, qkv_out, seg_out, vec_out,
-    held, weight, vecs, ha, hm, qkv, vectors,
-    own_sem, store_sem, last_store, v_send, v_recv, spread_send, spread_recv, spread_own, *sems,
+def same_document(query_marks, key_marks):
+    def one_hot(marks):
+        number = lax.broadcasted_iota(jnp.int32, marks.shape, 0).astype(F32)
+        return jnp.where(marks == number, 1.0, 0.0).astype(BF16)
+
+    return contract_first(one_hot(query_marks), one_hot(key_marks)) > 0.5
+
+
+def probabilities(block, size, q_ref, k_ref, marks_ref):
+    start = block * size
+    rows, keys = pl.ds(start, size), pl.ds(0, start + size)
+    scores = contract_last(q_ref[rows, :], k_ref[keys, :]) * HEAD ** (-0.5)
+    shape = scores.shape
+    query_pos = start + lax.broadcasted_iota(jnp.int32, shape, 0)
+    key_pos = lax.broadcasted_iota(jnp.int32, shape, 1)
+    key_marks = jnp.concatenate([marks_ref[index] for index in range(block + 1)], -1)
+    allowed = (query_pos >= key_pos) & same_document(marks_ref[block], key_marks)
+    scores = jnp.where(allowed, scores, MASKED)
+    expanded = jnp.exp(scores - jnp.max(scores, -1, keepdims=True))
+    return expanded / jnp.sum(expanded, -1, keepdims=True)
+
+
+def gelu_terms(values):
+    chance = 0.5 * (1.0 + lax.erf(values * (0.5**0.5)))
+    density = jnp.exp(-0.5 * values * values) * 0.3989422804014327
+    return values * chance, chance + values * density
+
+
+ANY = pl.BlockSpec(memory_space=pl.ANY)
+VMEM = pl.BlockSpec(memory_space=pltpu.VMEM)
+DMA = pltpu.SemaphoreType.DMA
+LIMIT = 60 << 20
+
+
+def gather_kernel(
+    x_ref, dy_ref, vec_ref, wo_ref, wd_ref, upb_ref, cos_ref, above_ref, below_ref, wq_ref, wu_ref,
+    x_out, ha_out, hm_out, wq_out, wu_out, qkv_out, marks_out, vec_out,
+    dy_out, a_out, du_out, do_out, o_out, sum_out,
+    xs, dys, hm, head, units, vecs, vectors, ha, qkv, whole, marks, mixed, act, grad, attended,
+    table, own_sem, x_store, ha_store, du_store, dy_store, late_store, v_send, v_recv, back_send, back_recv,
+    *sems,
 ):
     base, line, side, quarter = spot()
     rank = line * 2 + side
     tokens, width = x_ref.shape
+    hidden = act.shape[-1]
     rows = wq_ref.shape[0]
     part = rows // QUARTERS
-    relay = Relay(held, *sems[:6])
-    spread = Spread(
+    take = iter(range(0, len(sems)))
+
+    def some(count):
+        return [sems[next(take)] for _ in range(count)]
+
+    relay_x, relay_dy = Relay(xs, *some(6)), Relay(dys, *some(6))
+    head_columns, unit_columns = some(9), some(9)
+    spread_x = Spread(
         [
             (
                 lambda s: qkv.at[s],
-                lambda j, origin: qkv_out.at[j, :, pl.ds(origin * tokens, tokens), :],
+                lambda j, origin: whole.at[j, :, pl.ds(origin * tokens, tokens), :],
             ),
-            (lambda s: vecs.at[s, pl.ds(16, 8), :], lambda j, origin: seg_out.at[j, origin]),
+            (lambda s: vecs.at[s, pl.ds(16, 8), :], lambda j, origin: marks.at[j, origin]),
         ],
-        spread_send, spread_recv, spread_own,
-    )
-    columns = Columns(
-        lambda target: [
-            (
-                wq_ref.at[
-                    pl.ds(pl.multiple_of(quarter * part, 16), part),
-                    pl.ds(pl.multiple_of(kind * width + target * HEAD, HEAD), HEAD),
-                ],
-                kind * HEAD,
-                HEAD,
-            )
-            for kind in range(3)
-        ],
-        lambda source, slice_of, lane, lanes: weight.at[
-            pl.ds(pl.multiple_of(source * rows + slice_of * part, 16), part), pl.ds(lane, lanes)
-        ],
-        0, 3 * HEAD, sems[6:15],
-    )
-    greet_team(base, line, side, quarter)
-
-    def vector_copy(source, target, peer):
-        return send(
-            vec_ref, vecs.at[source], v_send.at[target], v_recv.at[source], base + peer, quarter
-        )
-
-    own_x = pltpu.make_async_copy(x_ref, held.at[rank], own_sem.at[0])
-    own_x.start()
-    own_v = pltpu.make_async_copy(vec_ref, vecs.at[rank], own_sem.at[1])
-    own_v.start()
-
-    def send_vector(step, _):
-        target = lax.rem(rank + step, TEAM)
-        vector_copy(rank, target, target).start()
-
-    lax.fori_loop(1, TEAM, send_vector, None)
-    columns.start()
-    own_x.wait()
-    own_v.wait()
-    relay.start(0)
-    columns.forward()
-    relay.start_halves()
-    relay.start(1)
-    columns.forward_last()
-
-    def take_vector(step, _):
-        origin = lax.rem(rank + TEAM - step, TEAM)
-        vector_copy(origin, rank, origin).wait_recv()
-
-    lax.fori_loop(1, TEAM, take_vector, None)
-    for source in range(TEAM):
-        for row in range(4):
-            vectors[pl.ds(row, 1), pl.ds(source * rows, rows)] = vecs[source, pl.ds(row, 1), :]
-    columns.arrive()
-    last_stores = [
-        pltpu.make_async_copy(weight, w_out, last_store.at[0]),
-        pltpu.make_async_copy(vecs, vec_out, last_store.at[1]),
-    ]
-    for copy in last_stores:
-        copy.start()
-
-    strip = 32
-    own_rows = pl.ds(pl.multiple_of(quarter * tokens, tokens), tokens)
-
-    def stores(which):
-        return [
-            pltpu.make_async_copy(src.at[which], dst.at[which], store_sem.at[index, which])
-            for index, (src, dst) in enumerate(((held, x_out), (ha, ha_out), (hm, hm_out)))
-        ]
-
-    def work(which):
-        def norm(index, _):
-            chunk = pl.ds(pl.multiple_of(index * strip, strip), strip)
-            unit, _ = normalize(held[which, chunk, :].astype(F32))
-            ha[which, chunk, :] = (unit * vectors[0:1, :] + vectors[2:3, :]).astype(BF16)
-            hm[which, chunk, :] = (unit * vectors[1:2, :] + vectors[3:4, :]).astype(BF16)
-
-        lax.fori_loop(0, tokens // strip, norm, None)
-        for kind in range(3):
-            chunk = kind * TEAM + rank
-            bias = vecs[lax.div(chunk, 3), pl.ds(8 + lax.rem(chunk, 3), 1), :]
-            made = dot(ha[which], weight[:, pl.ds(kind * HEAD, HEAD)]) + bias
-            if kind < 2:
-                low = rotate_low(
-                    made[:, :128], cos_ref[own_rows, :], above_ref[own_rows, :],
-                    below_ref[own_rows, :],
-                )
-                qkv[which, kind, :, pl.ds(0, 128)] = low.astype(BF16)
-                qkv[which, kind, :, pl.ds(128, HEAD - 128)] = made[:, 128:].astype(BF16)
-            else:
-                qkv[which, kind] = made.astype(BF16)
-        spread.start(which)
-        for copy in stores(which):
-            copy.start()
-
-    for step, place in enumerate(near_first(line)):
-
-        def one(other, _, step=step, place=place):
-            @pl.when(other == 1)
-            def _():
-                if 0 < step < PAIRS - 1:
-                    relay.start(step + 1)
-                if step > 0:
-                    relay.pass_halves(step)
-                relay.wait_over(step, place)
-
-            work(place * 2 + side + other * (1 - 2 * side))
-
-        lax.fori_loop(0, 2, one, None)
-
-    relay.finish()
-    spread.finish()
-    columns.finish()
-
-    def sent(step, _):
-        target = lax.rem(rank + step, TEAM)
-        vector_copy(rank, target, target).wait_send()
-
-    lax.fori_loop(1, TEAM, sent, None)
-
-    def stored(which, _):
-        for copy in stores(which):
-            copy.wait()
-
-    lax.fori_loop(0, TEAM, stored, None)
-    for copy in last_stores:
-        copy.wait()
-
-
-ANY = pl.BlockSpec(memory_space=pl.ANY)
-VMEM = pl.BlockSpec(memory_space=pltpu.VMEM)
-DMA = pltpu.SemaphoreType.DMA
-LIMIT = 60 << 20
-
-
-def first(x, w_qkv, vec, tables):
-    tokens, width = x.shape
-    shapes = [
-        ((TEAM, tokens, width), BF16),
-        ((TEAM, tokens, width), BF16),
-        ((TEAM, tokens, width), BF16),
-        ((width, 3 * HEAD), BF16),
-        ((2, 3, QUARTERS * tokens, HEAD), BF16),
-        ((2, QUARTERS, 8, tokens), F32),
-        ((TEAM, VECTOR_ROWS, vec.shape[-1]), F32),
-    ]
-    return pl.pallas_call(
-        first_kernel,
-        out_shape=[jax.ShapeDtypeStruct(*shape) for shape in shapes],
-        in_specs=[VMEM, ANY, VMEM, VMEM, VMEM, VMEM],
-        out_specs=[ANY] * len(shapes),
-        scratch_shapes=[
-            pltpu.VMEM((TEAM, tokens, width), BF16),
-            pltpu.VMEM((width, 3 * HEAD), BF16),
-            pltpu.VMEM((TEAM, VECTOR_ROWS, vec.shape[-1]), F32),
-            pltpu.VMEM((TEAM, tokens, width), BF16),
-            pltpu.VMEM((TEAM, tokens, width), BF16),
-            pltpu.VMEM((TEAM, 3, tokens, HEAD), BF16),
-            pltpu.VMEM((8, width), F32),
-            DMA((2,)),
-            DMA((3, TEAM)),
-            DMA((2,)),
-            DMA((TEAM,)),
-            DMA((TEAM,)),
-        ]
-        + spread_sems(2)
-        + RELAY_SEMS
-        + column_sems(3),
-        compiler_params=pltpu.CompilerParams(
-            collective_id=0, has_side_effects=True, vmem_limit_bytes=LIMIT
-        ),
-        name="gather_x",
-    )(x, w_qkv, vec, *tables)
-
-
-def gelu_terms(values):
-    chance = 0.5 * (1.0 + lax.erf(values * (0.5**0.5)))
-    density = jnp.exp(-0.5 * values * values) * 0.3989422804014327
-    return values * chance, chance + values * density
-
-
-def probabilities(start, block, q_ref, k_ref, col_ref, row_ref):
-    rows, keys = pl.ds(start, block), pl.ds(0, start + block)
-    scores = contract_last(q_ref[rows, :], k_ref[keys, :]) * HEAD ** (-0.5)
-    shape = scores.shape
-    query_pos = start + lax.broadcasted_iota(jnp.int32, shape, 0)
-    key_pos = lax.broadcasted_iota(jnp.int32, shape, 1)
-    allowed = (query_pos >= key_pos) & (col_ref[rows, :] == row_ref[:, keys])
-    scores = jnp.where(allowed, scores, MASKED)
-    expanded = jnp.exp(scores - jnp.max(scores, -1, keepdims=True))
-    return expanded / jnp.sum(expanded, -1, keepdims=True)
-
-
-def second_kernel(
-    dy_ref, wo_ref, wd_ref, upb_ref, col_ref, row_ref, wu_ref, hm_ref, qkv_ref,
-    dy_out, a_out, du_out, do_out, o_out, w_out, sum_out,
-    held, hm, weight, qkv, mixed, act, grad, attended,
-    own_sem, load_sem, store_sem, w_store, back_send, back_recv,
-    spread_send, spread_recv, spread_own, *sems,
-):
-    base, line, side, quarter = spot()
-    rank = line * 2 + side
-    tokens, width = dy_ref.shape
-    hidden = act.shape[-1]
-    rows = wu_ref.shape[0]
-    part = rows // QUARTERS
-    relay = Relay(held, *sems[:6])
-    spread = Spread(
+        *some(3),
+    )
+    spread_do = Spread(
         [
             (
                 lambda s: attended.at[s],
                 lambda j, origin: do_out.at[j, pl.ds(origin * tokens, tokens), :],
             )
         ],
-        spread_send, spread_recv, spread_own,
-    )
-    columns = Columns(
+        *some(3),
+    )
+    mine = pl.ds(pl.multiple_of(quarter * part, 16), part)
+
+    def landing(weight):
+        def place(source, slice_of, lane, lanes):
+            band = pl.ds(pl.multiple_of(source * rows + slice_of * part, 16), part)
+            return weight.at[band, pl.ds(lane, lanes)]
+
+        return place
+
+    head_columns = Columns(
         lambda target: [
             (
-                wu_ref.at[
-                    pl.ds(pl.multiple_of(quarter * part, 16), part),
-                    pl.ds(pl.multiple_of(target * hidden, hidden), hidden),
-                ],
-                0,
-                hidden,
+                wq_ref.at[mine, pl.ds(pl.multiple_of(kind * width + target * HEAD, HEAD), HEAD)],
+                kind * HEAD,
+                HEAD,
             )
+            for kind in range(3)
         ],
-        lambda source, slice_of, lane, lanes: weight.at[
-            pl.ds(pl.multiple_of(source * rows + slice_of * part, 16), part), pl.ds(lane, lanes)
+        landing(head), 0, 3 * HEAD, head_columns,
+    )
+    unit_columns = Columns(
+        lambda target: [
+            (wu_ref.at[mine, pl.ds(pl.multiple_of(target * hidden, hidden), hidden)], 0, hidden)
         ],
-        0, hidden, sems[6:15],
-    )
-    load_qkv = pltpu.make_async_copy(qkv_ref, qkv, load_sem.at[0])
-    load_hm = pltpu.make_async_copy(hm_ref, hm, load_sem.at[1])
-    load_qkv.start()
-    load_hm.start()
+        landing(units), 0, hidden, unit_columns,
+    )
+    own_rows = pl.ds(pl.multiple_of(quarter * tokens, tokens), tokens)
     greet_team(base, line, side, quarter)
-    own = pltpu.make_async_copy(dy_ref, held.at[rank], own_sem.at[0])
-    own.start()
-    columns.start()
-    own.wait()
-    relay.start(0)
-
-    load_qkv.wait()
-    length = QUARTERS * tokens
+
+    def vector_copy(source, target, peer):
+        return send(
+            vec_ref, vecs.at[source], v_send.at[target], v_recv.at[source], base + peer, quarter
+        )
+
+    owns = [
+        pltpu.make_async_copy(src, dst, own_sem.at[index])
+        for index, (src, dst) in enumerate(
+            (
+                (x_ref, xs.at[rank]),
+                (vec_ref, vecs.at[rank]),
+                (dy_ref, dys.at[rank]),
+                (cos_ref.at[own_rows, :], table.at[0]),
+                (above_ref.at[own_rows, :], table.at[1]),
+                (below_ref.at[own_rows, :], table.at[2]),
+            )
+        )
+    ]
+    for copy in owns:
+        copy.start()
+
+    def send_vector(step, _):
+        target = lax.rem(rank + step, TEAM)
+        vector_copy(rank, target, target).start()
+
+    lax.fori_loop(1, TEAM, send_vector, None)
+    head_columns.start()
+    for copy in owns:
+        copy.wait()
+    relay_x.start(0)
+    head_columns.forward()
+    relay_x.start_halves()
+    relay_x.start(1)
+    head_columns.forward_last()
+
+    def take_vector(step, _):
+        origin = lax.rem(rank + TEAM - step, TEAM)
+        vector_copy(origin, rank, origin).wait_recv()
+
+    lax.fori_loop(1, TEAM, take_vector, None)
+    for source in range(TEAM):
+        for row in range(4):
+            vectors[pl.ds(row, 1), pl.ds(source * rows, rows)] = vecs[source, pl.ds(row, 1), :]
+    head_columns.arrive()
+    late = [
+        pltpu.make_async_copy(src, dst, late_store.at[index])
+        for index, (src, dst) in enumerate(
+            ((head, wq_out), (vecs, vec_out), (units, wu_out), (whole, qkv_out), (marks, marks_out))
+        )
+    ]
+    late[0].start()
+    late[1].start()
+
+    strip = 128
+    order = near_first(line)
+
+    def member(step, other):
+        return order[step] * 2 + side + other * (1 - 2 * side)
+
+    def store_x(which):
+        return [
+            pltpu.make_async_copy(xs.at[which], x_out.at[which], x_store.at[0, which]),
+            pltpu.make_async_copy(hm.at[which], hm_out.at[which], x_store.at[1, which]),
+        ]
+
+    def store_ha(slot, which):
+        return pltpu.make_async_copy(ha.at[slot], ha_out.at[which], ha_store.at[slot])
+
+    def project(slot, which):
+        def norm(index, _):
+            chunk = pl.ds(pl.multiple_of(index * strip, strip), strip)
+            unit, _ = normalize(xs[which, chunk, :].astype(F32))
+            ha[slot, chunk, :] = (unit * vectors[0:1, :] + vectors[2:3, :]).astype(BF16)
+            hm[which, chunk, :] = (unit * vectors[1:2, :] + vectors[3:4, :]).astype(BF16)
+
+        lax.fori_loop(0, tokens // strip, norm, None)
+        for kind in range(3):
+            chunk = kind * TEAM + rank
+            bias = vecs[lax.div(chunk, 3), pl.ds(8 + lax.rem(chunk, 3), 1), :]
+            made = dot(ha[slot], head[:, pl.ds(kind * HEAD, HEAD)]) + bias
+            if kind < 2:
+                low = rotate_low(made[:, :128], table[0], table[1], table[2])
+                qkv[which, kind, :, pl.ds(0, 128)] = low.astype(BF16)
+                qkv[which, kind, :, pl.ds(128, HEAD - 128)] = made[:, 128:].astype(BF16)
+            else:
+                qkv[which, kind] = made.astype(BF16)
+        spread_x.start(which)
+        store_ha(slot, which).start()
+        for copy in store_x(which):
+            copy.start()
+
+    for step, place in enumerate(order):
+
+        def one(other, _, step=step, place=place):
+            @pl.when(other == 1)
+            def _():
+                if 0 < step < PAIRS - 1:
+                    relay_x.start(step + 1)
+                if step > 0:
+                    relay_x.pass_halves(step)
+                if step == 2:
+                    unit_columns.start()
+                    relay_dy.start(0)
+                relay_x.wait_over(step, place)
+
+            if step > 0:
+                store_ha(other, member(step - 1, other)).wait()
+            project(other, member(step, other))
+
+        lax.fori_loop(0, 2, one, None)
+
+    unit_columns.forward()
+    sum_out[...] = jnp.zeros_like(sum_out)
+    relay_dy.start_halves()
+    relay_dy.start(1)
+    unit_columns.forward_last()
+    spread_x.finish()
+    late[3].start()
+    late[4].start()
 
     def attend(sequence, _):
-        q, k, v = (qkv.at[sequence, kind] for kind in range(3))
-        for start in range(0, length, tokens):
-            probs = probabilities(
-                start, tokens, q, k, col_ref.at[sequence], row_ref.at[sequence]
-            )
-            value_block = v[pl.ds(0, start + tokens), :]
-            mixed[sequence, pl.ds(start, tokens), :] = dot(
+        q, k, v = (whole.at[sequence, kind] for kind in range(3))
+        for block in range(QUARTERS):
+            probs = probabilities(block, tokens, q, k, marks.at[sequence])
+            value_block = v[pl.ds(0, (block + 1) * tokens), :]
+            mixed[sequence, pl.ds(block * tokens, tokens), :] = dot(
                 probs.astype(BF16), value_block
             ).astype(BF16)
 
@@ -709,129 +669,170 @@
 
     def back(to, origin):
         return send(
-            mixed.at[:, pl.ds(to * tokens, tokens), :], o_out.at[pl.ds(2 * origin, 2)],
+            mixed.at[:, pl.ds(to * tokens, tokens), :], o_out.at[:, among(origin)],
             back_send.at[to], back_recv.at[origin], base + rank, to,
         )
 
     own_back = pltpu.make_async_copy(
-        mixed.at[:, pl.ds(quarter * tokens, tokens), :], o_out.at[pl.ds(2 * quarter, 2)],
-        own_sem.at[1],
+        mixed.at[:, pl.ds(quarter * tokens, tokens), :], o_out.at[:, among(quarter)],
+        own_sem.at[6],
     )
     own_back.start()
     for step in range(1, QUARTERS):
         to = lax.rem(quarter + step, QUARTERS)
         back(to, quarter).start()
-    columns.forward()
-    sum_out[...] = jnp.zeros_like(sum_out)
-    relay.start_halves()
-    relay.start(1)
-    columns.forward_last()
-    columns.arrive()
-    store_weight = pltpu.make_async_copy(weight, w_out, w_store)
-    store_weight.start()
-    load_hm.wait()
-
-    def stores(which):
+    unit_columns.arrive()
+    late[2].start()
+
+    def store_dy(which):
+        return pltpu.make_async_copy(dys.at[which], dy_out.at[which], dy_store.at[which])
+
+    def store_du(slot, which):
         return [
-            pltpu.make_async_copy(src.at[which], dst.at[which], store_sem.at[index, which])
-            for index, (src, dst) in enumerate(((held, dy_out), (act, a_out), (grad, du_out)))
+            pltpu.make_async_copy(act.at[slot], a_out.at[which], du_store.at[0, slot]),
+            pltpu.make_async_copy(grad.at[slot], du_out.at[which], du_store.at[1, slot]),
         ]
 
-    def work(which):
-        attended[which] = contract_last(held[which], wo_ref[...]).astype(BF16)
-        spread.start(which)
+    def pull(slot, which):
+        attended[which] = contract_last(dys[which], wo_ref[...]).astype(BF16)
+        spread_do.start(which)
         for start in range(0, hidden, 256):
             span = pl.ds(start, 256)
-            up = dot(hm[which], weight[:, span]) + upb_ref[:, span]
+            up = dot(hm[which], units[:, span]) + upb_ref[:, span]
             value, slope = gelu_terms(up)
-            act[which, :, span] = value.astype(BF16)
-            pulled = contract_last(held[which], wd_ref[span, :])
-            grad[which, :, span] = (pulled * slope).astype(BF16)
-        for copy in stores(which):
+            act[slot, :, span] = value.astype(BF16)
+            pulled = contract_last(dys[which], wd_ref[span, :])
+            grad[slot, :, span] = (pulled * slope).astype(BF16)
+        for copy in store_du(slot, which):
             copy.start()
-        sum_out[0:1, :] += jnp.sum(held[which].astype(F32), 0, keepdims=True)
-
-    for step, place in enumerate(near_first(line)):
+        store_dy(which).start()
+        sum_out[0:1, :] += jnp.sum(dys[which].astype(F32), 0, keepdims=True)
+
+    for step, place in enumerate(order):
 
         def one(other, _, step=step, place=place):
             @pl.when(other == 1)
             def _():
                 if 0 < step < PAIRS - 1:
-                    relay.start(step + 1)
+                    relay_dy.start(step + 1)
                 if step > 0:
-                    relay.pass_halves(step)
-                relay.wait_over(step, place)
-
-            work(place * 2 + side + other * (1 - 2 * side))
+                    relay_dy.pass_halves(step)
+                relay_dy.wait_over(step, place)
+
+            if step > 0:
+                for copy in store_du(other, member(step - 1, other)):
+                    copy.wait()
+            pull(other, member(step, other))
 
         lax.fori_loop(0, 2, one, None)
 
-    relay.finish()
-    spread.finish()
-    columns.finish()
+    relay_x.finish()
+    relay_dy.finish()
+    spread_do.finish()
+    head_columns.finish()
+    unit_columns.finish()
     for step in range(1, QUARTERS):
         other = lax.rem(quarter + step, QUARTERS)
         back(other, quarter).wait_send()
         back(other, other).wait_recv()
     own_back.wait()
-    store_weight.wait()
+
+    def sent(step, _):
+        target = lax.rem(rank + step, TEAM)
+        vector_copy(rank, target, target).wait_send()
+
+    lax.fori_loop(1, TEAM, sent, None)
 
     def stored(which, _):
-        for copy in stores(which):
+        for copy in store_x(which):
             copy.wait()
+        store_dy(which).wait()
 
     lax.fori_loop(0, TEAM, stored, None)
-
-
-def second(dy, w_out, w_down, up_bias, column, row, w_up, mlp_input, qkv):
-    tokens, width = dy.shape
+    for other in range(2):
+        store_ha(other, member(PAIRS - 1, other)).wait()
+        for copy in store_du(other, member(PAIRS - 1, other)):
+            copy.wait()
+    for copy in late:
+        copy.wait()
+
+
+def gather(x, dy, vec, w_out, w_down, up_bias, tables, w_qkv, w_up):
+    tokens, width = x.shape
     hidden = up_bias.shape[-1]
+    all_tokens = (TEAM, tokens, width)
+    whole = (2, 3, QUARTERS * tokens, HEAD)
+    marks = ((2, QUARTERS, 8, tokens), F32)
+    vecs = ((TEAM, VECTOR_ROWS, vec.shape[-1]), F32)
+    units = ((TEAM, tokens, hidden), BF16)
     shapes = [
-        ((TEAM, tokens, width), BF16),
-        ((TEAM, tokens, hidden), BF16),
-        ((TEAM, tokens, hidden), BF16),
+        (all_tokens, BF16),
+        (all_tokens, BF16),
+        (all_tokens, BF16),
+        ((width, 3 * HEAD), BF16),
+        ((width, hidden), BF16),
+        (whole, BF16),
+        marks,
+        vecs,
+        (all_tokens, BF16),
+        units,
+        units,
         ((2, QUARTERS * tokens, HEAD), BF16),
-        ((TEAM, tokens, HEAD), BF16),
-        ((width, hidden), BF16),
+        ((2, QUARTERS, tokens, HEAD), BF16),
         ((8, width), F32),
     ]
     return pl.pallas_call(
-        second_kernel,
+        gather_kernel,
         out_shape=[jax.ShapeDtypeStruct(*shape) for shape in shapes],
-        in_specs=[VMEM] * 6 + [ANY] * 3,
-        out_specs=[ANY] * 6 + [VMEM],
+        in_specs=[ANY] * 2 + [VMEM] * 4 + [ANY] * 5,
+        out_specs=[ANY] * 13 + [VMEM],
         scratch_shapes=[
-            pltpu.VMEM((TEAM, tokens, width), BF16),
-            pltpu.VMEM((TEAM, tokens, width), BF16),
+            pltpu.VMEM(all_tokens, BF16),
+            pltpu.VMEM(all_tokens, BF16),
+            pltpu.VMEM(all_tokens, BF16),
+            pltpu.VMEM((width, 3 * HEAD), BF16),
             pltpu.VMEM((width, hidden), BF16),
-            pltpu.VMEM(qkv.shape, BF16),
+            pltpu.VMEM(*vecs),
+            pltpu.VMEM((8, width), F32),
+            pltpu.VMEM((2, tokens, width), BF16),
+            pltpu.VMEM((TEAM, 3, tokens, HEAD), BF16),
+            pltpu.VMEM(whole, BF16),
+            pltpu.VMEM(*marks),
             pltpu.VMEM((2, QUARTERS * tokens, HEAD), BF16),
-            pltpu.VMEM((TEAM, tokens, hidden), BF16),
-            pltpu.VMEM((TEAM, tokens, hidden), BF16),
+            pltpu.VMEM((2, tokens, hidden), BF16),
+            pltpu.VMEM((2, tokens, hidden), BF16),
             pltpu.VMEM((TEAM, tokens, HEAD), BF16),
+            pltpu.VMEM((3, tokens, 128), F32),
+            DMA((7,)),
+            DMA((2, TEAM)),
             DMA((2,)),
-            DMA((2,)),
-            DMA((3, TEAM)),
-            DMA,
+            DMA((2, 2)),
+            DMA((TEAM,)),
+            DMA((5,)),
+            DMA((TEAM,)),
+            DMA((TEAM,)),
             DMA((QUARTERS,)),
             DMA((QUARTERS,)),
         ]
-        + spread_sems(1)
-        + RELAY_SEMS
-        + column_sems(1),
+        + RELAY_SEMS * 2
+        + column_sems(3)
+        + column_sems(1)
+        + spread_sems(2)
+        + spread_sems(1),
         compiler_params=pltpu.CompilerParams(
-            collective_id=1, has_side_effects=True, vmem_limit_bytes=LIMIT
+            collective_id=0, has_side_effects=True, vmem_limit_bytes=LIMIT
         ),
-        name="gather_dy",
-    )(dy, w_out, w_down, up_bias, column, row, w_up, mlp_input, qkv)
+        name="gather",
+    )(x, dy, vec, w_out, w_down, up_bias, *tables, w_qkv, w_up)
 
 
 def backward_kernel(
-    block, qkv_ref, do_ref, col_ref, row_ref, cos_ref, above_ref, below_ref, d_ref, dk_sum, dv_sum
+    qkv_ref, do_ref, marks_ref, cos_ref, above_ref, below_ref, d_ref, dk_sum, dv_sum
 ):
     scale = HEAD ** (-0.5)
     q_ref, k_ref, v_ref = (qkv_ref.at[kind] for kind in range(3))
     length = q_ref.shape[0]
+    size = marks_ref.shape[-1]
 
     def put(kind, rows, grads):
         low = unrotate_low(
@@ -842,9 +843,10 @@
 
     dk_sum[...] = jnp.zeros_like(dk_sum)
     dv_sum[...] = jnp.zeros_like(dv_sum)
-    for start in range(0, length, block):
-        rows, keys = pl.ds(start, block), pl.ds(0, start + block)
-        probs = probabilities(start, block, q_ref, k_ref, col_ref, row_ref)
+    for block in range(length // size):
+        start = block * size
+        rows, keys = pl.ds(start, size), pl.ds(0, start + size)
+        probs = probabilities(block, size, q_ref, k_ref, marks_ref)
         grads = do_ref[rows, :]
         grad_probs = contract_last(grads, v_ref[keys, :])
         row_dot = jnp.sum(probs * grad_probs, -1, keepdims=True)
@@ -856,49 +858,55 @@
     d_ref[2] = dv_sum[...].astype(BF16)
 
 
-def attention_specs(seqs, length):
+def attend_back(qkv, grads, marks, tables):
+    seqs, _, length, head = qkv.shape
     three = pl.BlockSpec((None, 3, length, HEAD), lambda s: (s, 0, 0, 0))
     one = pl.BlockSpec((None, length, HEAD), lambda s: (s, 0, 0))
-    masks = [
-        pl.BlockSpec((None, length, 1), lambda s: (s, 0, 0)),
-        pl.BlockSpec((None, 1, length), lambda s: (s, 0, 0)),
-    ]
-    return three, one, masks
-
-
-def attend_back(qkv, grads, column, row, tables):
-    seqs, _, length, head = qkv.shape
-    three, one, masks = attention_specs(seqs, length)
     table = pl.BlockSpec((length, 128), lambda s: (0, 0))
     return pl.pallas_call(
-        partial(backward_kernel, min(256, length)),
+        backward_kernel,
         grid=(seqs,),
-        in_specs=[three, one] + masks + [table] * 3,
+        in_specs=[three, one, pl.BlockSpec((None, *marks.shape[1:]), lambda s: (s, 0, 0, 0))]
+        + [table] * 3,
         out_specs=three,
         out_shape=jax.ShapeDtypeStruct(qkv.shape, BF16),
         scratch_shapes=[pltpu.VMEM((length, head), F32)] * 2,
         compiler_params=pltpu.CompilerParams(vmem_limit_bytes=48 << 20),
         name="attend_back",
-    )(qkv, grads, column, row, *tables)
+    )(qkv, grads, marks, *tables)
 
 
 class Reduce:
-    def __init__(self, own, side_out, side_in, line_in, sems):
-        self.own, self.side_out, self.side_in, self.line_in = own, side_out, side_in, line_in
-        self.sems = sems
+    def __init__(self, cut, own, side_out, side_in, line_in, half_in, sems):
+        self.cut = cut
+        self.own, self.side_out, self.side_in = own, side_out, side_in
+        self.line_in, self.half_in, self.sems = line_in, half_in, sems
         self.base, self.line, self.side, self.quarter = spot()
         self.order = near_first(self.line)
-
-    def over(self, step):
+        self.inner = (self.line > 0) & (self.line < PAIRS - 1)
+        self.tokens = own.shape[1]
+
+    def over(self, step, low):
         side_send, side_recv = self.sems[:2]
         place = self.base + self.line * 2 + 1 - self.side
+        rows = pl.ds(self.cut, self.tokens - self.cut) if low else pl.ds(0, self.tokens)
         return send(
-            self.side_out.at[step], self.side_in.at[step], side_send.at[step], side_recv.at[step],
-            place, self.quarter,
-        )
+            self.side_out.at[step, rows], self.side_in.at[step, rows],
+            side_send.at[step], side_recv.at[step], place, self.quarter,
+        )
+
+    def crossing(self, step, act):
+        if step == PAIRS - 1:
+            act(self.over(step, True))
+        elif step == 1:
+            act(self.over(step, False))
+        else:
+            first, second = (True, False) if step == PAIRS - 2 else (False, True)
+            pl.when(self.inner)(lambda: act(self.over(step, first)))
+            pl.when(jnp.logical_not(self.inner))(lambda: act(self.over(step, second)))
 
     def along(self, step, target, way):
-        line_send, line_recv = self.sems[2:]
+        line_send, line_recv = self.sems[2:4]
         move = 1 if way == RIGHT else -1
         slot = target if way == RIGHT else jnp.where(target == self.line - 1, PAIRS, target)
         place = self.base + (self.line + move) * 2 + self.side
@@ -908,23 +916,84 @@
         )
 
     def arrive(self, slot):
-        line_send, line_recv = self.sems[2:]
+        line_send, line_recv = self.sems[2:4]
         return send(
             self.side_out.at[0], self.line_in.at[slot], line_send.at[0], line_recv.at[slot],
             self.base + self.line * 2 + 1 - self.side, self.quarter,
         )
 
+    def upper(self, step, way):
+        half_send, half_recv = self.sems[4:6]
+        move = 1 if way == RIGHT else -1
+        rows = pl.ds(0, self.cut)
+        place = self.base + (self.line + move) * 2 + self.side
+        return send(
+            self.side_out.at[step, rows], self.half_in.at[way], half_send.at[way],
+            half_recv.at[way], place, self.quarter,
+        )
+
+    def upper_over(self):
+        cross_send, cross_recv = self.sems[6:8]
+        rows = pl.ds(0, self.cut)
+        place = self.base + self.line * 2 + 1 - self.side
+        return send(
+            self.side_out.at[0, rows], self.side_in.at[0, rows], cross_send, cross_recv, place,
+            self.quarter,
+        )
+
     def begin(self, step):
-        self.over(step).start()
-
-    def mine(self, step, chunk):
+        self.crossing(step, lambda copy: copy.start())
+
+    def launch(self):
+        pl.when(self.line == 0)(lambda: self.upper(PAIRS - 1, RIGHT).start())
+        pl.when(self.line == PAIRS - 1)(lambda: self.upper(PAIRS - 1, LEFT).start())
+
+    def hop(self, count):
+        for way in (RIGHT, LEFT):
+            here = count if way == RIGHT else PAIRS - 1 - count
+            step = (None, PAIRS - 1, PAIRS - 2, 0)[count]
+
+            @pl.when(self.line == here)
+            def _(way=way, step=step):
+                self.upper(step, way).wait_recv()
+                rows = pl.ds(0, self.cut)
+                total = self.side_out[step, rows].astype(F32) + self.half_in[way].astype(F32)
+                self.side_out[step, rows] = total.astype(BF16)
+                if count < PAIRS - 1:
+                    self.upper(step, way).start()
+                else:
+                    self.upper_over().start()
+
+    def upper_sent(self, step):
+        first, second = (RIGHT, LEFT) if step == PAIRS - 1 else (LEFT, RIGHT)
+        low_line = self.line < PAIRS // 2
+
+        def wait():
+            pl.when(low_line)(lambda: self.upper(step, first).wait_send())
+            pl.when(jnp.logical_not(low_line))(lambda: self.upper(step, second).wait_send())
+
+        if step == PAIRS - 1:
+            wait()
+        elif step == PAIRS - 2:
+            pl.when(self.inner)(wait)
+
+    def mine(self, step, index, strip):
+        chunk = pl.ds(pl.multiple_of(index * strip, strip), strip)
         slot = step if self.own.shape[0] > 1 else 0
-        return self.own[slot, chunk, :].astype(F32) + self.side_in[step, chunk, :].astype(F32)
+        own = self.own[slot, chunk, :].astype(F32)
+        other = self.side_in[step, chunk, :].astype(F32)
+        if step == PAIRS - 1:
+            return jnp.where(index * strip >= self.cut, own + other, own)
+        if step == PAIRS - 2:
+            whole = (index * strip >= self.cut) | jnp.logical_not(self.inner)
+            return jnp.where(whole, own + other, own)
+        return own + other
 
     def advance(self, step):
         target = self.order[step]
-        self.over(step).wait_recv()
-        self.over(step).wait_send()
+        self.crossing(step, lambda copy: copy.wait_recv())
+        self.crossing(step, lambda copy: copy.wait_send())
+        self.upper_sent(step)
 
         def forward(way, upstream):
             pl.when(upstream)(lambda: self.arrive(target).wait_recv())
@@ -932,25 +1001,32 @@
 
             def add(index, _):
                 chunk = pl.ds(pl.multiple_of(index * strip, strip), strip)
-                total = self.mine(step, chunk)
+                total = self.mine(step, index, strip)
                 passing = self.line_in[target, chunk, :].astype(F32)
                 total = jnp.where(upstream, total + passing, total)
                 self.side_out[step, chunk, :] = total.astype(BF16)
 
-            lax.fori_loop(0, self.own.shape[1] // strip, add, None)
+            lax.fori_loop(0, self.tokens // strip, add, None)
             self.along(step, target, way).start()
 
         pl.when(target > self.line)(lambda: forward(RIGHT, self.line > 0))
         pl.when(target < self.line)(lambda: forward(LEFT, self.line < PAIRS - 1))
 
     def last(self):
-        self.over(0).wait_recv()
-        self.over(0).wait_send()
+        self.crossing(0, lambda copy: copy.wait_recv())
+        self.crossing(0, lambda copy: copy.wait_send())
+
+        @pl.when(jnp.logical_not(self.inner))
+        def _():
+            self.upper_over().wait_recv()
+            self.upper_over().wait_send()
+
         pl.when(self.line > 0)(lambda: self.arrive(self.line).wait_recv())
         pl.when(self.line < PAIRS - 1)(lambda: self.arrive(PAIRS).wait_recv())
 
-    def total(self, chunk):
-        total = self.mine(0, chunk)
+    def total(self, index, strip):
+        chunk = pl.ds(pl.multiple_of(index * strip, strip), strip)
+        total = self.mine(0, index, strip)
         left = self.line_in[self.line, chunk, :].astype(F32)
         right = self.line_in[PAIRS, chunk, :].astype(F32)
         total = jnp.where(self.line > 0, total + left, total)
@@ -963,16 +1039,24 @@
             pl.when(target < self.line)(lambda: self.along(step, target, LEFT).wait_send())
 
 
-def reduce_scratch(tokens, width, slots, dtype):
+REDUCE = 13
+
+
+def reduce_scratch(tokens, width, slots, dtype, cut):
     return [
         pltpu.VMEM((slots, tokens, width), dtype),
         pltpu.VMEM((PAIRS, tokens, width), BF16),
         pltpu.VMEM((PAIRS, tokens, width), BF16),
         pltpu.VMEM((PAIRS + 1, tokens, width), BF16),
+        pltpu.VMEM((2, cut, width), BF16),
         DMA((PAIRS,)),
         DMA((PAIRS,)),
         DMA((PAIRS,)),
         DMA((PAIRS + 1,)),
+        DMA((2,)),
+        DMA((2,)),
+        DMA,
+        DMA,
     ]
 
 
@@ -1065,15 +1149,16 @@
 
 def third_kernel(
     x_ref, o_ref, a_ref, wo_ref, wd_ref, vec_ref, du_ref, d_ref, hm_ref, dy_ref,
-    result_ref, back_out, up_out, rows_out,
+    result_out, back_out, up_out, rows_out,
     own_sem, back_send, back_recv, load_sem, store_sem, hm_tiles, tile_sum, dy, bias, *rest,
 ):
     base, line, side, quarter = spot()
     rank = line * 2 + side
     tokens, width = x_ref.shape
     part = width // TEAM // QUARTERS
-    reduce = Reduce(*rest[:4], rest[4:8])
-    ups, downs = Quarters(*rest[8:16]), Quarters(*rest[16:24])
+    reduce = Reduce(tokens // 2, *rest[:5], rest[5:REDUCE])
+    rest = rest[REDUCE:]
+    ups, downs = Quarters(*rest[:8]), Quarters(*rest[8:16])
     stream = Stream(hm_ref, hm_tiles, load_sem)
     load_dy = pltpu.make_async_copy(dy_ref, dy, own_sem.at[3])
     load_dy.start()
@@ -1084,7 +1169,7 @@
     def pieces(to, origin, kind):
         return (
             d_ref.at[:, kind, pl.ds(to * tokens, tokens), :],
-            back_out.at[pl.ds(2 * origin, 2), :, pl.ds(kind * HEAD, HEAD)],
+            back_out.at[:, among(origin), :, pl.ds(kind * HEAD, HEAD)],
         )
 
     def back(to, origin, kind):
@@ -1108,7 +1193,7 @@
             )
 
     def put_own(span, value):
-        reduce.own[0, :, span] = value
+        reduce.own[0, :, span] = value.astype(BF16)
 
     for step in reversed(range(PAIRS)):
 
@@ -1118,6 +1203,7 @@
         make(reduce.order[step] * 2 + 1 - side, put_out)
         reduce.begin(step)
         if step == PAIRS - 1:
+            reduce.launch()
             for kind in range(3):
                 own_back[kind].start()
                 for hop in range(1, QUARTERS):
@@ -1130,9 +1216,11 @@
         ups.put(tile, lambda q: tile_sum[pl.ds(pl.multiple_of(q * part, part), part), :])
 
     stream.run(TEAM, up_tile)
+    reduce.hop(1)
+    ups.over_cores()
     make(reduce.order[3] * 2 + side, put_own)
     reduce.advance(3)
-    ups.over_cores()
+    reduce.hop(2)
     load_dy.wait()
     share = width // QUARTERS
 
@@ -1151,6 +1239,7 @@
     lax.fori_loop(0, HEAD // 128, partial(down_tile, o_ref, hidden), None)
     make(reduce.order[2] * 2 + side, put_own)
     reduce.advance(2)
+    reduce.hop(3)
     downs.over_cores()
     make(reduce.order[1] * 2 + side, put_own)
     reduce.advance(1)
@@ -1172,10 +1261,12 @@
 
     def close(index, _):
         chunk = pl.ds(pl.multiple_of(index * strip, strip), strip)
-        total = reduce.total(chunk) + bias[0:1, :]
-        result_ref[chunk, :] = (x_ref[chunk, :].astype(F32) + total).astype(BF16)
+        total = reduce.total(index, strip) + bias[0:1, :]
+        reduce.own[0, chunk, :] = (x_ref[chunk, :].astype(F32) + total).astype(BF16)
 
     lax.fori_loop(0, tokens // strip, close, None)
+    store_result = pltpu.make_async_copy(reduce.own.at[0], result_out, store_sem.at[2])
+    store_result.start()
     downs.over_chips(lambda tile: store_down(tile).start())
     reduce.finish()
     for kind in range(3):
@@ -1184,6 +1275,7 @@
             origin = lax.rem(quarter + hop, QUARTERS)
             back(origin, quarter, kind).wait_send()
             back(origin, origin, kind).wait_recv()
+    store_result.wait()
     ups.finish()
     downs.finish()
     lax.fori_loop(0, ups.tiles, lambda tile, _: store_up(tile).wait(), None)
@@ -1197,7 +1289,7 @@
     tiles = (hidden + HEAD) // 128
     shapes = [
         (tokens, width),
-        (TEAM, tokens, 3 * HEAD),
+        (2, QUARTERS, tokens, 3 * HEAD),
         (TEAM, part, hidden),
         (tiles * 128, share),
     ]
@@ -1205,19 +1297,19 @@
         third_kernel,
         out_shape=[jax.ShapeDtypeStruct(shape, BF16) for shape in shapes],
         in_specs=[VMEM] * 7 + [ANY] * 3,
-        out_specs=[VMEM, ANY, ANY, ANY],
+        out_specs=[ANY] * 4,
         scratch_shapes=[
             DMA((4,)),
             DMA((QUARTERS, 3)),
             DMA((QUARTERS, 3)),
             DMA((2,)),
-            DMA((2,)),
+            DMA((3,)),
             pltpu.VMEM((2, TEAM * tokens, width // TEAM), BF16),
             pltpu.VMEM((width // TEAM, hidden), F32),
             pltpu.VMEM((TEAM * tokens, width), BF16),
             pltpu.VMEM((8, width), F32),
         ]
-        + reduce_scratch(tokens, width, 1, F32)
+        + reduce_scratch(tokens, width, 1, BF16, tokens // 2)
         + quarters_scratch(TEAM, part, hidden)
         + quarters_scratch(tiles, 128, share),
         compiler_params=pltpu.CompilerParams(
@@ -1240,18 +1332,19 @@
     part = width // TEAM // QUARTERS
     block = width // TEAM
     core, chip = core_peer(quarter), chip_peer(quarter)
-    reduce = Reduce(*rest[:4], rest[4:8])
-    qkvs = Quarters(*rest[8:16])
+    reduce = Reduce(tokens // 4, *rest[:5], rest[5:REDUCE])
+    rest = rest[REDUCE:]
+    qkvs = Quarters(*rest[:8])
 
     def place(source, slice_of, lane, lanes):
         rows = pl.ds(pl.multiple_of(slice_of * part, 16), part)
         return landed.at[source, rows, pl.ds(lane, lanes)]
 
     up_columns = Columns(
-        lambda n: [(up_ref.at[n], 3 * HEAD, hidden)], place, 3 * HEAD, hidden, rest[16:25]
+        lambda n: [(up_ref.at[n], 3 * HEAD, hidden)], place, 3 * HEAD, hidden, rest[8:17]
     )
     qkv_columns = Columns(
-        lambda n: [(qkvs.total(n), 0, 3 * HEAD)], place, 0, 3 * HEAD, rest[25:34]
+        lambda n: [(qkvs.total(n), 0, 3 * HEAD)], place, 0, 3 * HEAD, rest[17:26]
     )
     stream = Stream(ha_ref, ha_tiles, tile_load)
     loads = [
@@ -1274,7 +1367,6 @@
     own_rows = pltpu.make_async_copy(rows_ref, rows_out.at[quarter], row_own)
     own_rows.start()
     rows_copy(0, quarter, core).start()
-    rows_copy(1, quarter, chip).start()
     up_columns.start()
     sums[...] = jnp.zeros_like(sums)
     for source in range(TEAM):
@@ -1310,6 +1402,8 @@
 
         make(reduce.order[step] * 2 + 1 - side, put_out)
         reduce.begin(step)
+        if step == PAIRS - 1:
+            reduce.launch()
 
     def qkv_tile(tile, held):
         tile_sum[...] = contract_first(held[...], dqkv_ref[...])
@@ -1317,6 +1411,8 @@
 
     stream.run(TEAM, qkv_tile)
     qkvs.over_cores()
+    rows_copy(1, quarter, chip).start()
+    reduce.hop(1)
     for step in reversed(range(PAIRS)):
 
         def put_own(span, value, step=step):
@@ -1325,6 +1421,8 @@
         make(reduce.order[step] * 2 + side, put_own)
         if step == PAIRS - 1:
             reduce.advance(step)
+
+    reduce.hop(2)
 
     def pack(target, _):
         span = pl.ds(pl.multiple_of(target * block, block), block)
@@ -1355,12 +1453,13 @@
 
     up_columns.forward()
     reduce.advance(2)
+    reduce.hop(3)
+    qkvs.over_chips(lambda tile: None)
+    qkv_columns.start()
+    reduce.advance(1)
     rows_copy(1, chip, chip).wait_recv()
     rows_copy(2, chip, core).start()
-    qkvs.over_chips(lambda tile: None)
-    qkv_columns.start()
     up_columns.forward_last()
-    reduce.advance(1)
 
     def take_packets(step, _):
         source = lax.rem(rank + TEAM - step, TEAM)
@@ -1389,7 +1488,7 @@
 
     def close(index, _):
         chunk = pl.ds(pl.multiple_of(index * strip, strip), strip)
-        pulled = reduce.total(chunk)
+        pulled = reduce.total(index, strip)
         unit, inverse = normalize(x_ref[chunk, :].astype(F32))
         pulled = (
             pulled
@@ -1466,7 +1565,7 @@
             DMA((QUARTERS,)),
             DMA((QUARTERS,)),
         ]
-        + reduce_scratch(tokens, width, PAIRS, BF16)
+        + reduce_scratch(tokens, width, PAIRS, BF16, tokens // 4)
         + quarters_scratch(TEAM, part, 3 * HEAD)
         + column_sems(1) * 2,
         compiler_params=pltpu.CompilerParams(
@@ -1678,16 +1777,14 @@
     mine_team = team_order(mine)
     positions = jnp.arange(ctx * tokens, dtype=jnp.int32)
     tables = rotary_tables(positions.astype(F32))
-    everyone, attn_input, mlp_input, w_head, qkv, marks, vectors = first(
-        mine_team, w_qkv, packet, tables
-    )
-    marks = marks[:, :, 0, :].reshape(2, ctx * tokens)
-    column, row = marks[:, :, None], marks[:, None, :]
-    grad_rows, activated, grad_up, grad_attended, attended, w_units, dy_sum = second(
-        grad_mine, w_out, w_down, b_up.astype(F32).reshape(1, hidden), column, row, w_up, mlp_input,
-        qkv,
-    )
-    grads = attend_back(qkv, grad_attended, column, row, tables)
+    (
+        everyone, attn_input, mlp_input, w_head, w_units, qkv, marks, vectors,
+        grad_rows, activated, grad_up, grad_attended, attended, dy_sum,
+    ) = gather(
+        mine_team, grad_mine, packet, w_out, w_down, b_up.astype(F32).reshape(1, hidden), tables,
+        w_qkv, w_up,
+    )
+    grads = attend_back(qkv, grad_attended, marks, tables)
     flat = (TEAM * tokens, -1)
     attn_input, mlp_input, grad_rows, activated, grad_up, attended = (
         values.reshape(flat)

time: 548 us -> 506 us (0.923)
  Pallas kernels: 523 us -> 479 us
    pallas_call x3 -> x2, Pallas kernels: 230 us -> 208 us  [the longest x1 198 us: gather(): pl.pallas_call(gather_kernel, out_shape=[jax.ShapeDtypeStruct(*shape) for...]
    pallas_call x1, Pallas kernels: 146 us -> 130 us  [fourth(): pl.pallas_call(fourth_kernel, out_shape=[jax.ShapeDtypeStruct(*shape) for...]
    pallas_call x1, Pallas kernels: 132 us -> 125 us  [third(): pl.pallas_call(third_kernel, out_shape=[jax.ShapeDtypeStruct(shape, BF16)...]
where the time goes in v5:
time: 506 us; the launch traced here: 499 us
  Pallas kernels  479 us (95%)
  local copies, waits for them, and re-layouts  13.7 us (3%)
  other arithmetic  5.47 us (1%)
    pallas_call x1, Pallas kernels, gather(): pl.pallas_call(gather_kernel, out_shape=[jax.ShapeDtypeStruct(*shape) for...  198 us
    pallas_call x1, Pallas kernels, fourth(): pl.pallas_call(fourth_kernel, out_shape=[jax.ShapeDtypeStruct(*shape) for...  130 us
    pallas_call x1, Pallas kernels, third(): pl.pallas_call(third_kernel, out_shape=[jax.ShapeDtypeStruct(shape, BF16)...  125 us
    pallas_call x1, Pallas kernels, settle(): pl.pallas_call(settle_kernel, out_shape=[jax.ShapeDtypeStruct(*shape) for...  15.2 us

profile of v5, /device:TPU:19, one launch (start us, length us, event | category | flops | bytes accessed | tf_op | source)
XLA Modules:
  0.0 498.9 jit_solution(9299774107251536108)
XLA Ops:
  0.7 0.1 pad.5.clone
  0.7 0.1 pad.8.clone
  0.8 0.7 convert_element_type.43
  1.5 0.7 stack.9
  2.2 0.7 stack.10
  2.8 0.7 reshape.104
  3.5 1.3 reshape.105
  4.8 2.5 concatenate.12.vec_ref
  7.3 1.9 multiply_sine_fusion
  9.3 1.6 maximum_maximum_fusion.2
  10.9 0.0 copy-start.1
  10.9 0.0 copy-start.2
  10.9 0.0 copy-start.3
  10.9 197.9 %gather.1 = (bf16[8,256,2048]{2,1,0:T(8,128)(2,1)}, bf16[8,256,2048]{2,1,0:T(8,128)(2,1)}, bf16[8,256,2048]{2,1,0:T(8,128)(2,1)}, bf16[2048,768]{1,0:T(8,128)(2,...) custom-call(bf16[256,2048]{1,0:T(8,128)(2,1)} %bitcast.19, ...), custom_call_target="tpu_custom_call" | custom-call | tf_op jit(solution)/shard_map/gather/pallas_call | solution.py:784
  208.8 0.0 copy-done.1
  208.8 0.0 copy-done.2
  208.8 0.0 copy-done.3
  208.8 0.0 copy-start.4
  208.8 1.2 copy-done.4
  210.1 0.0 copy-start.5
  210.1 0.8 copy-done.5
  210.9 9.9 %attend_back.1.d_ref = bf16[2,3,1024,256]{3,2,1,0:T(8,128)(2,1)S(1)} custom-call(bf16[2,3,1024,256]{3,2,1,0:T(8,128)(2,1)} %get-tuple-element.44.qkv_ref, bf16[2,1024,256]{2,1,0:T(8,128)(2,1)S(1)} %copy-done.4, f32[2,4,8,256]{3,2,1,0:T(8,128)S(1)} %copy-done.5, f32[1024,128]{1,0:T(8,128)S(1)} %copy-done.3, f32[1024,128]{1,0:T(8,128)S(1)} %copy-done.2, ...), custom_call_target="tpu_custom_call" | custom-call | tf_op jit(solution)/shard_map/attend_back/pallas_call | solution.py:866
  220.8 0.0 copy-start
  220.8 1.7 copy-done
  222.4 125.5 %scatter_result.1 = (bf16[256,2048]{1,0:T(8,128)(2,1)}, bf16[2,4,256,768]{3,2,1,0:T(8,128)(2,1)}, bf16[8,64,1024]{2,1,0:T(8,128)(2,1)}, bf16[1280,512]{1,0:T(8,128)(2,1)}) custom-call(bf16[256,2048]{1,0:T(8,128)(2,1)} %bitcast.20, bf16[2048,256]{1,0:T(8,128)(2,1)} %bitcast.29, bf16[2048,1024]{1,0:T(8,128)(2,1)} %bitcast.25, bf16[256,2048]{1,0:T(8,128)(2,1)} %wo_ref.3, ...), custom_call_target="tpu_custom_call" | custom-call | tf_op jit(solution)/shard_map/scatter_result/pallas_call | solution.py:1296
  347.9 130.4 %scatter_grad.1 = (bf16[256,2048]{1,0:T(8,128)(2,1)}, bf16[8,256,1792]{2,1,0:T(8,128)(2,1)}, bf16[4,1280,512]{2,1,0:T(8,128)(2,1)}, f32[16,256]{1,0:T(8,128)}) custom-call(bf16[256,2048]{1,0:T(8,128)(2,1)} %bitcast.21, bf16[256,2048]{1,0:T(8,128)(2,1)} %bitcast.27, bf16[2048,768]{1,0:T(8,128)(2,1)} %bitcast.28, bf16[2048,1024]{1,0:T(8,128)(2,1)} %bitcast.18, ...), custom_call_target="tpu_custom_call" | custom-call | tf_op jit(solution)/shard_map/scatter_grad/pallas_call | solution.py:1541
  478.3 0.7 slice.18
  479.0 0.0 copy-start.6
  479.0 0.7 slice.17
  479.7 0.6 reshape.101
  480.3 0.7 slice_bitcast_fusion
  481.0 1.4 fusion.1
  482.3 0.6 copy.25
  482.9 15.2 %settle.1 = (f32[256,6144]{1,0:T(8,128)}, f32[256,8192]{1,0:T(8,128)}, f32[1024,2048]{1,0:T(8,128)}, f32[256,2048]{1,0:T(8,128)}, bf16[256,2048]{1,0:T(8,128)(2,1)}, /*index=5*/bf16[256,2048]{1,0:T(8,128)(2,1)}) custom-call(bf16[8,256,1792]{2,1,0:T(8,128)(2,1)} %get-tuple-element.57.columns_ref, bf16[4,1280,512]{2,1,0:T(8,128)(2,1)} %get-tuple-element.58.rows_ref, ...), custom_call_target="tpu_custom_call" | custom-call | tf_op jit(solution)/shard_map/settle/pallas_call | solution.py:1685
  498.1 0.0 copy-done.6
  498.1 0.6 copy.27
  (9 shorter events, 0.1 us)
Async XLA Ops:
  10.9 197.9 %copy-start.1 = (f32[1024,128]{1,0:T(8,128)S(1)}, f32[1024,128]{1,0:T(8,128)}, u32[]{:S(2)}) copy-start(f32[1024,128]{1,0:T(8,128)} %get-tuple-element.68.below_ref) | copy-start | bytes 1572868
  10.9 197.9 %copy-start.2 = (f32[1024,128]{1,0:T(8,128)S(1)}, f32[1024,128]{1,0:T(8,128)}, u32[]{:S(2)}) copy-start(f32[1024,128]{1,0:T(8,128)} %get-tuple-element.69.above_ref) | copy-start | bytes 1572868
  10.9 197.9 %copy-start.3 = (f32[1024,128]{1,0:T(8,128)S(1)}, f32[1024,128]{1,0:T(8,128)}, u32[]{:S(2)}) copy-start(f32[1024,128]{1,0:T(8,128)} %get-tuple-element.75.cos_ref) | copy-start | bytes 1572868
  208.8 1.2 copy-start.4
  210.1 0.8 copy-start.5
  220.8 1.7 copy-start
  479.0 19.1 %copy-start.6 = (f32[1,256]{1,0:T(1,128)}, f32[1,256]{1,0:T(1,128)S(1)}, u32[]{:S(2)}) copy-start(f32[1,256]{1,0:T(1,128)S(1)} %slice.18) | copy-start | bytes 3076

commit v6 on v5

--- a/solution.py
+++ b/solution.py
@@ -2,6 +2,7 @@
 
 import jax
 import jax.numpy as jnp
+import numpy as np
 from jax import lax
 from jax.experimental import pallas as pl
 from jax.experimental.pallas import tpu as pltpu
@@ -34,20 +35,16 @@
     return lax.dot_general(left, right, (((0,), (0,)), ((), ())), preferred_element_type=F32)
 
 
-def rotary_tables(positions):
+def rotary_tables(length):
     half = ROT // 2
-    exponent = jnp.arange(0, ROT, 2).astype(F32) / ROT
-    frequency = 10000.0 ** (-exponent)
-    angles = positions[:, None] * frequency[None, :]
-    rows = positions.shape[0]
-    cosine, sine = jnp.cos(angles), jnp.sin(angles)
-    one, nought = jnp.ones((rows, 64), F32), jnp.zeros((rows, 64), F32)
-    blank = jnp.zeros((rows, half), F32)
-    return (
-        jnp.concatenate([cosine, cosine, one], -1),
-        jnp.concatenate([-sine, blank, nought], -1),
-        jnp.concatenate([blank, sine, nought], -1),
-    )
+    exponent = np.arange(0, ROT, 2).astype(np.float32) / np.float32(ROT)
+    frequency = np.float32(10000.0) ** (-exponent)
+    angles = np.arange(length, dtype=np.float32)[:, None] * frequency[None, :]
+    cosine, sine = np.cos(angles), np.sin(angles)
+    one, nought = np.ones((length, 64), np.float32), np.zeros((length, 64), np.float32)
+    blank = np.zeros((length, half), np.float32)
+    tables = ([cosine, cosine, one], [-sine, blank, nought], [blank, sine, nought])
+    return [jnp.asarray(np.concatenate(table, -1)) for table in tables]
 
 
 def spot():
@@ -468,11 +465,12 @@
 
 
 def gather_kernel(
-    x_ref, dy_ref, vec_ref, wo_ref, wd_ref, upb_ref, cos_ref, above_ref, below_ref, wq_ref, wu_ref,
+    x_ref, dy_ref, gain_ref, shift_ref, out_b_ref, down_b_ref, qkv_b_ref, up_b_ref, marks_ref,
+    wo_in, wd_in, cos_ref, above_ref, below_ref, wq_ref, wu_ref,
     x_out, ha_out, hm_out, wq_out, wu_out, qkv_out, marks_out, vec_out,
     dy_out, a_out, du_out, do_out, o_out, sum_out,
-    xs, dys, hm, head, units, vecs, vectors, ha, qkv, whole, marks, mixed, act, grad, attended,
-    table, own_sem, x_store, ha_store, du_store, dy_store, late_store, v_send, v_recv, back_send, back_recv,
+    xs, dys, hm, head, units, vec_ref, vecs, vectors, ha, qkv, whole, marks, mixed, act, grad, attended,
+    table, wo_ref, wd_ref, late_load, own_sem, x_store, ha_store, du_store, dy_store, late_store, v_send, v_recv, back_send, back_recv,
     *sems,
 ):
     base, line, side, quarter = spot()
@@ -534,6 +532,21 @@
         landing(units), 0, hidden, unit_columns,
     )
     own_rows = pl.ds(pl.multiple_of(quarter * tokens, tokens), tokens)
+
+    def put_row(row, values):
+        vec_ref[row : row + 1, :] = values.astype(F32).reshape(1, rows)
+
+    vec_ref[...] = jnp.zeros_like(vec_ref)
+    vec_ref[0:2, :] = gain_ref[...].astype(F32)
+    vec_ref[2:4, :] = shift_ref[...].astype(F32)
+    put_row(4, out_b_ref[...])
+    put_row(5, down_b_ref[...])
+    for index in range(3):
+        put_row(8 + index, qkv_b_ref[pl.ds(index * rows, rows)])
+    vec_ref[16:24, :] = jnp.broadcast_to(marks_ref[...].astype(F32), (8, tokens))
+    for start in range(0, hidden, 256):
+        values = up_b_ref[pl.ds(start, 256)].astype(F32)
+        vectors[4:5, pl.ds(start, 256)] = values.reshape(1, 256)
     greet_team(base, line, side, quarter)
 
     def vector_copy(source, target, peer):
@@ -556,6 +569,10 @@
     ]
     for copy in owns:
         copy.start()
+    load_out = pltpu.make_async_copy(wo_in, wo_ref, late_load.at[0])
+    load_down = pltpu.make_async_copy(wd_in, wd_ref, late_load.at[1])
+    load_out.start()
+    load_down.start()
 
     def send_vector(step, _):
         target = lax.rem(rank + step, TEAM)
@@ -683,6 +700,8 @@
         back(to, quarter).start()
     unit_columns.arrive()
     late[2].start()
+    load_out.wait()
+    load_down.wait()
 
     def store_dy(which):
         return pltpu.make_async_copy(dys.at[which], dy_out.at[which], dy_store.at[which])
@@ -698,7 +717,7 @@
         spread_do.start(which)
         for start in range(0, hidden, 256):
             span = pl.ds(start, 256)
-            up = dot(hm[which], units[:, span]) + upb_ref[:, span]
+            up = dot(hm[which], units[:, span]) + vectors[4:5, span]
             value, slope = gelu_terms(up)
             act[slot, :, span] = value.astype(BF16)
             pulled = contract_last(dys[which], wd_ref[span, :])
@@ -757,13 +776,14 @@
         copy.wait()
 
 
-def gather(x, dy, vec, w_out, w_down, up_bias, tables, w_qkv, w_up):
+def gather(x, dy, parameters, w_out, w_down, tables, w_qkv, w_up):
     tokens, width = x.shape
-    hidden = up_bias.shape[-1]
+    hidden, rows = w_down.shape[0], w_qkv.shape[0]
     all_tokens = (TEAM, tokens, width)
     whole = (2, 3, QUARTERS * tokens, HEAD)
     marks = ((2, QUARTERS, 8, tokens), F32)
-    vecs = ((TEAM, VECTOR_ROWS, vec.shape[-1]), F32)
+    vec = (VECTOR_ROWS, rows)
+    vecs = ((TEAM, *vec), F32)
     units = ((TEAM, tokens, hidden), BF16)
     shapes = [
         (all_tokens, BF16),
@@ -784,7 +804,7 @@
     return pl.pallas_call(
         gather_kernel,
         out_shape=[jax.ShapeDtypeStruct(*shape) for shape in shapes],
-        in_specs=[ANY] * 2 + [VMEM] * 4 + [ANY] * 5,
+        in_specs=[ANY] * 2 + [VMEM] * 7 + [ANY] * 7,
         out_specs=[ANY] * 13 + [VMEM],
         scratch_shapes=[
             pltpu.VMEM(all_tokens, BF16),
@@ -792,6 +812,7 @@
             pltpu.VMEM(all_tokens, BF16),
             pltpu.VMEM((width, 3 * HEAD), BF16),
             pltpu.VMEM((width, hidden), BF16),
+            pltpu.VMEM(vec, F32),
             pltpu.VMEM(*vecs),
             pltpu.VMEM((8, width), F32),
             pltpu.VMEM((2, tokens, width), BF16),
@@ -803,6 +824,9 @@
             pltpu.VMEM((2, tokens, hidden), BF16),
             pltpu.VMEM((TEAM, tokens, HEAD), BF16),
             pltpu.VMEM((3, tokens, 128), F32),
+            pltpu.VMEM(w_out.shape, BF16),
+            pltpu.VMEM(w_down.shape, BF16),
+            DMA((2,)),
             DMA((7,)),
             DMA((2, TEAM)),
             DMA((2,)),
@@ -823,7 +847,7 @@
             collective_id=0, has_side_effects=True, vmem_limit_bytes=LIMIT
         ),
         name="gather",
-    )(x, dy, vec, w_out, w_down, up_bias, *tables, w_qkv, w_up)
+    )(x, dy, *parameters, w_out, w_down, *tables, w_qkv, w_up)
 
 
 def backward_kernel(
@@ -1148,9 +1172,9 @@
 
 
 def third_kernel(
-    x_ref, o_ref, a_ref, wo_ref, wd_ref, vec_ref, du_ref, d_ref, hm_ref, dy_ref,
+    vec_ref, x_in, o_in, a_in, wo_in, wd_in, du_in, d_ref, hm_ref, dy_ref,
     result_out, back_out, up_out, rows_out,
-    own_sem, back_send, back_recv, load_sem, store_sem, hm_tiles, tile_sum, dy, bias, *rest,
+    x_ref, o_ref, a_ref, wo_ref, wd_ref, du_ref, in_sem, own_sem, back_send, back_recv, load_sem, store_sem, hm_tiles, tile_sum, dy, bias, *rest,
 ):
     base, line, side, quarter = spot()
     rank = line * 2 + side
@@ -1160,6 +1184,17 @@
     rest = rest[REDUCE:]
     ups, downs = Quarters(*rest[:8]), Quarters(*rest[8:16])
     stream = Stream(hm_ref, hm_tiles, load_sem)
+    loads = [
+        pltpu.make_async_copy(src, dst, in_sem.at[index])
+        for index, (src, dst) in enumerate(
+            (
+                (o_in, o_ref), (wo_in, wo_ref), (a_in, a_ref), (wd_in, wd_ref), (du_in, du_ref),
+                (x_in, x_ref),
+            )
+        )
+    ]
+    for copy in loads:
+        copy.start()
     load_dy = pltpu.make_async_copy(dy_ref, dy, own_sem.at[3])
     load_dy.start()
     for tile in range(2):
@@ -1195,6 +1230,8 @@
     def put_own(span, value):
         reduce.own[0, :, span] = value.astype(BF16)
 
+    for copy in loads:
+        copy.wait()
     for step in reversed(range(PAIRS)):
 
         def put_out(span, value, step=step):
@@ -1296,9 +1333,14 @@
     return pl.pallas_call(
         third_kernel,
         out_shape=[jax.ShapeDtypeStruct(shape, BF16) for shape in shapes],
-        in_specs=[VMEM] * 7 + [ANY] * 3,
+        in_specs=[VMEM] + [ANY] * 9,
         out_specs=[ANY] * 4,
         scratch_shapes=[
+            pltpu.VMEM(values.shape, BF16)
+            for values in (x, attended, activated, w_out, w_down, grad_up)
+        ]
+        + [
+            DMA((6,)),
             DMA((4,)),
             DMA((QUARTERS, 3)),
             DMA((QUARTERS, 3)),
@@ -1316,13 +1358,13 @@
             collective_id=2, has_side_effects=True, vmem_limit_bytes=LIMIT
         ),
         name="scatter_result",
-    )(x, attended, activated, w_out, w_down, vectors, grad_up, grads, mlp_input, grad_rows)
+    )(vectors, x, attended, activated, w_out, w_down, grad_up, grads, mlp_input, grad_rows)
 
 
 def fourth_kernel(
-    x_ref, dy_ref, dqkv_ref, du_ref, vec_ref, dy_sum_ref, xs_ref, wq_ref, wu_ref, ha_ref, up_ref, rows_ref,
+    vec_ref, dy_sum_ref, x_in, dy_in, dqkv_in, du_in, xs_ref, wq_ref, wu_ref, ha_ref, up_ref, rows_ref,
     grad_ref, landed, rows_out, vector_ref,
-    wq, wu, xs, gains, load_sem, tile_load, ha_tiles, tile_sum, sums, packets, packets_in, ring, ring_in,
+    x_ref, dy_ref, dqkv_ref, du_ref, wq, wu, xs, gains, load_sem, xs_sem, tile_load, ha_tiles, tile_sum, sums, packets, packets_in, ring, ring_in,
     row_own, row_send, row_recv, pack_send, pack_recv, ring_send, ring_recv, *rest,
 ):
     base, line, side, quarter = spot()
@@ -1348,12 +1390,23 @@
     )
     stream = Stream(ha_ref, ha_tiles, tile_load)
     loads = [
-        pltpu.make_async_copy(wq_ref, wq, load_sem.at[0]),
-        pltpu.make_async_copy(wu_ref, wu, load_sem.at[1]),
-        pltpu.make_async_copy(xs_ref, xs, load_sem.at[2]),
+        pltpu.make_async_copy(src, dst, load_sem.at[index])
+        for index, (src, dst) in enumerate(
+            (
+                (dqkv_in, dqkv_ref), (wq_ref, wq), (du_in, du_ref), (wu_ref, wu), (x_in, x_ref),
+                (dy_in, dy_ref),
+            )
+        )
     ]
     for copy in loads:
         copy.start()
+
+    def load_x(which):
+        return pltpu.make_async_copy(xs_ref.at[which], xs.at[which], xs_sem.at[which])
+
+    for other in (1 - side, side):
+        for step in reversed(range(PAIRS)):
+            load_x(reduce.order[step] * 2 + other).start()
     for tile in range(2):
         stream.copy(tile).start()
     greet_team(base, line, side, quarter)
@@ -1367,7 +1420,6 @@
     own_rows = pltpu.make_async_copy(rows_ref, rows_out.at[quarter], row_own)
     own_rows.start()
     rows_copy(0, quarter, core).start()
-    up_columns.start()
     sums[...] = jnp.zeros_like(sums)
     for source in range(TEAM):
         gains[0:2, pl.ds(source * block, block)] = vec_ref[source, 0:2, :]
@@ -1376,6 +1428,7 @@
 
     def make(which, put):
         rows = pl.ds(pl.multiple_of(which * tokens, tokens), tokens)
+        load_x(which).wait()
         values = xs[which].astype(F32)
         average = jnp.mean(values, -1, keepdims=True)
         variance = jnp.mean(jnp.square(values - average), -1, keepdims=True)
@@ -1404,6 +1457,7 @@
         reduce.begin(step)
         if step == PAIRS - 1:
             reduce.launch()
+            up_columns.start()
 
     def qkv_tile(tile, held):
         tile_sum[...] = contract_first(held[...], dqkv_ref[...])
@@ -1541,14 +1595,19 @@
     return pl.pallas_call(
         fourth_kernel,
         out_shape=[jax.ShapeDtypeStruct(*shape) for shape in shapes],
-        in_specs=[VMEM] * 6 + [ANY] * 6,
+        in_specs=[VMEM] * 2 + [ANY] * 10,
         out_specs=[VMEM, ANY, ANY, VMEM],
         scratch_shapes=[
+            pltpu.VMEM(x.shape, BF16),
+            pltpu.VMEM(dy.shape, BF16),
+            pltpu.VMEM(grad_qkv.shape, BF16),
+            pltpu.VMEM(grad_up.shape, BF16),
             pltpu.VMEM(w_qkv.shape, BF16),
             pltpu.VMEM(w_up.shape, BF16),
             pltpu.VMEM(everyone.shape, BF16),
             pltpu.VMEM((8, width), F32),
-            DMA((3,)),
+            DMA((6,)),
+            DMA((TEAM,)),
             DMA((2,)),
             pltpu.VMEM((2, TEAM * tokens, block), BF16),
             pltpu.VMEM((block, 3 * HEAD), F32),
@@ -1573,13 +1632,14 @@
         ),
         name="scatter_grad",
     )(
-        x, dy, grad_qkv, grad_up, vectors, dy_sum, everyone, w_qkv, w_up, attn_input, up_sums,
+        vectors, dy_sum, x, dy, grad_qkv, grad_up, everyone, w_qkv, w_up, attn_input, up_sums,
         row_sums,
     )
 
 
 def settle_kernel(
-    columns_ref, rows_ref, result_ref, grad_ref,
+    vector_ref, columns_ref, rows_ref, result_ref, grad_ref,
+    gain_out, shift_out, bias_out, bias_again, qkv_bias_out, up_bias_out,
     qkv_out, up_out, down_out, out_out, result_out, grad_out,
     low, wide, low_rows, wide_rows, passing, load_sem, store_sem, rows_load, rows_store, copy_sem,
 ):
@@ -1596,6 +1656,17 @@
     ]
     for load_in, _ in plain:
         load_in.start()
+    size = vector_ref.shape[1]
+    gain_out[...] = vector_ref[0:2, :]
+    shift_out[...] = vector_ref[2:4, :]
+    bias_out[...] = vector_ref[4:5, :].reshape(size)
+    bias_again[...] = vector_ref[4:5, :].reshape(size)
+    for index in range(3):
+        row = vector_ref[5 + index : 6 + index, :]
+        qkv_bias_out[pl.ds(index * size, size)] = row.reshape(size)
+    for index in range(hidden // size):
+        row = vector_ref[8 + index : 9 + index, :]
+        up_bias_out[pl.ds(index * size, size)] = row.reshape(size)
 
     def load(source):
         slot = lax.rem(source, 2)
@@ -1671,10 +1742,17 @@
         store_out.wait()
 
 
-def settle(columns, row_sums, result, grad_inputs):
+def settle(vector, columns, row_sums, result, grad_inputs):
     team, block, span = columns.shape
     quarters, tall, share = row_sums.shape
+    size = vector.shape[1]
     shapes = [
+        ((2, size), F32),
+        ((2, size), F32),
+        ((size,), F32),
+        ((size,), F32),
+        ((3 * size,), F32),
+        ((tall - HEAD,), F32),
         ((block, team * 3 * HEAD), F32),
         ((block, team * (span - 3 * HEAD)), F32),
         ((tall - HEAD, quarters * share), F32),
@@ -1685,8 +1763,8 @@
     return pl.pallas_call(
         settle_kernel,
         out_shape=[jax.ShapeDtypeStruct(*shape) for shape in shapes],
-        in_specs=[ANY] * 4,
-        out_specs=[ANY] * 6,
+        in_specs=[VMEM] + [ANY] * 4,
+        out_specs=[VMEM] * 6 + [ANY] * 6,
         scratch_shapes=[
             pltpu.VMEM((2, block, span), BF16),
             pltpu.VMEM((2, block, span), F32),
@@ -1701,7 +1779,7 @@
         ],
         compiler_params=pltpu.CompilerParams(vmem_limit_bytes=LIMIT),
         name="settle",
-    )(columns, row_sums, result, grad_inputs)
+    )(vector, columns, row_sums, result, grad_inputs)
 
 
 def on_device(
@@ -1761,27 +1839,15 @@
         b_qkv, b_up = cut(whole(qkv_bias)), cut(whole(up_bias))
         b_rows = [cut(whole(out_bias)), cut(whole(down_bias))]
     rows = w_qkv.shape[0]
-    packet = jnp.concatenate(
-        [
-            gain.astype(F32),
-            shift.astype(F32),
-            jnp.stack(b_rows).astype(F32),
-            jnp.zeros((2, rows), F32),
-            b_qkv.astype(F32).reshape(3, rows),
-            jnp.zeros((5, rows), F32),
-            jnp.broadcast_to(segments.astype(F32), (8, tokens)),
-        ]
-    )
     mine = inputs.reshape(tokens, width)
     grad_mine = cotangent.reshape(tokens, width)
     mine_team = team_order(mine)
-    positions = jnp.arange(ctx * tokens, dtype=jnp.int32)
-    tables = rotary_tables(positions.astype(F32))
+    tables = rotary_tables(ctx * tokens)
     (
         everyone, attn_input, mlp_input, w_head, w_units, qkv, marks, vectors,
         grad_rows, activated, grad_up, grad_attended, attended, dy_sum,
     ) = gather(
-        mine_team, grad_mine, packet, w_out, w_down, b_up.astype(F32).reshape(1, hidden), tables,
+        mine_team, grad_mine, (gain, shift, *b_rows, b_qkv, b_up, segments), w_out, w_down, tables,
         w_qkv, w_up,
     )
     grads = attend_back(qkv, grad_attended, marks, tables)
@@ -1798,24 +1864,26 @@
         w_head, w_units, attn_input, up_sums, row_sums,
     )
     grad_inputs = plain_order(grad_inputs)
-    if teams == 1:
-        grad_gain, grad_shift, grad_out_b = vector[0:2], vector[2:4], vector[4]
-        grad_qkv_b, grad_up_b = vector[5:8].reshape(-1), vector[8 : 8 + hidden // rows].reshape(-1)
-    else:
+    if teams > 1:
+        columns = lax.psum_scatter(
+            columns, "dp", scatter_dimension=1, axis_index_groups=across, tiled=True
+        )
+    (
+        grad_gain, grad_shift, grad_out_b, grad_down_b, grad_qkv_b, grad_up_b,
+        grad_qkv_w, grad_up_w, grad_down_w, grad_out_w, result, grad_inputs,
+    ) = settle(vector, columns, row_sums, result, grad_inputs)
+    if teams > 1:
         near = partial(lax.all_gather, axis_name="dp", axis_index_groups=together, tiled=True)
 
         def own(values):
             size = values.shape[0] // dp
-            total = lax.psum(values, "dp", axis_index_groups=across)
-            return lax.dynamic_slice_in_dim(total, place * size, size, 0)
-
-        ends = lax.psum_scatter(
-            vector[:4], "dp", scatter_dimension=1, axis_index_groups=across, tiled=True
-        )
-        grad_gain, grad_shift = ends[0:2], ends[2:4]
-        grad_out_b = own(near(vector[4], axis=0))
-        grad_qkv_b = own(near(vector[5:8].reshape(-1), axis=0))
-        grad_up_b = own(near(vector[8 : 8 + hidden // rows].reshape(-1), axis=0))
+            total = lax.psum(near(values, axis=0), "dp", axis_index_groups=across)
+            return lax.dynamic_slice_in_dim(total, place * (TEAM * size), TEAM * size, 0)
+
+        def own_end(values):
+            return lax.psum_scatter(
+                values, "dp", scatter_dimension=1, axis_index_groups=across, tiled=True
+            )
 
         def scatter_rows(term):
             size = term.shape[0]
@@ -1825,13 +1893,9 @@
                 full.reshape(TEAM * size, width), "dp", scatter_dimension=0, tiled=True
             ).astype(F32)
 
-        columns = lax.psum_scatter(
-            columns, "dp", scatter_dimension=1, axis_index_groups=across, tiled=True
-        )
-    grad_qkv_w, grad_up_w, grad_down_w, grad_out_w, result, grad_inputs = settle(
-        columns, row_sums, result, grad_inputs
-    )
-    if teams > 1:
+        grad_gain, grad_shift = own_end(grad_gain), own_end(grad_shift)
+        grad_out_b, grad_down_b = own(grad_out_b), own(grad_down_b)
+        grad_qkv_b, grad_up_b = own(grad_qkv_b), own(grad_up_b)
         grad_out_w, grad_down_w = scatter_rows(grad_out_w), scatter_rows(grad_down_w)
     return (
         result.reshape(inputs.shape),
@@ -1845,7 +1909,7 @@
         grad_up_w,
         grad_up_b,
         grad_down_w,
-        grad_out_b,
+        grad_down_b,
     )
 
 

time: 506 us -> 496 us (0.980)
  local copies, waits for them, and re-layouts: 13.7 us -> 3.74 us
  other arithmetic: 5.47 us -> 0 us
where the time goes in v6:
time: 496 us; the launch traced here: 487 us
  Pallas kernels  482 us (97%)
    pallas_call x1, Pallas kernels, gather(): pl.pallas_call(gather_kernel, out_shape=[jax.ShapeDtypeStruct(*shape) for...  196 us
    pallas_call x1, Pallas kernels, fourth(): pl.pallas_call(fourth_kernel, out_shape=[jax.ShapeDtypeStruct(*shape) for...  134 us
    pallas_call x1, Pallas kernels, third(): pl.pallas_call(third_kernel, out_shape=[jax.ShapeDtypeStruct(shape, BF16)...  125 us
    pallas_call x1, Pallas kernels, settle(): pl.pallas_call(settle_kernel, out_shape=[jax.ShapeDtypeStruct(*shape) for...  16.5 us

profile of v6, /device:TPU:19, one launch (start us, length us, event | category | flops | bytes accessed | tf_op | source)
XLA Modules:
  0.0 486.9 jit_solution(979309280970899216)
XLA Ops:
  0.6 0.0 copy-start.1
  0.7 0.0 copy-start.2
  0.7 0.0 copy-start.3
  0.7 196.1 %gather.1 = (bf16[8,256,2048]{2,1,0:T(8,128)(2,1)}, bf16[8,256,2048]{2,1,0:T(8,128)(2,1)}, bf16[8,256,2048]{2,1,0:T(8,128)(2,1)}, bf16[2048,768]{1,0:T(8,128)(2,...) custom-call(bf16[256,2048]{1,0:T(8,128)(2,1)} %bitcast.13, ...), custom_call_target="tpu_custom_call" | custom-call | tf_op jit(solution)/shard_map/gather/pallas_call | solution.py:804
  196.8 0.0 copy-done.1
  196.8 0.0 copy-done.2
  196.8 0.0 copy-done.3
  196.8 0.0 copy-start.4
  196.8 1.2 copy-done.4
  198.0 0.0 copy-start.5
  198.0 0.8 copy-done.5
  198.9 9.9 %attend_back.1.d_ref = bf16[2,3,1024,256]{3,2,1,0:T(8,128)(2,1)S(1)} custom-call(bf16[2,3,1024,256]{3,2,1,0:T(8,128)(2,1)} %get-tuple-element.51.qkv_ref, bf16[2,1024,256]{2,1,0:T(8,128)(2,1)S(1)} %copy-done.4, f32[2,4,8,256]{3,2,1,0:T(8,128)S(1)} %copy-done.5, f32[1024,128]{1,0:T(8,128)S(1)} %copy-done.3, f32[1024,128]{1,0:T(8,128)S(1)} %copy-done.2, ...), custom_call_target="tpu_custom_call" | custom-call | tf_op jit(solution)/shard_map/attend_back/pallas_call | solution.py:890
  208.8 0.0 copy-start
  208.8 1.7 copy-done
  210.4 125.2 %scatter_result.1 = (bf16[256,2048]{1,0:T(8,128)(2,1)}, bf16[2,4,256,768]{3,2,1,0:T(8,128)(2,1)}, bf16[8,64,1024]{2,1,0:T(8,128)(2,1)}, bf16[1280,512]{1,0:T(8,128)(2,1)}) custom-call(f32[8,24,256]{2,1,0:T(8,128)} %get-tuple-element.46.vec_ref, bf16[256,2048]{1,0:T(8,128)(2,1)} %bitcast.14, bf16[2048,256]{1,0:T(8,128)(2,1)} %bitcast.23, ...), custom_call_target="tpu_custom_call" | custom-call | tf_op jit(solution)/shard_map/scatter_result/pallas_call | solution.py:1333
  335.6 134.4 %scatter_grad.1 = (bf16[256,2048]{1,0:T(8,128)(2,1)}, bf16[8,256,1792]{2,1,0:T(8,128)(2,1)}, bf16[4,1280,512]{2,1,0:T(8,128)(2,1)}, f32[16,256]{1,0:T(8,128)}) custom-call(f32[8,24,256]{2,1,0:T(8,128)} %get-tuple-element.46.vec_ref, f32[8,2048]{1,0:T(8,128)} %get-tuple-element.47.dy_sum_ref, bf16[256,2048]{1,0:T(8,128)(2,1)} %bitcast.15, ...), custom_call_target="tpu_custom_call" | custom-call | tf_op jit(solution)/shard_map/scatter_grad/pallas_call | solution.py:1595
  470.0 16.5 %settle.1 = (f32[2,256]{1,0:T(2,128)}, f32[2,256]{1,0:T(2,128)}, f32[256]{0:T(256)}, f32[256]{0:T(256)}, f32[768]{0:T(1024)}, /*index=5*/f32[1024]{0:T(1024)}, f...) custom-call(f32[16,256]{1,0:T(8,128)} %get-tuple-element.63.vector_r, ...), custom_call_target="tpu_custom_call" | custom-call | tf_op jit(solution)/shard_map/settle/pallas_call | solution.py:1763
Async XLA Ops:
  0.6 196.1 %copy-start.1 = (f32[1024,128]{1,0:T(8,128)S(1)}, f32[1024,128]{1,0:T(8,128)}, u32[]{:S(2)}) copy-start(f32[1024,128]{1,0:T(8,128)} %constant.8.clone.below_ref) | copy-start | bytes 1572868
  0.7 196.1 %copy-start.2 = (f32[1024,128]{1,0:T(8,128)S(1)}, f32[1024,128]{1,0:T(8,128)}, u32[]{:S(2)}) copy-start(f32[1024,128]{1,0:T(8,128)} %constant.7.clone.above_ref) | copy-start | bytes 1572868
  0.7 196.1 %copy-start.3 = (f32[1024,128]{1,0:T(8,128)S(1)}, f32[1024,128]{1,0:T(8,128)}, u32[]{:S(2)}) copy-start(f32[1024,128]{1,0:T(8,128)} %constant.6.clone.cos_ref) | copy-start | bytes 1572868
  196.8 1.2 copy-start.4
  198.0 0.8 copy-start.5
  208.8 1.7 copy-start

commit v7 on v6

--- a/solution.py
+++ b/solution.py
@@ -1294,7 +1294,7 @@
     for source in range(TEAM):
         bias[0:1, pl.ds(source * block, block)] = vec_ref[source, 4:5, :] + vec_ref[source, 5:6, :]
     reduce.last()
-    strip = 64
+    strip = 128
 
     def close(index, _):
         chunk = pl.ds(pl.multiple_of(index * strip, strip), strip)
@@ -1538,7 +1538,7 @@
     ring_in[quarter] = ring[...]
     qkv_columns.forward()
     reduce.last()
-    strip = 64
+    strip = 128
 
     def close(index, _):
         chunk = pl.ds(pl.multiple_of(index * strip, strip), strip)
@@ -1730,8 +1730,8 @@
     for load_in, store_out in plain:
         load_in.wait()
         store_out.start()
-    run(quarters, load_rows, stores_rows, low_rows, wide_rows, 64)
-    run(team, load, stores, low, wide, min(64, block))
+    run(quarters, load_rows, stores_rows, low_rows, wide_rows, 256)
+    run(team, load, stores, low, wide, min(128, block))
     for index in (quarters - 2, quarters - 1):
         for copy in stores_rows(index):
             copy.wait()

time: 496 us -> 495 us (level)
  no operation moved by 1% of the time
where the time goes in v7:
time: 495 us; the launch traced here: 487 us
  Pallas kernels  482 us (97%)
    pallas_call x1, Pallas kernels, gather(): pl.pallas_call(gather_kernel, out_shape=[jax.ShapeDtypeStruct(*shape) for...  196 us
    pallas_call x1, Pallas kernels, fourth(): pl.pallas_call(fourth_kernel, out_shape=[jax.ShapeDtypeStruct(*shape) for...  134 us
    pallas_call x1, Pallas kernels, third(): pl.pallas_call(third_kernel, out_shape=[jax.ShapeDtypeStruct(shape, BF16)...  125 us
    pallas_call x1, Pallas kernels, settle(): pl.pallas_call(settle_kernel, out_shape=[jax.ShapeDtypeStruct(*shape) for...  16.3 us

profile of v7, /device:TPU:19, one launch (start us, length us, event | category | flops | bytes accessed | tf_op | source)
XLA Modules:
  0.0 486.8 jit_solution(15340580811015511451)
XLA Ops:
  0.6 0.0 copy-start.1
  0.7 0.0 copy-start.2
  0.7 0.0 copy-start.3
  0.7 196.1 %gather.1 = (bf16[8,256,2048]{2,1,0:T(8,128)(2,1)}, bf16[8,256,2048]{2,1,0:T(8,128)(2,1)}, bf16[8,256,2048]{2,1,0:T(8,128)(2,1)}, bf16[2048,768]{1,0:T(8,128)(2,...) custom-call(bf16[256,2048]{1,0:T(8,128)(2,1)} %bitcast.13, ...), custom_call_target="tpu_custom_call" | custom-call | tf_op jit(solution)/shard_map/gather/pallas_call | solution.py:804
  196.8 0.0 copy-done.1
  196.8 0.0 copy-done.2
  196.8 0.0 copy-done.3
  196.8 0.0 copy-start.4
  196.8 1.2 copy-done.4
  198.0 0.0 copy-start.5
  198.0 0.8 copy-done.5
  198.9 9.9 %attend_back.1.d_ref = bf16[2,3,1024,256]{3,2,1,0:T(8,128)(2,1)S(1)} custom-call(bf16[2,3,1024,256]{3,2,1,0:T(8,128)(2,1)} %get-tuple-element.51.qkv_ref, bf16[2,1024,256]{2,1,0:T(8,128)(2,1)S(1)} %copy-done.4, f32[2,4,8,256]{3,2,1,0:T(8,128)S(1)} %copy-done.5, f32[1024,128]{1,0:T(8,128)S(1)} %copy-done.3, f32[1024,128]{1,0:T(8,128)S(1)} %copy-done.2, ...), custom_call_target="tpu_custom_call" | custom-call | tf_op jit(solution)/shard_map/attend_back/pallas_call | solution.py:890
  208.8 0.0 copy-start
  208.8 1.7 copy-done
  210.4 125.2 %scatter_result.1 = (bf16[256,2048]{1,0:T(8,128)(2,1)}, bf16[2,4,256,768]{3,2,1,0:T(8,128)(2,1)}, bf16[8,64,1024]{2,1,0:T(8,128)(2,1)}, bf16[1280,512]{1,0:T(8,128)(2,1)}) custom-call(f32[8,24,256]{2,1,0:T(8,128)} %get-tuple-element.46.vec_ref, bf16[256,2048]{1,0:T(8,128)(2,1)} %bitcast.14, bf16[2048,256]{1,0:T(8,128)(2,1)} %bitcast.23, ...), custom_call_target="tpu_custom_call" | custom-call | tf_op jit(solution)/shard_map/scatter_result/pallas_call | solution.py:1333
  335.6 134.4 %scatter_grad.1 = (bf16[256,2048]{1,0:T(8,128)(2,1)}, bf16[8,256,1792]{2,1,0:T(8,128)(2,1)}, bf16[4,1280,512]{2,1,0:T(8,128)(2,1)}, f32[16,256]{1,0:T(8,128)}) custom-call(f32[8,24,256]{2,1,0:T(8,128)} %get-tuple-element.46.vec_ref, f32[8,2048]{1,0:T(8,128)} %get-tuple-element.47.dy_sum_ref, bf16[256,2048]{1,0:T(8,128)(2,1)} %bitcast.15, ...), custom_call_target="tpu_custom_call" | custom-call | tf_op jit(solution)/shard_map/scatter_grad/pallas_call | solution.py:1595
  470.0 16.3 %settle.1 = (f32[2,256]{1,0:T(2,128)}, f32[2,256]{1,0:T(2,128)}, f32[256]{0:T(256)}, f32[256]{0:T(256)}, f32[768]{0:T(1024)}, /*index=5*/f32[1024]{0:T(1024)}, f...) custom-call(f32[16,256]{1,0:T(8,128)} %get-tuple-element.63.vector_r, ...), custom_call_target="tpu_custom_call" | custom-call | tf_op jit(solution)/shard_map/settle/pallas_call | solution.py:1763
Async XLA Ops:
  0.6 196.1 %copy-start.1 = (f32[1024,128]{1,0:T(8,128)S(1)}, f32[1024,128]{1,0:T(8,128)}, u32[]{:S(2)}) copy-start(f32[1024,128]{1,0:T(8,128)} %constant.8.clone.below_ref) | copy-start | bytes 1572868
  0.7 196.1 %copy-start.2 = (f32[1024,128]{1,0:T(8,128)S(1)}, f32[1024,128]{1,0:T(8,128)}, u32[]{:S(2)}) copy-start(f32[1024,128]{1,0:T(8,128)} %constant.7.clone.above_ref) | copy-start | bytes 1572868
  0.7 196.1 %copy-start.3 = (f32[1024,128]{1,0:T(8,128)S(1)}, f32[1024,128]{1,0:T(8,128)}, u32[]{:S(2)}) copy-start(f32[1024,128]{1,0:T(8,128)} %constant.6.clone.cos_ref) | copy-start | bytes 1572868
  196.8 1.2 copy-start.4
  198.0 0.8 copy-start.5
  208.8 1.7 copy-start
